TPU v7x, 32 devices: a whole 2x2x4 slice. The times are simulated.
32 devices in a mesh: groups: 2 (over x), ctx: 8 (over z, y), head: 2 (over core).
Axes of the slice: x: 2, y: 2, z: 4, core: 2. Of those that a mesh axis runs over, the one named last changes fastest.
Arguments:
- features: bfloat16 [8192, 8192], P(('groups', 'ctx'), 'head'), parts along dimension 0, may hold values from -6 to 6
- output_switch: bfloat16 [8192, 8192], P(('groups', 'ctx'), 'head'), parts along dimension 0, may hold values from -6 to 6
- input_proj: bfloat16 [8192, 512], P(('groups', 'ctx'), 'head'), parts along dimension 0, may hold values from -1.796875 to 1.796875
- output_proj: bfloat16 [8192, 512], P(('groups', 'ctx'), 'head'), parts along dimension 0, may hold values from -1.796875 to 1.796875
- step_codes: int32 [8192, 128], P(('groups', 'ctx'), 'head'), parts along dimension 0, may hold values from 1 to 12288
- head_rate: float32 [128], P('head'), may hold values from 0 to 12
- conv_weight: bfloat16 [4, 8192], P(None, 'head'), may hold values from -3 to 3
- conv_bias: bfloat16 [8192], P('head'), may hold values from -3 to 3
- bypass_factor: float32 [128], P('head'), may hold values from 2 to 32
- norm_gain: float32 [8192], P('head'), may hold values from 0.5 to 1.5
Outputs:
- ssm_output: bfloat16 [8192, 8192], P(('groups', 'ctx'), 'head'), parts along dimension 0
There are 2 independent parts, one for each index of `groups`. A program takes and returns all parts, laid end to end along the dimension named above; an argument that names none is the same for every part. Nothing has to cross between parts.
All inputs are finite; a program needn't handle non-finite values.
Results may differ from a plain program's by a relative error of at most 0.0063.
Values may be sent and summed in bfloat16 or wider, within the bound.
No kernel may reach another device: no remote copies, remote signals or barrier semaphores. Data moves between devices by JAX's collectives and lax.ppermute only.
A program may use at most 128 MiB of HBM per device.

v0:
```python
import math

import jax
import jax.numpy as jnp
from jax import lax
from jax.sharding import PartitionSpec as P

NSTATE = 128
KERNEL = 4
BLOCK = 512


highest = lax.Precision.HIGHEST
code_unit = 1024.0


def shifted(block, axis, distance):
    devices = range(lax.axis_size(axis))
    route = [(i - distance, i) for i in devices if i - distance in devices]
    return lax.ppermute(block, axis, route)


def per_device(
    features,
    output_switch,
    input_proj,
    output_proj,
    step_codes,
    head_rate,
    conv_weight,
    conv_bias,
    bypass_factor,
    norm_gain,
):
    tokens_here = features.shape[0]
    width_here = features.shape[1]
    heads_here = head_rate.shape[0]
    head_width = width_here // heads_here
    groups_here = input_proj.shape[1] // NSTATE
    per_group = heads_here // groups_here
    nblocks = tokens_here // BLOCK
    tail_rows = features[tokens_here - (KERNEL - 1) :]
    before = shifted(tail_rows, "ctx", 1)
    padded = jnp.concatenate([before, features], axis=0)
    summed_values = jnp.zeros(features.shape, jnp.float32) + conv_bias.astype(jnp.float32)[None, :]
    for start_offset in range(KERNEL):
        summed_values = summed_values + conv_weight[start_offset].astype(jnp.float32)[
            None, :
        ] * padded[start_offset : start_offset + tokens_here].astype(jnp.float32)
    filtered = (summed_values * jax.nn.sigmoid(summed_values)).astype(jnp.bfloat16)
    log_decay = -(head_rate[None, :] * (step_codes.astype(jnp.float32) / code_unit))
    cumulative = jnp.cumsum(log_decay.reshape(nblocks, BLOCK, heads_here), axis=1)
    block_total = cumulative[:, -1, :]
    filt_blocks = filtered.reshape(nblocks, BLOCK, heads_here, head_width)
    write_blocks = input_proj.reshape(nblocks, BLOCK, groups_here, NSTATE)
    read_blocks = output_proj.reshape(nblocks, BLOCK, groups_here, NSTATE)
    scores = jnp.einsum(
        "btgn,bjgn->bgtj", read_blocks, write_blocks, preferred_element_type=jnp.float32
    )
    cumul_heads = cumulative.transpose(0, 2, 1)
    causal = jnp.arange(BLOCK)[:, None] >= jnp.arange(BLOCK)[None, :]
    step_heads = math.gcd(8, per_group)
    nsteps = heads_here // step_heads

    def per_heads(position):
        head_start = position * step_heads
        group_index = head_start // per_group
        group_scores = lax.dynamic_index_in_dim(scores, group_index, 1, keepdims=False)
        group_writes = lax.dynamic_index_in_dim(write_blocks, group_index, 2, keepdims=False)
        cumul_part = lax.dynamic_slice_in_dim(cumul_heads, head_start, step_heads, 1)
        filt_part = lax.dynamic_slice_in_dim(filt_blocks, head_start, step_heads, 2)
        spread = cumul_part[..., :, None] - cumul_part[..., None, :]
        decays = jnp.where(causal, jnp.exp(jnp.where(causal, spread, 0.0)), 0.0)
        mixing = (decays * group_scores[:, None]).astype(jnp.bfloat16)
        interior_share = jnp.einsum(
            "bhtj,bjhp->bthp", mixing, filt_part, preferred_element_type=jnp.float32
        )
        end_weights = jnp.exp(cumul_part[..., -1:] - cumul_part).transpose(0, 2, 1)
        weighted = (end_weights[..., None] * filt_part.astype(jnp.float32)).astype(jnp.bfloat16)
        states_part = jnp.einsum(
            "bjhp,bjn->bhpn", weighted, group_writes, preferred_element_type=jnp.float32
        )
        return (interior_share, states_part)

    inside_steps, state_steps = lax.map(per_heads, jnp.arange(nsteps))
    inside = inside_steps.transpose(1, 2, 0, 3, 4).reshape(nblocks, BLOCK, heads_here, head_width)
    block_states = state_steps.transpose(1, 0, 2, 3, 4).reshape(
        nblocks, heads_here, head_width, NSTATE
    )

    def absorb(running, operands):
        return (jnp.exp(operands[1])[:, None, None] * running + operands[0], None)

    zero_state = jnp.zeros((heads_here, head_width, NSTATE), jnp.float32)
    device_state, _ = lax.scan(absorb, zero_state, (block_states, block_total))
    device_decay = jnp.sum(block_total, axis=0)
    all_decays = lax.all_gather(device_decay[None, :], "ctx", axis=0, tiled=True)
    owners = lax.axis_size("ctx")
    owner_id = lax.axis_index("ctx")
    row_share = heads_here * head_width // owners
    row_ids = owner_id * row_share + jnp.arange(row_share)
    selector = (row_ids[:, None] // head_width == jnp.arange(heads_here)[None, :]).astype(
        jnp.float32
    )
    row_decay = jnp.dot(all_decays, selector.T, precision=highest)
    inclusive = jnp.cumsum(row_decay, axis=0)
    exclusive = inclusive - row_decay
    lower = (jnp.arange(owners)[:, None] > jnp.arange(owners)[None, :])[:, :, None]
    weight_matrix = jnp.where(
        lower, jnp.exp(jnp.where(lower, exclusive[:, None, :] - inclusive[None, :, :], 0.0)), 0.0
    )
    portion = lax.all_to_all(
        device_state.reshape(heads_here * head_width, NSTATE),
        "ctx",
        split_axis=0,
        concat_axis=0,
        tiled=True,
    )
    columns = portion.shape[1]
    blocks = portion.reshape(owners, row_share, columns)
    prefix = jnp.einsum("efr,frc->erc", weight_matrix, blocks, precision=highest).reshape(
        owners * row_share, columns
    )
    settled = lax.all_to_all(
        prefix.astype(jnp.bfloat16), "ctx", split_axis=0, concat_axis=0, tiled=True
    ).astype(prefix.dtype)
    entering_run = settled.reshape(heads_here, head_width, NSTATE)

    def advance(running, operands):
        return (jnp.exp(operands[1])[:, None, None] * running + operands[0], running)

    _, entering = lax.scan(advance, entering_run, (block_states, block_total))
    carried_state = entering.astype(jnp.bfloat16).reshape(
        nblocks, groups_here, per_group, head_width, NSTATE
    )
    carried = jnp.einsum(
        "btgn,bgkpn->btgkp", read_blocks, carried_state, preferred_element_type=jnp.float32
    )
    carried = carried.reshape(nblocks, BLOCK, heads_here, head_width)
    output_pre = (
        inside
        + jnp.exp(cumulative)[..., None] * carried
        + bypass_factor[None, None, :, None] * filt_blocks.astype(jnp.float32)
    )
    gates = output_switch.reshape(nblocks, BLOCK, heads_here, head_width).astype(jnp.float32)
    gated = output_pre * gates * jax.nn.sigmoid(gates)
    meansq = jnp.mean(gated * gated, axis=-1, keepdims=True)
    normed = gated * lax.rsqrt(meansq + 1e-05) * norm_gain.reshape(heads_here, head_width)
    return normed.astype(jnp.bfloat16).reshape(tokens_here, width_here)


def solution(mesh):
    placed = (
        P(("groups", "ctx"), "head"),
        P(("groups", "ctx"), "head"),
        P(("groups", "ctx"), "head"),
        P(("groups", "ctx"), "head"),
        P(("groups", "ctx"), "head"),
        P("head"),
        P(None, "head"),
        P("head"),
        P("head"),
        P("head"),
    )
    return jax.shard_map(
        per_device,
        mesh=mesh,
        in_specs=placed,
        out_specs=P(("groups", "ctx"), "head"),
        check_vma=False,
    )
```

profile of v0, /device:TPU:0, one launch (start us, length us, event | category | flops | bytes accessed | tf_op | source)
XLA Modules:
  0.0 240.3 jit_solution(7668846057528088788)
XLA Ops:
  0.9 5.5 %collective-permute-start = (bf16[3,4096]{1,0:T(4,128)(2,1)S(1)}, bf16[3,4096]{1,0:T(4,128)(2,1)}, u32[]{:S(2)}, u32[]{:S(2)}) collective-permute-start(bf16[3,4096]{1,0:T(4,128)(2,1)S(1)} %slice.40), channel_id=1, source_target_pairs={{0,2},{2,4},{4,6},{6,8},{8,10},{10,12},{12,14},{1,3},{3,5},{5,7},{... | collective-permute-start | bytes 73736 | tf_op jit(solution)/shard_map/ppermute | solution.py:20
  7.1 1.0 copy_bitcast_fusion.1
  8.0 1.2 reduce-window.6
  9.5 1.6 slice_convert_fusion.3
  11.6 1.5 fusion.64
  13.1 1.5 convolution_bitcast_fusion.1
  14.6 6.4 %copy.70 = bf16[512,4096]{0,1:T(8,128)(2,1)} copy(bf16[512,4096]{1,0:T(8,128)(2,1)} %param.12) | data formatting | bytes 8388608 | tf_op args[0]
  22.0 1.3 copy.69
  23.3 16.3 %multiply_convert_fusion.7 = bf16[512,4096]{0,1:T(8,128)(2,1)} fusion(bf16[512,4096]{0,1:T(8,128)(2,1)} %copy.70, bf16[3,4096]{0,1:T(8,128)(2,1)S(1)} %copy.69, f32[4096]{0:T(1024)} %bitcast.166, f32[4096]{0:T(1024)} %bitcast.167, f32[4096]{0:T(1024)} %bitcast.165, f32[4096]{0:T(1024)} %bitcast.164, f32[4096]{0:T(1024)} %convert_element_type.115), kind=kLoop, calls=%fused_computation.39 | loop fusion | flops 54525952 | bytes 8495104 | tf_op jit(solution)/shard_map/convert_element_type | solution.py:50
  40.1 79.0 %while.11 = (s32[]{:T(128)}, f32[8,1,512,8,64]{2,4,3,1,0:T(8,128)}, f32[8,1,8,64,128]{4,3,2,1,0:T(8,128)}, s32[8]{0:T(128)}, bf16[1,512,64,64]{1,3,2,0:T(8,128)(...) while((s32[]{:T(128)}, f32[8,1,512,8,64]{2,4,3,1,0:T(8,128)}, ...), condition=%wide.region_3.4_spmd.clone.clone, body=%wide.region_2.3_spmd.clone.clone.sunk | while | flops 347082784 | bytes 6325746 | solution.py:85
  40.1 1.3 dynamic_slice.78
  43.3 4.6 %fusion.77 = f32[8,1,512,8,64]{2,4,3,1,0:T(8,128)} fusion(f32[8,1,512,8,64]{2,4,3,1,0:T(8,128)} %get-tuple-element.322, s32[]{:T(128)} %get-tuple-element.321, f32[512,512]{1,0:T(8,128)S(1)} %dynamic-slice_bitcast_fusion.2, f32[8,512]{1,0:T(8,128)S(1)} %get-tuple-element.303, pred[512,512]{1,0:T(8,128)(4,1)S(1)} %iota_compare_fusion.5, ...), kind=kOutput, calls=%fused_computation.5.clone.1 | convolution fusion | flops 278921216 | bytes 2916868 | tf_op jit(solution)/shard_map/while/body/eval_jaxpr/bhtj,bjhp->bthp/dot_general | solution.py:75
  47.9 2.1 fusion.78
  49.9 1.3 dynamic_slice.78
  53.1 4.6 %fusion.77 = f32[8,1,512,8,64]{2,4,3,1,0:T(8,128)} fusion(f32[8,1,512,8,64]{2,4,3,1,0:T(8,128)} %get-tuple-element.322, s32[]{:T(128)} %get-tuple-element.321, f32[512,512]{1,0:T(8,128)S(1)} %dynamic-slice_bitcast_fusion.2, f32[8,512]{1,0:T(8,128)S(1)} %get-tuple-element.303, pred[512,512]{1,0:T(8,128)(4,1)S(1)} %iota_compare_fusion.5, ...), kind=kOutput, calls=%fused_computation.5.clone.1 | convolution fusion | flops 278921216 | bytes 2916868 | tf_op jit(solution)/shard_map/while/body/eval_jaxpr/bhtj,bjhp->bthp/dot_general | solution.py:75
  57.8 2.1 fusion.78
  59.8 1.3 dynamic_slice.78
  63.0 4.6 %fusion.77 = f32[8,1,512,8,64]{2,4,3,1,0:T(8,128)} fusion(f32[8,1,512,8,64]{2,4,3,1,0:T(8,128)} %get-tuple-element.322, s32[]{:T(128)} %get-tuple-element.321, f32[512,512]{1,0:T(8,128)S(1)} %dynamic-slice_bitcast_fusion.2, f32[8,512]{1,0:T(8,128)S(1)} %get-tuple-element.303, pred[512,512]{1,0:T(8,128)(4,1)S(1)} %iota_compare_fusion.5, ...), kind=kOutput, calls=%fused_computation.5.clone.1 | convolution fusion | flops 278921216 | bytes 2916868 | tf_op jit(solution)/shard_map/while/body/eval_jaxpr/bhtj,bjhp->bthp/dot_general | solution.py:75
  67.6 2.1 fusion.78
  69.7 1.3 dynamic_slice.78
  72.9 4.6 %fusion.77 = f32[8,1,512,8,64]{2,4,3,1,0:T(8,128)} fusion(f32[8,1,512,8,64]{2,4,3,1,0:T(8,128)} %get-tuple-element.322, s32[]{:T(128)} %get-tuple-element.321, f32[512,512]{1,0:T(8,128)S(1)} %dynamic-slice_bitcast_fusion.2, f32[8,512]{1,0:T(8,128)S(1)} %get-tuple-element.303, pred[512,512]{1,0:T(8,128)(4,1)S(1)} %iota_compare_fusion.5, ...), kind=kOutput, calls=%fused_computation.5.clone.1 | convolution fusion | flops 278921216 | bytes 2916868 | tf_op jit(solution)/shard_map/while/body/eval_jaxpr/bhtj,bjhp->bthp/dot_general | solution.py:75
  77.5 2.1 fusion.78
  79.5 1.3 dynamic_slice.78
  82.8 4.6 %fusion.77 = f32[8,1,512,8,64]{2,4,3,1,0:T(8,128)} fusion(f32[8,1,512,8,64]{2,4,3,1,0:T(8,128)} %get-tuple-element.322, s32[]{:T(128)} %get-tuple-element.321, f32[512,512]{1,0:T(8,128)S(1)} %dynamic-slice_bitcast_fusion.2, f32[8,512]{1,0:T(8,128)S(1)} %get-tuple-element.303, pred[512,512]{1,0:T(8,128)(4,1)S(1)} %iota_compare_fusion.5, ...), kind=kOutput, calls=%fused_computation.5.clone.1 | convolution fusion | flops 278921216 | bytes 2916868 | tf_op jit(solution)/shard_map/while/body/eval_jaxpr/bhtj,bjhp->bthp/dot_general | solution.py:75
  87.4 2.1 fusion.78
  89.4 1.3 dynamic_slice.78
  92.6 4.6 %fusion.77 = f32[8,1,512,8,64]{2,4,3,1,0:T(8,128)} fusion(f32[8,1,512,8,64]{2,4,3,1,0:T(8,128)} %get-tuple-element.322, s32[]{:T(128)} %get-tuple-element.321, f32[512,512]{1,0:T(8,128)S(1)} %dynamic-slice_bitcast_fusion.2, f32[8,512]{1,0:T(8,128)S(1)} %get-tuple-element.303, pred[512,512]{1,0:T(8,128)(4,1)S(1)} %iota_compare_fusion.5, ...), kind=kOutput, calls=%fused_computation.5.clone.1 | convolution fusion | flops 278921216 | bytes 2916868 | tf_op jit(solution)/shard_map/while/body/eval_jaxpr/bhtj,bjhp->bthp/dot_general | solution.py:75
  97.2 2.0 fusion.78
  99.3 1.3 dynamic_slice.78
  102.5 4.6 %fusion.77 = f32[8,1,512,8,64]{2,4,3,1,0:T(8,128)} fusion(f32[8,1,512,8,64]{2,4,3,1,0:T(8,128)} %get-tuple-element.322, s32[]{:T(128)} %get-tuple-element.321, f32[512,512]{1,0:T(8,128)S(1)} %dynamic-slice_bitcast_fusion.2, f32[8,512]{1,0:T(8,128)S(1)} %get-tuple-element.303, pred[512,512]{1,0:T(8,128)(4,1)S(1)} %iota_compare_fusion.5, ...), kind=kOutput, calls=%fused_computation.5.clone.1 | convolution fusion | flops 278921216 | bytes 2916868 | tf_op jit(solution)/shard_map/while/body/eval_jaxpr/bhtj,bjhp->bthp/dot_general | solution.py:75
  107.1 2.0 fusion.78
  109.1 1.3 dynamic_slice.78
  112.4 4.6 %fusion.77 = f32[8,1,512,8,64]{2,4,3,1,0:T(8,128)} fusion(f32[8,1,512,8,64]{2,4,3,1,0:T(8,128)} %get-tuple-element.322, s32[]{:T(128)} %get-tuple-element.321, f32[512,512]{1,0:T(8,128)S(1)} %dynamic-slice_bitcast_fusion.2, f32[8,512]{1,0:T(8,128)S(1)} %get-tuple-element.303, pred[512,512]{1,0:T(8,128)(4,1)S(1)} %iota_compare_fusion.5, ...), kind=kOutput, calls=%fused_computation.5.clone.1 | convolution fusion | flops 278921216 | bytes 2916868 | tf_op jit(solution)/shard_map/while/body/eval_jaxpr/bhtj,bjhp->bthp/dot_general | solution.py:75
  117.0 2.1 fusion.78
  119.0 3.6 %bitcast_add_fusion.1 = f32[8,512,128]{2,1,0:T(8,128)} fusion(f32[8,1,8,64,128]{4,3,2,1,0:T(8,128)} %get-tuple-element.151, f32[8,512]{1,0:T(8,128)S(1)} %mul.275), kind=kLoop, calls=%fused_computation.47 | loop fusion | flops 524288 | bytes 4210688 | tf_op jit(solution)/shard_map/while/body/eval_jaxpr/add | solution.py:92
  122.6 4.3 %all-to-all-start = ((f32[8,512,128]{2,1,0:T(8,128)}), f32[8,512,128]{2,1,0:T(8,128)S(1)}, u32[]{:S(2)}, u32[]{:S(2)}) async-start(f32[8,512,128]{2,1,0:T(8,128)} %bitcast_add_fusion.1), calls=%async_computation | async-start | bytes 4194304 | tf_op jit(solution)/shard_map/all_to_all | solution.py:112
  127.0 48.8 %all-gather = f32[8,1,64]{2,1,0:T(1,128)S(1)} all-gather(f32[1,1,64]{2,1,0:T(1,128)S(1)} %copy.81), channel_id=2, replica_groups=mesh['groups'=2,'ctx'=8,'head'=2] {'ctx'}, dimensions={0}, use_global_device_ids=true | all-gather | bytes 2304 | tf_op jit(solution)/shard_map/all_gather | solution.py:97
  176.5 4.9 %fusion.43 = bf16[8,512,128]{2,0,1:T(8,128)(2,1)S(1)} fusion(f32[8,512,128]{2,1,0:T(8,128)S(1)} %all-to-all-done, f32[8,512]{0,1:T(8,128)S(1)} %copy.83, f32[8,512]{0,1:T(8,128)S(1)} %copy.82, pred[8,8]{1,0:T(8,128)(4,1)S(1)} %iota_compare_fusion.3), kind=kOutput, calls=%fused_computation.56 | convolution fusion | flops 50954240 | bytes 3178560 | tf_op jit(solution)/shard_map/efr,frc->erc/dot_general | solution.py:121
  181.4 1.2 copy.85
  182.6 10.7 %all-to-all-start.1 = ((bf16[8,512,128]{2,1,0:T(8,128)(2,1)}), bf16[8,512,128]{2,1,0:T(8,128)(2,1)S(1)}, u32[]{:S(2)}, u32[]{:S(2)}) async-start(bf16[8,512,128]{2,1,0:T(8,128)(2,1)} %copy.85), calls=%async_computation.1 | async-start | bytes 2097152 | tf_op jit(solution)/shard_map/all_to_all | solution.py:124
  193.4 6.4 %copy.87 = bf16[512,4096]{0,1:T(8,128)(2,1)} copy(bf16[512,4096]{1,0:T(8,128)(2,1)} %param.13) | data formatting | bytes 8388608 | tf_op args[1]
  200.0 16.5 %all-to-all-done.1 = bf16[8,512,128]{2,1,0:T(8,128)(2,1)S(1)} async-done(((bf16[8,512,128]{2,1,0:T(8,128)(2,1)}), bf16[8,512,128]{2,1,0:T(8,128)(2,1)S(1)}, u32[]{:S(2)}, u32[]{:S(2)}) %all-to-all-start.1) | async-done | bytes 1048608 | tf_op jit(solution)/shard_map/all_to_all | solution.py:124
  216.5 1.2 fusion.56
  217.8 0.9 copy-done
  218.7 1.3 copy-done.1
  220.0 7.7 %fusion.29 = f32[512,8,8]{0,2,1:T(8,128)S(1)} fusion(f32[8,1,512,8,64]{2,4,3,1,0:T(8,128)} %get-tuple-element.150, f32[1,512,8,8,64]{1,4,3,2,0:T(8,128)S(1)} %bitcast.149, f32[8,8]{1,0:T(8,128)S(1)} %mul.288, f32[512,8,8]{0,2,1:T(8,128)S(1)} %bitcast.158, bf16[1,512,8,8,64]{1,4,3,2,0:T(8,128)(2,1)S(1)} %bitcast.151, bf16[1,512,8,8,64]{1,4,3,2,0:T(8,128)(2,1)S(1)} %bitcast.153), kind=kLoop, calls=%fused_computation.38 | loop fusion | flops 27230208 | bytes 25428224 | tf_op jit(solution)/shard_map/reduce_sum | solution.py:147
  227.7 6.2 %fusion.24 = bf16[512,4096]{0,1:T(8,128)(2,1)} fusion(f32[2,32,64,512]{3,2,1,0:T(8,128)S(1)} %fusion.56, f32[8,1,512,8,64]{2,4,3,1,0:T(8,128)S(1)} %bitcast.155, f32[4096]{0:T(1024)S(1)} %copy-done.6, f32[512,64]{0,1:T(8,128)S(1)} %rsqrt_bitcast_fusion, f32[4096]{0:T(1024)S(1)} %mul.280, f32[512,64]{0,1:T(8,128)S(1)} %bitcast.159, ...), kind=kLoop, calls=%fused_computation.32 | loop fusion | flops 29360128 | bytes 29655040 | tf_op jit(solution)/shard_map/convert_element_type | solution.py:149
  233.9 6.3 %copy.88 = bf16[512,4096]{1,0:T(8,128)(2,1)} copy(bf16[512,4096]{0,1:T(8,128)(2,1)} %fusion.24) | data formatting | bytes 8388608 | tf_op jit(solution)/shard_map/convert_element_type | solution.py:149
  (102 shorter events, 14.1 us)
Async XLA Ops:
  0.0 21.0 %copy-start.2 = (bf16[512,256]{1,0:T(8,128)(2,1)S(1)}, bf16[512,256]{1,0:T(8,128)(2,1)}, u32[]{:S(2)}) copy-start(bf16[512,256]{1,0:T(8,128)(2,1)} %param.14) | copy-start | bytes 786436
  0.0 21.2 %copy-start.7 = (bf16[4096]{0:T(1024)(128)(2,1)S(1)}, bf16[4096]{0:T(1024)(128)(2,1)}, u32[]{:S(2)}) copy-start(bf16[4096]{0:T(1024)(128)(2,1)} %param.19) | copy-start | bytes 24580
  0.9 21.1 %collective-permute-start = (bf16[3,4096]{1,0:T(4,128)(2,1)S(1)}, bf16[3,4096]{1,0:T(4,128)(2,1)}, u32[]{:S(2)}, u32[]{:S(2)}) collective-permute-start(bf16[3,4096]{1,0:T(4,128)(2,1)S(1)} %slice.40), channel_id=1, source_target_pairs={{0,2},{2,4},{4,6},{6,8},{8,10},{10,12},{12,14},{1,3},{3,5},{5,7},{... | collective-permute-start | bytes 73736 | tf_op jit(solution)/shard_map/ppermute | solution.py:20
  11.6 10.4 %copy-start.4 = (f32[1,64,512]{2,0,1:T(1,128)}, f32[1,64,512]{2,0,1:T(1,128)S(1)}, u32[]{:S(2)}) copy-start(f32[1,64,512]{2,0,1:T(1,128)S(1)} %get-tuple-element.310) | copy-start | bytes 393220
  119.0 7.9 %copy-start.5 = (f32[1,1,64]{1,0,2:T(1,128)S(1)}, f32[1,1,64]{1,0,2:T(1,128)}, u32[]{:S(2)}) copy-start(f32[1,1,64]{1,0,2:T(1,128)} %get-tuple-element.246) | copy-start | bytes 772
  119.0 74.2 %copy-start.3 = (bf16[512,256]{1,0:T(8,128)(2,1)S(1)}, bf16[512,256]{1,0:T(8,128)(2,1)}, u32[]{:S(2)}) copy-start(bf16[512,256]{1,0:T(8,128)(2,1)} %param.15) | copy-start | bytes 786436
  122.6 53.9 %all-to-all-start = ((f32[8,512,128]{2,1,0:T(8,128)}), f32[8,512,128]{2,1,0:T(8,128)S(1)}, u32[]{:S(2)}, u32[]{:S(2)}) async-start(f32[8,512,128]{2,1,0:T(8,128)} %bitcast_add_fusion.1), calls=%async_computation | async-start | bytes 4194304 | tf_op jit(solution)/shard_map/all_to_all | solution.py:112
  176.5 23.3 %copy-start.8 = (f32[64]{0:T(128)S(1)}, f32[64]{0:T(128)}, u32[]{:S(2)}) copy-start(f32[64]{0:T(128)} %param.20) | copy-start | bytes 772
  182.6 34.0 %all-to-all-start.1 = ((bf16[8,512,128]{2,1,0:T(8,128)(2,1)}), bf16[8,512,128]{2,1,0:T(8,128)(2,1)S(1)}, u32[]{:S(2)}, u32[]{:S(2)}) async-start(bf16[8,512,128]{2,1,0:T(8,128)(2,1)} %copy.85), calls=%async_computation.1 | async-start | bytes 2097152 | tf_op jit(solution)/shard_map/all_to_all | solution.py:124
  216.5 2.2 copy-start
  216.5 3.5 %copy-start.1 = (bf16[512,4096]{0,1:T(8,128)(2,1)S(1)}, bf16[512,4096]{0,1:T(8,128)(2,1)}, u32[]{:S(2)}) copy-start(bf16[512,4096]{0,1:T(8,128)(2,1)} %copy.87) | copy-start | bytes 12582916
  216.5 11.2 %slice-start = ((s8[8388608]{0:T(1024)(128)(4,1)}), s8[4194304]{0:T(1024)(128)(4,1)S(1)}, s32[]{:S(2)}) async-start(s8[8388608]{0:T(1024)(128)(4,1)} %bitcast.154), calls=%async_computation.2 | async-start | bytes 8388608
  220.0 7.7 %slice-start.1 = ((s8[8388608]{0:T(1024)(128)(4,1)}), s8[4194304]{0:T(1024)(128)(4,1)S(1)}, s32[]{:S(2)}) async-start(s8[8388608]{0:T(1024)(128)(4,1)} %bitcast.154), calls=%async_computation.3 | async-start | bytes 8388608
  220.0 7.7 %copy-start.6 = (f32[4096]{0:T(1024)S(1)}, f32[4096]{0:T(1024)}, u32[]{:S(2)}) copy-start(f32[4096]{0:T(1024)} %param.21) | copy-start | bytes 49156
where the time goes:
time: 242 us; the launch traced here: 240 us
  matrix products  61.1 us (25%)
  blocking collectives  48.8 us (20%)
  local copies, waits for them, and re-layouts  45.2 us (19%)
  other arithmetic  41.8 us (17%)
  starting transfers between devices  20.5 us (8%)
  waiting for transfers between devices  16.5 us (7%)
  loops' own time  6.03 us (2%)
    all_gather x1, blocking collectives, per_device(): lax.all_gather(device_decay[None, :], 'ctx', axis=0, tiled=True)  48.8 us
    dot_general x8, matrix products, per_heads(): jnp.einsum('bhtj,bjhp->bthp', mixing, filt_part, preferred_element_type=j...  36.8 us
    all_to_all x1, waiting for transfers between devices, per_device(): lax.all_to_all(prefix.astype(jnp.bfloat16), 'ctx', split_axis=0, concat_a...  16.5 us
    dot_general x8, matrix products, per_heads(): jnp.einsum('bjhp,bjn->bhpn', weighted, group_writes, preferred_element_ty...  16.5 us
    convert_element_type x1, other arithmetic, per_device(): (summed_values * jax.nn.sigmoid(summed_values)).astype(jnp.bfloat16)  16.3 us
    unnamed x26, local copies, waits for them, and re-layouts  15.2 us
    all_to_all x1, starting transfers between devices, per_device(): lax.all_to_all(prefix.astype(jnp.bfloat16), 'ctx', split_axis=0, concat_a...  10.7 us
    dynamic_slice x8, local copies, waits for them, and re-layouts, per_device(): inside_steps, state_steps = lax.map(per_heads, jnp.arange(nsteps))  10.5 us
  transfers between devices with their start and end apart: 3, of which 1 were waited for; matrix products, arithmetic and copies ran while one was open for 10% of the time, Pallas kernels for 0%

commit v1 on v0

v1 whole, which is shorter than its diff:
```python
import functools
import math

import jax
import jax.numpy as jnp
from jax import lax
from jax.experimental import pallas as pl
from jax.experimental.pallas import tpu as pltpu
from jax.sharding import PartitionSpec as P

NSTATE = 128
KERNEL = 4
BLOCK = 512
HEAD_DIM = 64
SUB = 128
NSUB = BLOCK // SUB
CHUNKS = 4
LANES = 512
ILANES = 1024
TAIL = 8

f32 = jnp.float32
bf16 = jnp.bfloat16
LOG2E = math.log2(math.e)
VMEM_LIMIT = 40 * 1024 * 1024


def iota(shape, axis):
    return lax.broadcasted_iota(jnp.int32, shape, axis)


def dot(a, b):
    return jnp.dot(a, b, preferred_element_type=f32)


def half_tanh_gate(values):
    return values * (0.5 * jnp.tanh(0.5 * values) + 0.5)


def spread_matrix(first_head, heads, lanes):
    row = iota((4 * heads, lanes), 0)
    lane = iota((4 * heads, lanes), 1)
    hit = (row % heads) == first_head + lane // HEAD_DIM
    part = row // heads
    scale = jnp.where(part == 0, 65536.0, jnp.where(part == 1, 256.0, jnp.where(part == 2, 1.0, 0.0)))
    return jnp.where(hit, scale, 0.0).astype(bf16)


def prep_kernel(codes_ref, heads_ref, b_ref, c_ref, pieces_ref, left_ref, right_ref, scores_ref, bt_ref, rows_ref):
    tokens, heads = codes_ref.shape
    width = rows_ref.shape[1]
    groups = b_ref.shape[1] // NSTATE
    codes = codes_ref[...]
    split = jnp.concatenate([codes >> 8, codes & 255], axis=1).astype(f32).astype(bf16)
    causal = iota((SUB, SUB), 0) >= iota((SUB, SUB), 1)
    lower = jnp.where(causal, 1.0, 0.0).astype(bf16)
    sums = jnp.concatenate([dot(lower, split[s * SUB : (s + 1) * SUB]) for s in range(NSUB)], axis=0)
    whole = sums[:, :heads].astype(jnp.int32) * 256 + sums[:, heads:].astype(jnp.int32)
    first, second, third = whole >> 16, (whole >> 8) & 255, whole & 255
    pieces = jnp.concatenate([first, second, third, jnp.zeros_like(first)], axis=1).astype(f32).astype(bf16)
    pieces_ref[...] = pieces
    row = iota((4 * heads, 8 * heads), 0)
    col = iota((4 * heads, 8 * heads), 1)
    kind = col % 8
    same = ((row % heads) == col // 8) & (row < 3 * heads)
    to_left = jnp.where(same & (row // heads == kind), 1.0, 0.0).astype(bf16)
    col_kind = iota((tokens, 8 * heads), 1) % 8
    left = dot(pieces, to_left) + jnp.where((col_kind >= 3) & (col_kind < 6), 1.0, 0.0)
    left_ref[...] = left.astype(bf16)
    scale = jnp.where(kind == 3, -65536.0, jnp.where(kind == 4, -256.0, -1.0))
    to_right = jnp.where(same & (row // heads == kind - 3), scale, 0.0).astype(bf16)
    fixed = jnp.where(col_kind == 0, 65536.0, jnp.where(col_kind == 1, 256.0, jnp.where(col_kind == 2, 1.0, 0.0)))
    right = dot(pieces, to_right) + fixed
    right_ref[...] = right.T.astype(bf16)
    for g in range(groups):
        cols = slice(g * NSTATE, (g + 1) * NSTATE)
        bt = b_ref[:, cols].astype(f32).T.astype(bf16)
        bt_ref[cols, :] = bt
        for s in range(NSUB):
            rows = slice(s * SUB, (s + 1) * SUB)
            scores = dot(c_ref[rows, cols], bt[:, rows])
            scores_ref[g, rows, :] = jnp.where(causal, scores, 0.0)
    spread = jnp.where(iota((heads, width), 0) == iota((heads, width), 1) // HEAD_DIM, 1.0, 0.0)
    totals = jnp.concatenate(
        [whole[(s + 1) * SUB - 1 : (s + 1) * SUB] for s in range(NSUB)], axis=0
    ).astype(f32)
    small = jnp.concatenate([heads_ref[...], totals, jnp.zeros_like(totals)], axis=0)
    wide = jnp.dot(small, spread, precision=lax.Precision.HIGHEST, preferred_element_type=f32)
    rate = wide[0:1] * (-LOG2E / 1024.0)
    base = jnp.zeros_like(rate)
    rows_ref[0:1, :] = rate
    rows_ref[1:2, :] = wide[1:2]
    for s in range(NSUB):
        total = wide[8 + s : 9 + s]
        rows_ref[2 + s : 3 + s, :] = jnp.exp2(rate * total)
        rows_ref[8 + s : 9 + s, :] = jnp.exp2(rate * base)
        base = base + total
    rows_ref[6:7, :] = jnp.exp2(rate * base)
    rows_ref[7:8, :] = jnp.zeros_like(rate)
    rows_ref[12:16, :] = jnp.zeros((4, width), f32)


def state_kernel(first_block, x_ref, tail_ref, w_ref, bias_ref, pieces_ref, bt_ref, rows_ref, f_ref, local_ref, state_ref):
    lanes = x_ref.shape[1]
    heads = pieces_ref.shape[1] // 4
    first_head = (first_block + pl.program_id(0)) * (lanes // HEAD_DIM)
    padded = jnp.concatenate([tail_ref[...].astype(f32), x_ref[...].astype(f32)], axis=0)
    weights = w_ref[...].astype(f32)
    summed = bias_ref[...].astype(f32) + weights[KERNEL - 1 : KERNEL] * padded[TAIL:]
    for back in range(1, KERNEL):
        moved = pltpu.roll(padded, back, 0)[TAIL:]
        summed = summed + weights[KERNEL - 1 - back : KERNEL - back] * moved
    filtered = half_tanh_gate(summed).astype(bf16)
    f_ref[...] = filtered
    spread = spread_matrix(first_head, heads, lanes)
    rate = rows_ref[0:1, :]
    running = None
    for s in range(NSUB):
        rows = slice(s * SUB, (s + 1) * SUB)
        wide = dot(pieces_ref[rows, :], spread)
        weight = jnp.exp2(rate * (wide[SUB - 1 : SUB] - wide))
        weighted = (weight * filtered[rows].astype(f32)).astype(bf16)
        part = dot(bt_ref[:, rows], weighted)
        running = part if s == 0 else rows_ref[2 + s : 3 + s, :] * running + part
        if s < NSUB - 1:
            local_ref[s] = running.astype(bf16)
    state_ref[...] = running.astype(bf16)


def inside_kernel(first_block, per_block, f_ref, local_ref, z_ref, c_ref, pieces_ref, left_ref, right_ref, scores_ref, rows_ref, rate_ref, p_ref, g_ref, wall):
    lanes = f_ref.shape[1]
    here = lanes // HEAD_DIM
    heads = pieces_ref.shape[1] // 4
    first_head = (first_block + pl.program_id(0)) * here
    spread = spread_matrix(first_head, heads, lanes)
    rate = rows_ref[0:1, :]
    bypass = rows_ref[1:2, :]
    wall[...] = jnp.zeros_like(wall)
    upper = iota((16, SUB), 0) < 8
    first_lanes = iota((SUB, 128), 1) < HEAD_DIM
    for s in range(NSUB):
        rows = slice(s * SUB, (s + 1) * SUB)
        for q in range(here // 2):
            tile = right_ref[16 * q : 16 * q + 16, rows].astype(f32)
            wall[16 * q : 16 * q + 16, 2 * q * SUB : (2 * q + 1) * SUB] = jnp.where(upper, tile, 0.0).astype(bf16)
            wall[16 * q : 16 * q + 16, (2 * q + 1) * SUB : (2 * q + 2) * SUB] = jnp.where(upper, 0.0, tile).astype(bf16)
        scores = scores_ref[0, rows, :]
        left = left_ref[rows, :]
        wide = dot(pieces_ref[rows, :], spread)
        growth = jnp.exp2(rate * wide)
        filtered = f_ref[rows, :].astype(f32)
        gate = half_tanh_gate(z_ref[rows, :].astype(f32))
        g_ref[rows, :] = (gate * growth * rows_ref[8 + s : 9 + s, :]).astype(bf16)
        total = bypass * filtered
        if s > 0:
            total = total + growth * dot(c_ref[rows, :], local_ref[s - 1])
        for q in range(here // 2):
            spans = dot(left, wall[:, 2 * q * SUB : (2 * q + 2) * SUB])
            mixing = []
            for k in range(2):
                scale = rate_ref[first_head + 2 * q + k] * (-LOG2E / 1024.0)
                decays = jnp.exp2(jnp.maximum(spans[:, k * SUB : (k + 1) * SUB], 0.0) * scale)
                mixing.append((decays * scores).astype(bf16))
            mine = filtered[:, 128 * q : 128 * q + 128]
            stacked = jnp.concatenate(
                [jnp.where(first_lanes, mine, 0.0), jnp.where(first_lanes, 0.0, mine)], axis=0
            ).astype(bf16)
            inside = dot(jnp.concatenate(mixing, axis=1), stacked)
            cols = slice(128 * q, 128 * q + 128)
            p_ref[rows, cols] = ((total[:, cols] + inside) * gate[:, cols]).astype(bf16)


def final_kernel(p_ref, g_ref, e_ref, c_ref, gain_ref, *rest):
    out_ref = rest[-1]
    lanes = p_ref.shape[1]
    same = iota((256, 256), 0) // HEAD_DIM == iota((256, 256), 1) // HEAD_DIM
    mean = jnp.where(same, 1.0 / HEAD_DIM, 0.0).astype(bf16)
    for q in range(lanes // 256):
        cols = slice(256 * q, 256 * q + 256)
        carried = dot(c_ref[...], e_ref[:, cols])
        gated = p_ref[:, cols].astype(f32) + carried * g_ref[:, cols].astype(f32)
        meansq = dot((gated * gated).astype(bf16), mean)
        out_ref[:, cols] = (gated * lax.rsqrt(meansq + 1e-05) * gain_ref[:, cols]).astype(bf16)


def params():
    return pltpu.CompilerParams(vmem_limit_bytes=VMEM_LIMIT)


def full(shape):
    return pl.BlockSpec(shape, lambda i: (0,) * len(shape))


def per_device(
    features,
    output_switch,
    input_proj,
    output_proj,
    step_codes,
    head_rate,
    conv_weight,
    conv_bias,
    bypass_factor,
    norm_gain,
):
    tokens, width = features.shape
    heads = head_rate.shape[0]
    groups = input_proj.shape[1] // NSTATE
    assert tokens == BLOCK and width == heads * HEAD_DIM
    runs = lax.axis_size("ctx")
    pairs = runs // 2
    odd = lax.axis_index("ctx") % 2 == 1
    swap = [(i, i ^ 1) for i in range(runs)]

    tail = lax.ppermute(features[tokens - TAIL :], "ctx", [(i, i + 1) for i in range(runs - 1)])

    def shape(dims, dtype):
        return jax.ShapeDtypeStruct(dims, dtype)

    small = jnp.concatenate([head_rate[None], bypass_factor[None], jnp.zeros((6, heads), f32)], axis=0)
    pieces, left, right, scores, bt, rows = pl.pallas_call(
        prep_kernel,
        out_shape=(
            shape((tokens, 4 * heads), bf16),
            shape((tokens, 8 * heads), bf16),
            shape((8 * heads, tokens), bf16),
            shape((groups, tokens, SUB), f32),
            shape((groups * NSTATE, tokens), bf16),
            shape((16, width), f32),
        ),
        compiler_params=params(),
        cost_estimate=pl.CostEstimate(flops=1 << 28, bytes_accessed=1 << 22, transcendentals=0),
    )(step_codes, small, input_proj, output_proj)

    decay_own = rows[6:7]
    decay_other = lax.ppermute(decay_own, "ctx", swap)
    decay_even = jnp.where(odd, decay_other, decay_own)
    decay_odd = jnp.where(odd, decay_own, decay_other)
    decay_pair = decay_even * decay_odd

    bias = conv_bias[None]
    gain = norm_gain[None]
    share = width // CHUNKS
    group_width = width // groups
    half = NSTATE // 2

    def conv_states(c):
        steps = share // LANES
        first = c * steps
        column = lambda i: (0, first + i)
        return pl.pallas_call(
            functools.partial(state_kernel, first),
            grid=(steps,),
            in_specs=[
                pl.BlockSpec((tokens, LANES), column),
                pl.BlockSpec((TAIL, LANES), column),
                pl.BlockSpec((KERNEL, LANES), column),
                pl.BlockSpec((1, LANES), column),
                full((tokens, 4 * heads)),
                pl.BlockSpec((NSTATE, tokens), lambda i: ((first + i) * LANES // group_width, 0)),
                pl.BlockSpec((16, LANES), column),
            ],
            out_specs=[
                pl.BlockSpec((tokens, LANES), lambda i: (0, i)),
                pl.BlockSpec((NSUB - 1, NSTATE, LANES), lambda i: (0, 0, i)),
                pl.BlockSpec((NSTATE, LANES), lambda i: (0, i)),
            ],
            out_shape=(
                shape((tokens, share), bf16),
                shape((NSUB - 1, NSTATE, share), bf16),
                shape((NSTATE, share), bf16),
            ),
            compiler_params=params(),
            cost_estimate=pl.CostEstimate(flops=1 << 30, bytes_accessed=3 << 20, transcendentals=0),
        )(features, tail, conv_weight, bias, pieces, bt, rows)

    def inside(c, filtered, local):
        steps = share // ILANES
        first = c * steps
        block_heads = ILANES // HEAD_DIM
        column = lambda i: (0, first + i)
        return pl.pallas_call(
            functools.partial(inside_kernel, first, block_heads),
            grid=(steps,),
            in_specs=[
                pl.BlockSpec((tokens, ILANES), lambda i: (0, i)),
                pl.BlockSpec((NSUB - 1, NSTATE, ILANES), lambda i: (0, 0, i)),
                pl.BlockSpec((tokens, ILANES), column),
                pl.BlockSpec((tokens, NSTATE), lambda i: (0, (first + i) * ILANES // group_width)),
                full((tokens, 4 * heads)),
                pl.BlockSpec((tokens, 8 * block_heads), column),
                pl.BlockSpec((8 * block_heads, tokens), lambda i: (first + i, 0)),
                pl.BlockSpec((1, tokens, SUB), lambda i: ((first + i) * ILANES // group_width, 0, 0)),
                pl.BlockSpec((16, ILANES), column),
                pl.BlockSpec(memory_space=pltpu.SMEM),
            ],
            out_specs=[
                pl.BlockSpec((tokens, ILANES), lambda i: (0, i)),
                pl.BlockSpec((tokens, ILANES), lambda i: (0, i)),
            ],
            out_shape=(shape((tokens, share), bf16), shape((tokens, share), bf16)),
            scratch_shapes=[pltpu.VMEM((8 * block_heads, block_heads * SUB), bf16)],
            compiler_params=params(),
            cost_estimate=pl.CostEstimate(flops=3 << 30, bytes_accessed=5 << 20, transcendentals=0),
        )(filtered, local, output_switch, output_proj, pieces, left, right, scores, rows, head_rate)

    def final(c, out, kept, growth, entering):
        steps = share // LANES
        first = c * steps
        column = lambda i: (0, first + i)
        mine = lambda i: (0, i)
        operands = [kept, growth, entering, output_proj, gain]
        in_specs = [
            pl.BlockSpec((tokens, LANES), mine),
            pl.BlockSpec((tokens, LANES), mine),
            pl.BlockSpec((NSTATE, LANES), mine),
            pl.BlockSpec((tokens, NSTATE), lambda i: (0, (first + i) * LANES // group_width)),
            pl.BlockSpec((1, LANES), column),
        ]
        aliases = {}
        if out is not None:
            aliases = {len(operands): 0}
            operands.append(out)
            in_specs.append(pl.BlockSpec(memory_space=pl.ANY))
        return pl.pallas_call(
            final_kernel,
            grid=(steps,),
            in_specs=in_specs,
            out_specs=pl.BlockSpec((tokens, LANES), column),
            out_shape=shape((tokens, width), bf16),
            input_output_aliases=aliases,
            compiler_params=params(),
            cost_estimate=pl.CostEstimate(flops=1 << 29, bytes_accessed=3 << 20, transcendentals=0),
        )(*operands)

    def carry(c, state):
        cols = slice(c * share, (c + 1) * share)
        even, pair = decay_even[:, cols], decay_pair[:, cols]
        later = decay_odd[:, cols]
        low, high = state[:half], state[half:]
        own = jnp.where(odd, high, low)
        got = lax.ppermute(jnp.where(odd, low, high), "ctx", swap)
        before = jnp.where(odd, got, own).astype(f32)
        after = jnp.where(odd, own, got).astype(f32)
        both = later * before + after
        entering = jnp.zeros_like(both)
        for step in range(pairs - 1):
            sent = (pair * entering + both).astype(bf16)
            route = [(2 * step + k, 2 * step + 2 + k) for k in range(2)]
            entering = entering + lax.ppermute(sent, "ctx", route).astype(f32)
        between = (even * entering + before).astype(bf16)
        entering = entering.astype(bf16)
        mine = jnp.where(odd, between, entering)
        other = lax.ppermute(jnp.where(odd, entering, between), "ctx", swap)
        return jnp.concatenate([jnp.where(odd, other, mine), jnp.where(odd, mine, other)], axis=0)

    parts = [conv_states(c) for c in range(CHUNKS)]
    insides = [inside(c, parts[c][0], parts[c][1]) for c in range(CHUNKS)]
    entering = [carry(c, parts[c][2]) for c in range(CHUNKS)]
    out = None
    for c in range(CHUNKS):
        out = final(c, out, insides[c][0], insides[c][1], entering[c])
    return out


def solution(mesh):
    placed = (
        P(("groups", "ctx"), "head"),
        P(("groups", "ctx"), "head"),
        P(("groups", "ctx"), "head"),
        P(("groups", "ctx"), "head"),
        P(("groups", "ctx"), "head"),
        P("head"),
        P(None, "head"),
        P("head"),
        P("head"),
        P("head"),
    )
    return jax.shard_map(
        per_device,
        mesh=mesh,
        in_specs=placed,
        out_specs=P(("groups", "ctx"), "head"),
        check_vma=False,
    )
```

time: 242 us -> 90.9 us (0.38)
  the two profiles are of different devices: /device:TPU:0 before, /device:TPU:16 now
where the time goes in v1:
time: 90.9 us; the launch traced here: 90.4 us
  Pallas kernels  37.2 us (41%)
  starting transfers between devices  25.3 us (28%)
  waiting for transfers between devices  15.6 us (17%)
  local copies, waits for them, and re-layouts  9.15 us (10%)
  other arithmetic  2.5 us (3%)
    pallas_call x4, Pallas kernels, conv_states(): pl.pallas_call(functools.partial(state_kernel, first), grid=(steps,), in_...  15.1 us
    ppermute x12, starting transfers between devices, carry(): entering = entering + lax.ppermute(sent, 'ctx', route).astype(f32)  13.3 us
    pallas_call x4, Pallas kernels, inside(): pl.pallas_call(functools.partial(inside_kernel, first, block_heads), grid...  11.9 us
    pallas_call x4, Pallas kernels, final(): pl.pallas_call(final_kernel, grid=(steps,), in_specs=in_specs, out_specs=...  8.78 us
    unnamed x25, local copies, waits for them, and re-layouts  7.49 us
    ppermute x12, waiting for transfers between devices, carry(): entering = entering + lax.ppermute(sent, 'ctx', route).astype(f32)  6.29 us
    ppermute x4, waiting for transfers between devices, carry(): other = lax.ppermute(jnp.where(odd, entering, between), 'ctx', swap)  5.5 us
    ppermute x4, starting transfers between devices, carry(): got = lax.ppermute(jnp.where(odd, low, high), 'ctx', swap)  4.28 us
  transfers between devices with their start and end apart: 22, of which 9 were waited for; matrix products, arithmetic and copies ran while one was open for 4% of the time, Pallas kernels for 26%

profile of v1, /device:TPU:16, one launch (start us, length us, event | category | flops | bytes accessed | tf_op | source)
XLA Modules:
  0.0 90.4 jit_solution(14356909719294350579)
XLA Ops:
  0.0 1.0 %copy.14.codes_ref = s32[512,64]{1,0:T(8,128)S(1)} copy(s32[512,64]{0,1:T(8,128)} %param.14) | data formatting | bytes 262144 | tf_op args[4]
  1.1 0.7 maximum_maximum_fusion.heads_ref
  1.9 0.9 %copy-done.1 = bf16[512,256]{1,0:T(8,128)(2,1)S(1)} copy-done((bf16[512,256]{1,0:T(8,128)(2,1)S(1)}, bf16[512,256]{1,0:T(8,128)(2,1)}, u32[]{:S(2)}) %copy-start.1) | copy-done | bytes 262168
  2.8 0.9 %copy-done.7 = bf16[512,256]{1,0:T(8,128)(2,1)S(1)} copy-done((bf16[512,256]{1,0:T(8,128)(2,1)S(1)}, bf16[512,256]{1,0:T(8,128)(2,1)}, u32[]{:S(2)}) %copy-start.7) | copy-done | bytes 262168
  3.8 1.4 %shard_map.100 = (bf16[512,256]{1,0:T(8,128)(2,1)S(1)}, bf16[512,512]{1,0:T(8,128)(2,1)S(1)}, bf16[512,512]{1,0:T(8,128)(2,1)S(1)}, f32[2,512,128]{2,1,0:T(8,128...) custom-call(s32[512,64]{1,0:T(8,128)S(1)} %copy.14.codes_ref, f32[8,64]{1,0:T(8,128)S(1)} %maximum_maximum_fusion.heads_ref, ...), custom_call_target="tpu_custom_call" | custom-call | flops 268435456 | bytes 4194304 | tf_op jit(solution)/shard_map/pallas_call | solution.py:221
  5.1 0.8 copy-done.8
  5.9 0.8 copy-done.10
  6.7 1.6 %collective-permute-start.1 = (f32[1,4096]{1,0:T(1,128)S(1)}, f32[1,4096]{1,0:T(1,128)S(1)}, u32[]{:S(2)}, u32[]{:S(2)}) collective-permute-start(f32[1,4096]{1,0:T(1,128)S(1)} %slice.67), channel_id=1, source_target_pairs={{0,2},{2,0},{4,6},{6,4},{8,10},{10,8},{12,14},{14,12},{1,3},{3,1},... | collective-permute-start | bytes 49160 | tf_op jit(solution)/shard_map/ppermute | solution.py:236
  8.3 0.8 slice.66
  9.2 2.4 %collective-permute-start = (bf16[8,4096]{1,0:T(8,128)(2,1)S(1)}, bf16[8,4096]{1,0:T(8,128)(2,1)S(1)}, u32[]{:S(2)}, u32[]{:S(2)}) collective-permute-start(bf16[8,4096]{1,0:T(8,128)(2,1)S(1)} %slice.66), channel_id=1, source_target_pairs={{0,2},{2,4},{4,6},{6,8},{8,10},{10,12},{12,14},{1,3},{3,5},{5,7},{... | collective-permute-start | bytes 196616 | tf_op jit(solution)/shard_map/ppermute | solution.py:215
  11.6 0.7 broadcast_in_dim.15.bias_ref
  12.4 3.8 %collective-permute-done.tail_ref = bf16[8,4096]{1,0:T(8,128)(2,1)S(1)} collective-permute-done((bf16[8,4096]{1,0:T(8,128)(2,1)S(1)}, bf16[8,4096]{1,0:T(8,128)(2,1)S(1)}, u32[]{:S(2)}, u32[]{:S(2)}) %collective-permute-start) | collective-permute-done | bytes 65568 | tf_op jit(solution)/shard_map/ppermute | solution.py:215
  16.2 2.2 %copy-done = bf16[512,4096]{1,0:T(8,128)(2,1)S(1)} copy-done((bf16[512,4096]{1,0:T(8,128)(2,1)S(1)}, bf16[512,4096]{1,0:T(8,128)(2,1)}, u32[]{:S(2)}) %copy-start) | copy-done | bytes 4194328
  18.4 0.8 copy-done.3
  19.2 3.7 %shard_map.107 = (bf16[512,1024]{1,0:T(8,128)(2,1)S(1)}, bf16[3,128,1024]{2,1,0:T(8,128)(2,1)S(1)}, bf16[128,1024]{1,0:T(8,128)(2,1)S(1)}) custom-call(bf16[512,4096]{1,0:T(8,128)(2,1)S(1)} %copy-done, bf16[8,4096]{1,0:T(8,128)(2,1)S(1)} %collective-permute-done.tail_ref, bf16[4,4096]{1,0:T(4,128)(2,1)S(1)} %copy-done.3, ...), custom_call_target="tpu_custom_call" | custom-call | flops 1073741824 | bytes 3145728 | tf_op jit(solution)/shard_map/pallas_call | solution.py:251
  23.0 3.8 %shard_map.105 = (bf16[512,1024]{1,0:T(8,128)(2,1)S(1)}, bf16[3,128,1024]{2,1,0:T(8,128)(2,1)S(1)}, bf16[128,1024]{1,0:T(8,128)(2,1)S(1)}) custom-call(bf16[512,4096]{1,0:T(8,128)(2,1)S(1)} %copy-done, bf16[8,4096]{1,0:T(8,128)(2,1)S(1)} %collective-permute-done.tail_ref, bf16[4,4096]{1,0:T(4,128)(2,1)S(1)} %copy-done.3, ...), custom_call_target="tpu_custom_call" | custom-call | flops 1073741824 | bytes 3145728 | tf_op jit(solution)/shard_map/pallas_call | solution.py:251
  26.8 2.1 %collective-permute-start.12 = (bf16[64,1024]{1,0:T(8,128)(2,1)S(1)}, bf16[64,1024]{1,0:T(8,128)(2,1)S(1)}, u32[]{:S(2)}, u32[]{:S(2)}) collective-permute-start(bf16[64,1024]{1,0:T(8,128)(2,1)S(1)} %broadcast_select_fusion.15), channel_id=1, source_target_pairs={{0,2},{2,0},{4,6},{6,4},{8,10},{10,8},{12,14},{14,12},{1,3},{3,1},... | collective-permute-start | bytes 393224 | tf_op jit(solution)/shard_map/ppermute | solution.py:342
  28.8 3.7 %shard_map.103 = (bf16[512,1024]{1,0:T(8,128)(2,1)S(1)}, bf16[3,128,1024]{2,1,0:T(8,128)(2,1)S(1)}, bf16[128,1024]{1,0:T(8,128)(2,1)S(1)}) custom-call(bf16[512,4096]{1,0:T(8,128)(2,1)S(1)} %copy-done, bf16[8,4096]{1,0:T(8,128)(2,1)S(1)} %collective-permute-done.tail_ref, bf16[4,4096]{1,0:T(4,128)(2,1)S(1)} %copy-done.3, ...), custom_call_target="tpu_custom_call" | custom-call | flops 1073741824 | bytes 3145728 | tf_op jit(solution)/shard_map/pallas_call | solution.py:251
  32.8 3.9 %shard_map.101 = (bf16[512,1024]{1,0:T(8,128)(2,1)S(1)}, bf16[3,128,1024]{2,1,0:T(8,128)(2,1)S(1)}, bf16[128,1024]{1,0:T(8,128)(2,1)S(1)}) custom-call(bf16[512,4096]{1,0:T(8,128)(2,1)S(1)} %copy-done, bf16[8,4096]{1,0:T(8,128)(2,1)S(1)} %collective-permute-done.tail_ref, bf16[4,4096]{1,0:T(4,128)(2,1)S(1)} %copy-done.3, ...), custom_call_target="tpu_custom_call" | custom-call | flops 1073741824 | bytes 3145728 | tf_op jit(solution)/shard_map/pallas_call | solution.py:251
  36.7 2.0 %collective-permute-start.2 = (bf16[64,1024]{1,0:T(8,128)(2,1)S(1)}, bf16[64,1024]{1,0:T(8,128)(2,1)S(1)}, u32[]{:S(2)}, u32[]{:S(2)}) collective-permute-start(bf16[64,1024]{1,0:T(8,128)(2,1)S(1)} %broadcast_select_fusion.31), channel_id=1, source_target_pairs={{0,2},{2,0},{4,6},{6,4},{8,10},{10,8},{12,14},{14,12},{1,3},{3,1},... | collective-permute-start | bytes 393224 | tf_op jit(solution)/shard_map/ppermute | solution.py:342
  38.8 3.0 %shard_map.108 = (bf16[512,1024]{1,0:T(8,128)(2,1)S(1)}, bf16[512,1024]{1,0:T(8,128)(2,1)S(1)}) custom-call(bf16[512,1024]{1,0:T(8,128)(2,1)S(1)} %get-tuple-element.52.f_ref, bf16[3,128,1024]{2,1,0:T(8,128)(2,1)S(1)} %get-tuple-element.53.local_ref, bf16[512,4096]{1,0:T(8,128)(2,1)S(1)} %copy-done.6, bf16[512,256]{1,0:T(8,128)(2,1)S(1)} %copy-done.2, ...), custom_call_target="tpu_custom_call" | custom-call | flops 3221225472 | bytes 5242880 | tf_op jit(solution)/shard_map/pallas_call | solution.py:282
  41.7 3.1 %shard_map.106 = (bf16[512,1024]{1,0:T(8,128)(2,1)S(1)}, bf16[512,1024]{1,0:T(8,128)(2,1)S(1)}) custom-call(bf16[512,1024]{1,0:T(8,128)(2,1)S(1)} %get-tuple-element.47.f_ref, bf16[3,128,1024]{2,1,0:T(8,128)(2,1)S(1)} %get-tuple-element.48.local_ref, bf16[512,4096]{1,0:T(8,128)(2,1)S(1)} %copy-done.6, bf16[512,256]{1,0:T(8,128)(2,1)S(1)} %copy-done.2, ...), custom_call_target="tpu_custom_call" | custom-call | flops 3221225472 | bytes 5242880 | tf_op jit(solution)/shard_map/pallas_call | solution.py:282
  44.8 3.0 %shard_map.104 = (bf16[512,1024]{1,0:T(8,128)(2,1)S(1)}, bf16[512,1024]{1,0:T(8,128)(2,1)S(1)}) custom-call(bf16[512,1024]{1,0:T(8,128)(2,1)S(1)} %get-tuple-element.42.f_ref, bf16[3,128,1024]{2,1,0:T(8,128)(2,1)S(1)} %get-tuple-element.43.local_ref, bf16[512,4096]{1,0:T(8,128)(2,1)S(1)} %copy-done.6, bf16[512,256]{1,0:T(8,128)(2,1)S(1)} %copy-done.2, ...), custom_call_target="tpu_custom_call" | custom-call | flops 3221225472 | bytes 5242880 | tf_op jit(solution)/shard_map/pallas_call | solution.py:282
  47.8 2.9 %shard_map.102 = (bf16[512,1024]{1,0:T(8,128)(2,1)S(1)}, bf16[512,1024]{1,0:T(8,128)(2,1)S(1)}) custom-call(bf16[512,1024]{1,0:T(8,128)(2,1)S(1)} %get-tuple-element.34.f_ref, bf16[3,128,1024]{2,1,0:T(8,128)(2,1)S(1)} %get-tuple-element.35.local_ref, bf16[512,4096]{1,0:T(8,128)(2,1)S(1)} %copy-done.6, bf16[512,256]{1,0:T(8,128)(2,1)S(1)} %copy-done.2, ...), custom_call_target="tpu_custom_call" | custom-call | flops 3221225472 | bytes 5242880 | tf_op jit(solution)/shard_map/pallas_call | solution.py:282
  50.9 0.7 collective-permute-start.18
  51.6 0.7 collective-permute-start.13
  52.4 0.7 collective-permute-start.8
  53.2 0.7 collective-permute-start.3
  54.0 1.3 %collective-permute-start.19 = (bf16[64,1024]{1,0:T(8,128)(2,1)S(1)}, bf16[64,1024]{1,0:T(8,128)(2,1)S(1)}, u32[]{:S(2)}, u32[]{:S(2)}) collective-permute-start(bf16[64,1024]{1,0:T(8,128)(2,1)S(1)} %fusion.15), channel_id=1, source_target_pairs={{4,8},{6,10},{5,9},{7,11},{20,24},{22,26},{21,25},{23,27}} | collective-permute-start | bytes 393224 | tf_op jit(solution)/shard_map/ppermute | solution.py:350
  55.4 1.3 %collective-permute-start.14 = (bf16[64,1024]{1,0:T(8,128)(2,1)S(1)}, bf16[64,1024]{1,0:T(8,128)(2,1)S(1)}, u32[]{:S(2)}, u32[]{:S(2)}) collective-permute-start(bf16[64,1024]{1,0:T(8,128)(2,1)S(1)} %fusion.11), channel_id=1, source_target_pairs={{4,8},{6,10},{5,9},{7,11},{20,24},{22,26},{21,25},{23,27}} | collective-permute-start | bytes 393224 | tf_op jit(solution)/shard_map/ppermute | solution.py:350
  56.8 1.3 %collective-permute-start.9 = (bf16[64,1024]{1,0:T(8,128)(2,1)S(1)}, bf16[64,1024]{1,0:T(8,128)(2,1)S(1)}, u32[]{:S(2)}, u32[]{:S(2)}) collective-permute-start(bf16[64,1024]{1,0:T(8,128)(2,1)S(1)} %fusion.7), channel_id=1, source_target_pairs={{4,8},{6,10},{5,9},{7,11},{20,24},{22,26},{21,25},{23,27}} | collective-permute-start | bytes 393224 | tf_op jit(solution)/shard_map/ppermute | solution.py:350
  58.2 1.3 %collective-permute-start.4 = (bf16[64,1024]{1,0:T(8,128)(2,1)S(1)}, bf16[64,1024]{1,0:T(8,128)(2,1)S(1)}, u32[]{:S(2)}, u32[]{:S(2)}) collective-permute-start(bf16[64,1024]{1,0:T(8,128)(2,1)S(1)} %fusion.3), channel_id=1, source_target_pairs={{4,8},{6,10},{5,9},{7,11},{20,24},{22,26},{21,25},{23,27}} | collective-permute-start | bytes 393224 | tf_op jit(solution)/shard_map/ppermute | solution.py:350
  59.5 5.2 %collective-permute-done.19 = bf16[64,1024]{1,0:T(8,128)(2,1)S(1)} collective-permute-done((bf16[64,1024]{1,0:T(8,128)(2,1)S(1)}, bf16[64,1024]{1,0:T(8,128)(2,1)S(1)}, u32[]{:S(2)}, u32[]{:S(2)}) %collective-permute-start.19) | collective-permute-done | bytes 131104 | tf_op jit(solution)/shard_map/ppermute | solution.py:350
  64.8 1.3 %collective-permute-start.20 = (bf16[64,1024]{1,0:T(8,128)(2,1)S(1)}, bf16[64,1024]{1,0:T(8,128)(2,1)S(1)}, u32[]{:S(2)}, u32[]{:S(2)}) collective-permute-start(bf16[64,1024]{1,0:T(8,128)(2,1)S(1)} %add_convert_fusion), channel_id=1, source_target_pairs={{8,12},{10,14},{9,13},{11,15},{24,28},{26,30},{25,29},{27,31}} | collective-permute-start | bytes 393224 | tf_op jit(solution)/shard_map/ppermute | solution.py:350
  66.1 0.5 collective-permute-done.14
  66.7 1.3 %collective-permute-start.15 = (bf16[64,1024]{1,0:T(8,128)(2,1)S(1)}, bf16[64,1024]{1,0:T(8,128)(2,1)S(1)}, u32[]{:S(2)}, u32[]{:S(2)}) collective-permute-start(bf16[64,1024]{1,0:T(8,128)(2,1)S(1)} %add_convert_fusion.2), channel_id=1, source_target_pairs={{8,12},{10,14},{9,13},{11,15},{24,28},{26,30},{25,29},{27,31}} | collective-permute-start | bytes 393224 | tf_op jit(solution)/shard_map/ppermute | solution.py:350
  68.2 1.3 %collective-permute-start.10 = (bf16[64,1024]{1,0:T(8,128)(2,1)S(1)}, bf16[64,1024]{1,0:T(8,128)(2,1)S(1)}, u32[]{:S(2)}, u32[]{:S(2)}) collective-permute-start(bf16[64,1024]{1,0:T(8,128)(2,1)S(1)} %add_convert_fusion.4), channel_id=1, source_target_pairs={{8,12},{10,14},{9,13},{11,15},{24,28},{26,30},{25,29},{27,31}} | collective-permute-start | bytes 393224 | tf_op jit(solution)/shard_map/ppermute | solution.py:350
  69.6 1.5 %collective-permute-start.5 = (bf16[64,1024]{1,0:T(8,128)(2,1)S(1)}, bf16[64,1024]{1,0:T(8,128)(2,1)S(1)}, u32[]{:S(2)}, u32[]{:S(2)}) collective-permute-start(bf16[64,1024]{1,0:T(8,128)(2,1)S(1)} %add_convert_fusion.6), channel_id=1, source_target_pairs={{8,12},{10,14},{9,13},{11,15},{24,28},{26,30},{25,29},{27,31}} | collective-permute-start | bytes 393224 | tf_op jit(solution)/shard_map/ppermute | solution.py:350
  71.5 2.0 %collective-permute-start.16 = (bf16[64,1024]{1,0:T(8,128)(2,1)S(1)}, bf16[64,1024]{1,0:T(8,128)(2,1)S(1)}, u32[]{:S(2)}, u32[]{:S(2)}) collective-permute-start(bf16[64,1024]{1,0:T(8,128)(2,1)S(1)} %get-tuple-element.63), channel_id=1, source_target_pairs={{0,2},{2,0},{4,6},{6,4},{8,10},{10,8},{12,14},{14,12},{1,3},{3,1},... | collective-permute-start | bytes 393224 | tf_op jit(solution)/shard_map/ppermute | solution.py:354
  74.3 1.6 %collective-permute-start.6 = (bf16[64,1024]{1,0:T(8,128)(2,1)S(1)}, bf16[64,1024]{1,0:T(8,128)(2,1)S(1)}, u32[]{:S(2)}, u32[]{:S(2)}) collective-permute-start(bf16[64,1024]{1,0:T(8,128)(2,1)S(1)} %get-tuple-element.75), channel_id=1, source_target_pairs={{0,2},{2,0},{4,6},{6,4},{8,10},{10,8},{12,14},{14,12},{1,3},{3,1},... | collective-permute-start | bytes 393224 | tf_op jit(solution)/shard_map/ppermute | solution.py:354
  75.9 1.5 %collective-permute-done.21 = bf16[64,1024]{1,0:T(8,128)(2,1)S(1)} collective-permute-done((bf16[64,1024]{1,0:T(8,128)(2,1)S(1)}, bf16[64,1024]{1,0:T(8,128)(2,1)S(1)}, u32[]{:S(2)}, u32[]{:S(2)}) %collective-permute-start.21) | collective-permute-done | bytes 131104 | tf_op jit(solution)/shard_map/ppermute | solution.py:354
  77.4 1.4 %collective-permute-done.16 = bf16[64,1024]{1,0:T(8,128)(2,1)S(1)} collective-permute-done((bf16[64,1024]{1,0:T(8,128)(2,1)S(1)}, bf16[64,1024]{1,0:T(8,128)(2,1)S(1)}, u32[]{:S(2)}, u32[]{:S(2)}) %collective-permute-start.16) | collective-permute-done | bytes 131104 | tf_op jit(solution)/shard_map/ppermute | solution.py:354
  78.8 1.3 %collective-permute-done.11 = bf16[64,1024]{1,0:T(8,128)(2,1)S(1)} collective-permute-done((bf16[64,1024]{1,0:T(8,128)(2,1)S(1)}, bf16[64,1024]{1,0:T(8,128)(2,1)S(1)}, u32[]{:S(2)}, u32[]{:S(2)}) %collective-permute-start.11) | collective-permute-done | bytes 131104 | tf_op jit(solution)/shard_map/ppermute | solution.py:354
  80.2 1.3 %collective-permute-done.6 = bf16[64,1024]{1,0:T(8,128)(2,1)S(1)} collective-permute-done((bf16[64,1024]{1,0:T(8,128)(2,1)S(1)}, bf16[64,1024]{1,0:T(8,128)(2,1)S(1)}, u32[]{:S(2)}, u32[]{:S(2)}) %collective-permute-start.6) | collective-permute-done | bytes 131104 | tf_op jit(solution)/shard_map/ppermute | solution.py:354
  81.6 2.2 %shard_map.109.rest_0_ = bf16[512,4096]{1,0:T(8,128)(2,1)} custom-call(bf16[512,1024]{1,0:T(8,128)(2,1)S(1)} %get-tuple-element.54.p_ref, bf16[512,1024]{1,0:T(8,128)(2,1)S(1)} %get-tuple-element.55.g_ref, bf16[128,1024]{1,0:T(8,128)(2,1)S(1)} %pad_maximum_fusion.3.e_ref, bf16[512,256]{1,0:T(8,128)(2,1)S(1)} %copy-done.2, f32[1,4096]{1,0:T(1,128)S(1)} %bitcast.15), custom_call_target="tpu_custom_call" | custom-call | flops 536870912 | bytes 3145728 | tf_op jit(solution)/shard_map/pallas_call | solution.py:325
  83.8 2.2 %shard_map.110.rest_0_ = bf16[512,4096]{1,0:T(8,128)(2,1)} custom-call(bf16[512,1024]{1,0:T(8,128)(2,1)S(1)} %get-tuple-element.49.p_ref, bf16[512,1024]{1,0:T(8,128)(2,1)S(1)} %get-tuple-element.50.g_ref, bf16[128,1024]{1,0:T(8,128)(2,1)S(1)} %pad_maximum_fusion.2.e_ref, bf16[512,256]{1,0:T(8,128)(2,1)S(1)} %copy-done.2, ...), custom_call_target="tpu_custom_call", output_to_operand_aliasing={{}: (5, {})} | custom-call | flops 536870912 | bytes 3145728 | tf_op jit(solution)/shard_map/pallas_call | solution.py:325
  86.0 2.2 %shard_map.111.rest_0_ = bf16[512,4096]{1,0:T(8,128)(2,1)} custom-call(bf16[512,1024]{1,0:T(8,128)(2,1)S(1)} %get-tuple-element.44.p_ref, bf16[512,1024]{1,0:T(8,128)(2,1)S(1)} %get-tuple-element.45.g_ref, bf16[128,1024]{1,0:T(8,128)(2,1)S(1)} %pad_maximum_fusion.1.e_ref, bf16[512,256]{1,0:T(8,128)(2,1)S(1)} %copy-done.2, ...), custom_call_target="tpu_custom_call", output_to_operand_aliasing={{}: (5, {})} | custom-call | flops 536870912 | bytes 3145728 | tf_op jit(solution)/shard_map/pallas_call | solution.py:325
  88.2 2.2 %shard_map.112 = bf16[512,4096]{1,0:T(8,128)(2,1)} custom-call(bf16[512,1024]{1,0:T(8,128)(2,1)S(1)} %get-tuple-element.39.p_ref, bf16[512,1024]{1,0:T(8,128)(2,1)S(1)} %get-tuple-element.40.g_ref, bf16[128,1024]{1,0:T(8,128)(2,1)S(1)} %pad_maximum_fusion.e_ref, bf16[512,256]{1,0:T(8,128)(2,1)S(1)} %copy-done.2, ...), custom_call_target="tpu_custom_call", output_to_operand_aliasing={{}: (5, {})} | custom-call | flops 536870912 | bytes 3145728 | tf_op jit(solution)/shard_map/pallas_call | solution.py:325
  (75 shorter events, 2.8 us)
Async XLA Ops:
  1.9 0.9 %copy-start.1 = (bf16[512,256]{1,0:T(8,128)(2,1)S(1)}, bf16[512,256]{1,0:T(8,128)(2,1)}, u32[]{:S(2)}) copy-start(bf16[512,256]{1,0:T(8,128)(2,1)} %c_ref.17) | copy-start | bytes 786436
  2.8 0.9 %copy-start.7 = (bf16[512,256]{1,0:T(8,128)(2,1)S(1)}, bf16[512,256]{1,0:T(8,128)(2,1)}, u32[]{:S(2)}) copy-start(bf16[512,256]{1,0:T(8,128)(2,1)} %b_ref.1) | copy-start | bytes 786436
  5.1 0.8 copy-start.8
  5.9 0.8 copy-start.10
  6.7 5.6 %collective-permute-start.1 = (f32[1,4096]{1,0:T(1,128)S(1)}, f32[1,4096]{1,0:T(1,128)S(1)}, u32[]{:S(2)}, u32[]{:S(2)}) collective-permute-start(f32[1,4096]{1,0:T(1,128)S(1)} %slice.67), channel_id=1, source_target_pairs={{0,2},{2,0},{4,6},{6,4},{8,10},{10,8},{12,14},{14,12},{1,3},{3,1},... | collective-permute-start | bytes 49160 | tf_op jit(solution)/shard_map/ppermute | solution.py:236
  9.2 7.0 %collective-permute-start = (bf16[8,4096]{1,0:T(8,128)(2,1)S(1)}, bf16[8,4096]{1,0:T(8,128)(2,1)S(1)}, u32[]{:S(2)}, u32[]{:S(2)}) collective-permute-start(bf16[8,4096]{1,0:T(8,128)(2,1)S(1)} %slice.66), channel_id=1, source_target_pairs={{0,2},{2,4},{4,6},{6,8},{8,10},{10,12},{12,14},{1,3},{3,5},{5,7},{... | collective-permute-start | bytes 196616 | tf_op jit(solution)/shard_map/ppermute | solution.py:215
  16.2 2.2 %copy-start = (bf16[512,4096]{1,0:T(8,128)(2,1)S(1)}, bf16[512,4096]{1,0:T(8,128)(2,1)}, u32[]{:S(2)}) copy-start(bf16[512,4096]{1,0:T(8,128)(2,1)} %x_ref.7) | copy-start | bytes 12582916
  18.4 0.8 copy-start.3
  22.9 27.8 %collective-permute-start.17 = (bf16[64,1024]{1,0:T(8,128)(2,1)S(1)}, bf16[64,1024]{1,0:T(8,128)(2,1)S(1)}, u32[]{:S(2)}, u32[]{:S(2)}) collective-permute-start(bf16[64,1024]{1,0:T(8,128)(2,1)S(1)} %broadcast_select_fusion.7), channel_id=1, source_target_pairs={{0,2},{2,0},{4,6},{6,4},{8,10},{10,8},{12,14},{14,12},{1,3},{3,1},... | collective-permute-start | bytes 393224 | tf_op jit(solution)/shard_map/ppermute | solution.py:342
  26.8 24.8 %collective-permute-start.12 = (bf16[64,1024]{1,0:T(8,128)(2,1)S(1)}, bf16[64,1024]{1,0:T(8,128)(2,1)S(1)}, u32[]{:S(2)}, u32[]{:S(2)}) collective-permute-start(bf16[64,1024]{1,0:T(8,128)(2,1)S(1)} %broadcast_select_fusion.15), channel_id=1, source_target_pairs={{0,2},{2,0},{4,6},{6,4},{8,10},{10,8},{12,14},{14,12},{1,3},{3,1},... | collective-permute-start | bytes 393224 | tf_op jit(solution)/shard_map/ppermute | solution.py:342
  32.6 6.2 %copy-start.2 = (bf16[512,256]{1,0:T(8,128)(2,1)S(1)}, bf16[512,256]{1,0:T(8,128)(2,1)}, u32[]{:S(2)}) copy-start(bf16[512,256]{1,0:T(8,128)(2,1)} %c_ref.17) | copy-start | bytes 786436
  32.6 6.2 %copy-start.5 = (f32[64]{0:T(128)S(1)}, f32[64]{0:T(128)}, u32[]{:S(2)}) copy-start(f32[64]{0:T(128)} %rate_ref.7) | copy-start | bytes 772
  32.6 6.2 %copy-start.6 = (bf16[512,4096]{1,0:T(8,128)(2,1)S(1)}, bf16[512,4096]{1,0:T(8,128)(2,1)}, u32[]{:S(2)}) copy-start(bf16[512,4096]{1,0:T(8,128)(2,1)} %z_ref.7) | copy-start | bytes 12582916
  32.6 6.2 %copy-start.9 = (bf16[512,512]{1,0:T(8,128)(2,1)S(1)}, bf16[512,512]{1,0:T(8,128)(2,1)}, u32[]{:S(2)}) copy-start(bf16[512,512]{1,0:T(8,128)(2,1)} %copy-done.8) | copy-start | bytes 1572868
  32.6 6.2 %copy-start.11 = (f32[2,512,128]{2,1,0:T(8,128)S(1)}, f32[2,512,128]{2,1,0:T(8,128)}, u32[]{:S(2)}) copy-start(f32[2,512,128]{2,1,0:T(8,128)} %copy-done.10) | copy-start | bytes 1572868
  32.7 19.7 %collective-permute-start.7 = (bf16[64,1024]{1,0:T(8,128)(2,1)S(1)}, bf16[64,1024]{1,0:T(8,128)(2,1)S(1)}, u32[]{:S(2)}, u32[]{:S(2)}) collective-permute-start(bf16[64,1024]{1,0:T(8,128)(2,1)S(1)} %broadcast_select_fusion.23), channel_id=1, source_target_pairs={{0,2},{2,0},{4,6},{6,4},{8,10},{10,8},{12,14},{14,12},{1,3},{3,1},... | collective-permute-start | bytes 393224 | tf_op jit(solution)/shard_map/ppermute | solution.py:342
  36.7 16.4 %collective-permute-start.2 = (bf16[64,1024]{1,0:T(8,128)(2,1)S(1)}, bf16[64,1024]{1,0:T(8,128)(2,1)S(1)}, u32[]{:S(2)}, u32[]{:S(2)}) collective-permute-start(bf16[64,1024]{1,0:T(8,128)(2,1)S(1)} %broadcast_select_fusion.31), channel_id=1, source_target_pairs={{0,2},{2,0},{4,6},{6,4},{8,10},{10,8},{12,14},{14,12},{1,3},{3,1},... | collective-permute-start | bytes 393224 | tf_op jit(solution)/shard_map/ppermute | solution.py:342
  50.9 3.1 %collective-permute-start.18 = (bf16[64,1024]{1,0:T(8,128)(2,1)S(1)}, bf16[64,1024]{1,0:T(8,128)(2,1)S(1)}, u32[]{:S(2)}, u32[]{:S(2)}) collective-permute-start(bf16[64,1024]{1,0:T(8,128)(2,1)S(1)} %get-tuple-element.60), channel_id=1, source_target_pairs={{0,4},{2,6},{1,5},{3,7},{16,20},{18,22},{17,21},{19,23}} | collective-permute-start | bytes 393224 | tf_op jit(solution)/shard_map/ppermute | solution.py:350
  51.6 3.7 %collective-permute-start.13 = (bf16[64,1024]{1,0:T(8,128)(2,1)S(1)}, bf16[64,1024]{1,0:T(8,128)(2,1)S(1)}, u32[]{:S(2)}, u32[]{:S(2)}) collective-permute-start(bf16[64,1024]{1,0:T(8,128)(2,1)S(1)} %get-tuple-element.66), channel_id=1, source_target_pairs={{0,4},{2,6},{1,5},{3,7},{16,20},{18,22},{17,21},{19,23}} | collective-permute-start | bytes 393224 | tf_op jit(solution)/shard_map/ppermute | solution.py:350
  52.4 4.3 %collective-permute-start.8 = (bf16[64,1024]{1,0:T(8,128)(2,1)S(1)}, bf16[64,1024]{1,0:T(8,128)(2,1)S(1)}, u32[]{:S(2)}, u32[]{:S(2)}) collective-permute-start(bf16[64,1024]{1,0:T(8,128)(2,1)S(1)} %get-tuple-element.72), channel_id=1, source_target_pairs={{0,4},{2,6},{1,5},{3,7},{16,20},{18,22},{17,21},{19,23}} | collective-permute-start | bytes 393224 | tf_op jit(solution)/shard_map/ppermute | solution.py:350
  53.2 4.9 %collective-permute-start.3 = (bf16[64,1024]{1,0:T(8,128)(2,1)S(1)}, bf16[64,1024]{1,0:T(8,128)(2,1)S(1)}, u32[]{:S(2)}, u32[]{:S(2)}) collective-permute-start(bf16[64,1024]{1,0:T(8,128)(2,1)S(1)} %get-tuple-element.78), channel_id=1, source_target_pairs={{0,4},{2,6},{1,5},{3,7},{16,20},{18,22},{17,21},{19,23}} | collective-permute-start | bytes 393224 | tf_op jit(solution)/shard_map/ppermute | solution.py:350
  54.0 10.7 %collective-permute-start.19 = (bf16[64,1024]{1,0:T(8,128)(2,1)S(1)}, bf16[64,1024]{1,0:T(8,128)(2,1)S(1)}, u32[]{:S(2)}, u32[]{:S(2)}) collective-permute-start(bf16[64,1024]{1,0:T(8,128)(2,1)S(1)} %fusion.15), channel_id=1, source_target_pairs={{4,8},{6,10},{5,9},{7,11},{20,24},{22,26},{21,25},{23,27}} | collective-permute-start | bytes 393224 | tf_op jit(solution)/shard_map/ppermute | solution.py:350
  55.4 11.3 %collective-permute-start.14 = (bf16[64,1024]{1,0:T(8,128)(2,1)S(1)}, bf16[64,1024]{1,0:T(8,128)(2,1)S(1)}, u32[]{:S(2)}, u32[]{:S(2)}) collective-permute-start(bf16[64,1024]{1,0:T(8,128)(2,1)S(1)} %fusion.11), channel_id=1, source_target_pairs={{4,8},{6,10},{5,9},{7,11},{20,24},{22,26},{21,25},{23,27}} | collective-permute-start | bytes 393224 | tf_op jit(solution)/shard_map/ppermute | solution.py:350
  56.8 11.3 %collective-permute-start.9 = (bf16[64,1024]{1,0:T(8,128)(2,1)S(1)}, bf16[64,1024]{1,0:T(8,128)(2,1)S(1)}, u32[]{:S(2)}, u32[]{:S(2)}) collective-permute-start(bf16[64,1024]{1,0:T(8,128)(2,1)S(1)} %fusion.7), channel_id=1, source_target_pairs={{4,8},{6,10},{5,9},{7,11},{20,24},{22,26},{21,25},{23,27}} | collective-permute-start | bytes 393224 | tf_op jit(solution)/shard_map/ppermute | solution.py:350
  58.2 11.3 %collective-permute-start.4 = (bf16[64,1024]{1,0:T(8,128)(2,1)S(1)}, bf16[64,1024]{1,0:T(8,128)(2,1)S(1)}, u32[]{:S(2)}, u32[]{:S(2)}) collective-permute-start(bf16[64,1024]{1,0:T(8,128)(2,1)S(1)} %fusion.3), channel_id=1, source_target_pairs={{4,8},{6,10},{5,9},{7,11},{20,24},{22,26},{21,25},{23,27}} | collective-permute-start | bytes 393224 | tf_op jit(solution)/shard_map/ppermute | solution.py:350
  64.8 6.3 %collective-permute-start.20 = (bf16[64,1024]{1,0:T(8,128)(2,1)S(1)}, bf16[64,1024]{1,0:T(8,128)(2,1)S(1)}, u32[]{:S(2)}, u32[]{:S(2)}) collective-permute-start(bf16[64,1024]{1,0:T(8,128)(2,1)S(1)} %add_convert_fusion), channel_id=1, source_target_pairs={{8,12},{10,14},{9,13},{11,15},{24,28},{26,30},{25,29},{27,31}} | collective-permute-start | bytes 393224 | tf_op jit(solution)/shard_map/ppermute | solution.py:350
  66.7 4.6 %collective-permute-start.15 = (bf16[64,1024]{1,0:T(8,128)(2,1)S(1)}, bf16[64,1024]{1,0:T(8,128)(2,1)S(1)}, u32[]{:S(2)}, u32[]{:S(2)}) collective-permute-start(bf16[64,1024]{1,0:T(8,128)(2,1)S(1)} %add_convert_fusion.2), channel_id=1, source_target_pairs={{8,12},{10,14},{9,13},{11,15},{24,28},{26,30},{25,29},{27,31}} | collective-permute-start | bytes 393224 | tf_op jit(solution)/shard_map/ppermute | solution.py:350
  68.2 5.3 %collective-permute-start.10 = (bf16[64,1024]{1,0:T(8,128)(2,1)S(1)}, bf16[64,1024]{1,0:T(8,128)(2,1)S(1)}, u32[]{:S(2)}, u32[]{:S(2)}) collective-permute-start(bf16[64,1024]{1,0:T(8,128)(2,1)S(1)} %add_convert_fusion.4), channel_id=1, source_target_pairs={{8,12},{10,14},{9,13},{11,15},{24,28},{26,30},{25,29},{27,31}} | collective-permute-start | bytes 393224 | tf_op jit(solution)/shard_map/ppermute | solution.py:350
  69.6 4.6 %collective-permute-start.5 = (bf16[64,1024]{1,0:T(8,128)(2,1)S(1)}, bf16[64,1024]{1,0:T(8,128)(2,1)S(1)}, u32[]{:S(2)}, u32[]{:S(2)}) collective-permute-start(bf16[64,1024]{1,0:T(8,128)(2,1)S(1)} %add_convert_fusion.6), channel_id=1, source_target_pairs={{8,12},{10,14},{9,13},{11,15},{24,28},{26,30},{25,29},{27,31}} | collective-permute-start | bytes 393224 | tf_op jit(solution)/shard_map/ppermute | solution.py:350
  71.1 10.5 %copy-start.4 = (f32[4096]{0:T(1024)S(1)}, f32[4096]{0:T(1024)}, u32[]{:S(2)}) copy-start(f32[4096]{0:T(1024)} %param.19) | copy-start | bytes 49156
  71.2 6.1 %collective-permute-start.21 = (bf16[64,1024]{1,0:T(8,128)(2,1)S(1)}, bf16[64,1024]{1,0:T(8,128)(2,1)S(1)}, u32[]{:S(2)}, u32[]{:S(2)}) collective-permute-start(bf16[64,1024]{1,0:T(8,128)(2,1)S(1)} %get-tuple-element.57), channel_id=1, source_target_pairs={{0,2},{2,0},{4,6},{6,4},{8,10},{10,8},{12,14},{14,12},{1,3},{3,1},... | collective-permute-start | bytes 393224 | tf_op jit(solution)/shard_map/ppermute | solution.py:354
  71.5 7.2 %collective-permute-start.16 = (bf16[64,1024]{1,0:T(8,128)(2,1)S(1)}, bf16[64,1024]{1,0:T(8,128)(2,1)S(1)}, u32[]{:S(2)}, u32[]{:S(2)}) collective-permute-start(bf16[64,1024]{1,0:T(8,128)(2,1)S(1)} %get-tuple-element.63), channel_id=1, source_target_pairs={{0,2},{2,0},{4,6},{6,4},{8,10},{10,8},{12,14},{14,12},{1,3},{3,1},... | collective-permute-start | bytes 393224 | tf_op jit(solution)/shard_map/ppermute | solution.py:354
  73.6 6.5 %collective-permute-start.11 = (bf16[64,1024]{1,0:T(8,128)(2,1)S(1)}, bf16[64,1024]{1,0:T(8,128)(2,1)S(1)}, u32[]{:S(2)}, u32[]{:S(2)}) collective-permute-start(bf16[64,1024]{1,0:T(8,128)(2,1)S(1)} %get-tuple-element.69), channel_id=1, source_target_pairs={{0,2},{2,0},{4,6},{6,4},{8,10},{10,8},{12,14},{14,12},{1,3},{3,1},... | collective-permute-start | bytes 393224 | tf_op jit(solution)/shard_map/ppermute | solution.py:354
  74.3 7.2 %collective-permute-start.6 = (bf16[64,1024]{1,0:T(8,128)(2,1)S(1)}, bf16[64,1024]{1,0:T(8,128)(2,1)S(1)}, u32[]{:S(2)}, u32[]{:S(2)}) collective-permute-start(bf16[64,1024]{1,0:T(8,128)(2,1)S(1)} %get-tuple-element.75), channel_id=1, source_target_pairs={{0,2},{2,0},{4,6},{6,4},{8,10},{10,8},{12,14},{14,12},{1,3},{3,1},... | collective-permute-start | bytes 393224 | tf_op jit(solution)/shard_map/ppermute | solution.py:354

commit v2 on v0

v2 whole, which is shorter than its diff:
```python
import functools
import math

import jax
import jax.numpy as jnp
from jax import lax
from jax.experimental import pallas as pl
from jax.experimental.pallas import tpu as pltpu
from jax.sharding import PartitionSpec as P

NSTATE = 128
KERNEL = 4
BLOCK = 512
HEAD_DIM = 64
SUB = 128
NSUB = BLOCK // SUB
WIDTHS = (2048, 2048)
HEAD_SHIFT = 6
LANES = 512
ILANES = 512
FLANES = 1024
TILE = 256
IWIDTH = 1024
TAIL = 8

f32 = jnp.float32
bf16 = jnp.bfloat16
LOG2E = math.log2(math.e)
MIB = 1024 * 1024
PREP_LIMIT, STATE_LIMIT, INSIDE_LIMIT, FINAL_LIMIT = 16, 16, 16, 16
PREP_BYTES, STATE_BYTES, INSIDE_BYTES, FINAL_BYTES = 1, 1, 1, 1


def iota(shape, axis):
    return lax.broadcasted_iota(jnp.int32, shape, axis)


def dot(a, b):
    return jnp.dot(a, b, preferred_element_type=f32)


def silu_of_twice(values):
    return values + values * jnp.tanh(values)


def bits(size):
    return size.bit_length() - 1


def prep_kernel(
    codes_hbm, rate_hbm, bypass_hbm, b_hbm, w_hbm, bias_hbm,
    pieces_ref, spread_ref, bt_ref, rows_ref, taps_ref, decay_ref, odd_ref,
    codes_ref, rate_ref, bypass_ref, b_ref, w_ref, bias_ref, sems,
):
    pairs = (
        (codes_hbm, codes_ref), (rate_hbm, rate_ref), (bypass_hbm, bypass_ref), (b_hbm, b_ref),
        (w_hbm, w_ref), (bias_hbm, bias_ref),
    )
    copies = [pltpu.make_async_copy(a, b, sems.at[k]) for k, (a, b) in enumerate(pairs)]
    for copy in copies:
        copy.start()
    heads, tokens = codes_ref.shape
    width = rows_ref.shape[1]
    groups = b_ref.shape[1] // NSTATE
    per_group = heads // groups
    group_width = width // groups
    causal = iota((SUB, SUB), 0) >= iota((SUB, SUB), 1)
    lower = jnp.where(causal, 1.0, 0.0).astype(bf16)
    row = iota((4 * per_group, group_width), 0)
    part = row >> bits(per_group)
    hit = (row & (per_group - 1)) == (iota((4 * per_group, group_width), 1) >> HEAD_SHIFT)
    scale = jnp.where(part == 0, 65536.0, jnp.where(part == 1, 256.0, jnp.where(part == 2, 1.0, 0.0)))
    spread_ref[...] = jnp.where(hit, scale, 0.0).astype(bf16)
    odd = (lax.axis_index("ctx") & 1) == 1
    odd_ref[...] = jnp.where(odd, jnp.ones(odd_ref.shape, f32), 0.0)
    spread = jnp.where(iota((heads, width), 0) == (iota((heads, width), 1) >> HEAD_SHIFT), 1.0, 0.0)
    for copy in copies:
        copy.wait()
    codes = codes_ref[...].T
    split = jnp.concatenate([codes >> 8, codes & 255], axis=1).astype(f32).astype(bf16)
    sums = jnp.concatenate([dot(lower, split[s * SUB : (s + 1) * SUB]) for s in range(NSUB)], axis=0)
    whole = sums[:, :heads].astype(jnp.int32) * 256 + sums[:, heads:].astype(jnp.int32)
    columns = []
    for g in range(groups):
        mine = whole[:, g * per_group : (g + 1) * per_group]
        columns += [mine >> 16, (mine >> 8) & 255, mine & 255, jnp.zeros_like(mine)]
    pieces_ref[...] = jnp.concatenate(columns, axis=1).astype(f32).astype(bf16)
    for g in range(groups):
        cols = slice(g * NSTATE, (g + 1) * NSTATE)
        writes = b_ref[:, cols].astype(f32)
        bt_ref[cols, :] = jnp.where(odd, pltpu.roll(writes, NSTATE // 2, 1), writes).T.astype(bf16)
    totals = jnp.concatenate(
        [whole[(s + 1) * SUB - 1 : (s + 1) * SUB] for s in range(NSUB)], axis=0
    ).astype(f32)
    empty = jnp.zeros((2, heads), f32)
    small = jnp.concatenate([rate_ref[...], bypass_ref[...], totals, empty], axis=0)
    wide = jnp.dot(small, spread, precision=lax.Precision.HIGHEST, preferred_element_type=f32)
    rate = wide[0:1] * (-LOG2E / 1024.0)
    base = jnp.zeros_like(rate)
    rows_ref[0:1, :] = rate
    rows_ref[1:2, :] = wide[1:2]
    for s in range(NSUB):
        total = wide[2 + s : 3 + s]
        rows_ref[2 + s : 3 + s, :] = jnp.exp2(rate * total)
        rows_ref[8 + s : 9 + s, :] = jnp.exp2(rate * base)
        base = base + total
    decay_ref[...] = jnp.exp2(rate * base)
    rows_ref[6:8, :] = jnp.zeros((2, width), f32)
    rows_ref[12:16, :] = jnp.zeros((4, width), f32)
    taps_ref[0:KERNEL, :] = 0.5 * w_ref[...].astype(f32)
    bias = 0.5 * bias_ref[...].astype(f32)
    taps_ref[KERNEL : KERNEL + 1, :] = jnp.concatenate([bias[k : k + 1] for k in range(width // 128)], axis=1)
    taps_ref[KERNEL + 1 :, :] = jnp.zeros((7 - KERNEL, width), f32)


def mixing_kernel(pieces_ref, bt_ref, c_ref, left_ref, right_ref, scores_ref, ct_ref):
    groups = c_ref.shape[1] // NSTATE
    heads = pieces_ref.shape[1] // 4
    per_group = heads // groups
    row = iota((4 * heads, 16 * heads), 0)
    col = iota((4 * heads, 16 * heads), 1)
    kind = col & 15
    part = (row >> bits(per_group)) & 3
    row_head = ((row >> bits(4 * per_group)) << bits(per_group)) | (row & (per_group - 1))
    same = (row_head == (col >> 4)) & (part < 3)
    to_left = jnp.where(same & (part == kind), 1.0, 0.0).astype(bf16)
    scale = jnp.where(kind == 3, -65536.0, jnp.where(kind == 4, -256.0, -1.0))
    to_right = jnp.where(same & (part == kind - 3), scale, 0.0).astype(bf16)
    col_kind = iota((1, 16 * heads), 1) & 15
    ones = jnp.where((col_kind >= 3) & (col_kind < 6), 1.0, 0.0)
    fixed = jnp.where(col_kind == 0, 65536.0, jnp.where(col_kind == 1, 256.0, jnp.where(col_kind == 2, 1.0, 0.0)))
    pieces = pieces_ref[...]
    left_ref[...] = (dot(pieces, to_left) + ones).astype(bf16)
    right_ref[...] = (dot(pieces, to_right) + fixed).T.astype(bf16)
    odd = (lax.axis_index("ctx") & 1) == 1
    causal = iota((SUB, SUB), 0) >= iota((SUB, SUB), 1)
    for g in range(groups):
        cols = slice(g * NSTATE, (g + 1) * NSTATE)
        reads = c_ref[:, cols].astype(f32)
        reads = jnp.where(odd, pltpu.roll(reads, NSTATE // 2, 1), reads).astype(bf16)
        ct_ref[:, cols] = reads
        for s in range(NSUB):
            rows = slice(s * SUB, (s + 1) * SUB)
            scores_ref[g, rows, :] = jnp.where(causal, dot(reads[rows], bt_ref[cols, rows]), 0.0)


def state_kernel(decay_in, x_ref, tail_ref, taps_ref, pieces_ref, spread_ref, bt_ref, rows_ref, f_ref, local_ref, own_ref, given_ref, decay_ref):
    half = NSTATE // 2
    decay_ref[...] = decay_in[...]
    for t in range(LANES // TILE):
        cols = slice(t * TILE, (t + 1) * TILE)
        taps = taps_ref[:, cols]
        rate = rows_ref[0:1, cols]
        running = None
        for s in range(NSUB):
            rows = slice(s * SUB, (s + 1) * SUB)
            if s == 0:
                before = tail_ref[:, cols].astype(f32)
            else:
                before = x_ref[s * SUB - 16 : s * SUB, cols].astype(f32)[16 - TAIL :]
            current = x_ref[rows, cols].astype(f32)
            padded = jnp.concatenate([before, current], axis=0)
            summed = taps[KERNEL : KERNEL + 1] + taps[KERNEL - 1 : KERNEL] * current
            for back in range(1, KERNEL):
                moved = pltpu.roll(padded, back, 0)[TAIL:]
                summed = summed + taps[KERNEL - 1 - back : KERNEL - back] * moved
            filtered = silu_of_twice(summed).astype(bf16)
            f_ref[rows, cols] = filtered
            wide = dot(pieces_ref[rows, :], spread_ref[:, cols])
            weight = jnp.exp2(rate * (wide[SUB - 1 : SUB] - wide))
            weighted = (weight * filtered.astype(f32)).astype(bf16)
            part = dot(bt_ref[:, rows], weighted)
            running = part if s == 0 else rows_ref[2 + s : 3 + s, cols] * running + part
            if s < NSUB - 1:
                local_ref[s, :, cols] = running.astype(bf16)
        running = running.astype(bf16)
        own_ref[:, cols] = running[:half]
        given_ref[:, cols] = running[half:]


def inside_kernel(
    start, decay_in, z_ref, f_ref, local_ref, c_ref, pieces_ref, spread_ref, left_ref, right_ref, scores_ref, rows_ref,
    rate_ref, *refs,
):
    decay_ref, p_ref, g_ref, wall = refs[-4:]
    decay_ref[...] = decay_in[...]
    first_head = (start + pl.program_id(0) * ILANES) >> HEAD_SHIFT
    wall[...] = jnp.zeros_like(wall)
    first_lanes = iota((SUB, 128), 1) < HEAD_DIM
    for s in range(NSUB):
        rows = slice(s * SUB, (s + 1) * SUB)
        for q in range(ILANES // HEAD_DIM):
            wall[16 * q : 16 * q + 16, q * SUB : (q + 1) * SUB] = right_ref[16 * q : 16 * q + 16, rows]
        scores = scores_ref[0, rows, :]
        left = left_ref[rows, :]
        pieces = pieces_ref[rows, :]
        reads = c_ref[rows, :]
        for r in range(ILANES // TILE):
            cols = slice(r * TILE, (r + 1) * TILE)
            growth = jnp.exp2(rows_ref[0:1, cols] * dot(pieces, spread_ref[:, cols]))
            gate = silu_of_twice(0.5 * z_ref[rows, cols].astype(f32))
            g_ref[rows, cols] = (gate * growth * rows_ref[8 + s : 9 + s, cols]).astype(bf16)
            filtered = f_ref[rows, cols].astype(f32)
            total = rows_ref[1:2, cols] * filtered
            if s > 0:
                total = total + growth * dot(reads, local_ref[s - 1, :, cols])
            insides = []
            for q in range(2 * r, 2 * r + 2):
                spans = dot(left, wall[:, 2 * q * SUB : (2 * q + 2) * SUB])
                mixing = []
                for k in range(2):
                    scale = rate_ref[first_head + 2 * q + k] * (-LOG2E / 1024.0)
                    decays = jnp.exp2(jnp.maximum(spans[:, k * SUB : (k + 1) * SUB], 0.0) * scale)
                    mixing.append((decays * scores).astype(bf16))
                pair = filtered[:, 128 * (q - 2 * r) : 128 * (q - 2 * r) + 128]
                stacked = jnp.concatenate(
                    [jnp.where(first_lanes, pair, 0.0), jnp.where(first_lanes, 0.0, pair)], axis=0
                ).astype(bf16)
                insides.append(dot(jnp.concatenate(mixing, axis=1), stacked))
            p_ref[rows, cols] = ((total + jnp.concatenate(insides, axis=1)) * gate).astype(bf16)


def final_kernel(p_ref, g_ref, mine_ref, other_ref, c_ref, gain_ref, *rest):
    out_ref = rest[-1]
    same = (iota((TILE, TILE), 0) >> HEAD_SHIFT) == (iota((TILE, TILE), 1) >> HEAD_SHIFT)
    mean = jnp.where(same, 1.0 / HEAD_DIM, 0.0).astype(bf16)
    for t in range(out_ref.shape[1] // TILE):
        cols = slice(t * TILE, (t + 1) * TILE)
        entering = jnp.concatenate([mine_ref[:, cols], other_ref[:, cols]], axis=0)
        gain = gain_ref[:, cols]
        for s in range(NSUB):
            rows = slice(s * SUB, (s + 1) * SUB)
            carried = dot(c_ref[rows, :], entering)
            gated = p_ref[rows, cols].astype(f32) + carried * g_ref[rows, cols].astype(f32)
            meansq = dot((gated * gated).astype(bf16), mean)
            out_ref[rows, cols] = (gated * lax.rsqrt(meansq + 1e-05) * gain).astype(bf16)


def full(shape):
    return pl.BlockSpec(shape, lambda *i: (0,) * len(shape))


def call(kernel, operands, in_specs, after=(), limit=16, cost=1, **kwargs):
    count = len(operands)

    def ordered(*refs):
        kernel(*refs[:count], *refs[count + len(after) :])

    return pl.pallas_call(
        ordered,
        in_specs=list(in_specs) + [pl.BlockSpec(memory_space=pl.ANY)] * len(after),
        compiler_params=pltpu.CompilerParams(vmem_limit_bytes=limit * MIB),
        cost_estimate=pl.CostEstimate(flops=1, bytes_accessed=cost, transcendentals=0),
        **kwargs,
    )(*operands, *after)


def per_device(
    features,
    output_switch,
    input_proj,
    output_proj,
    step_codes,
    head_rate,
    conv_weight,
    conv_bias,
    bypass_factor,
    norm_gain,
):
    tokens, width = features.shape
    heads = head_rate.shape[0]
    groups = input_proj.shape[1] // NSTATE
    assert tokens == BLOCK and width == heads * HEAD_DIM
    runs = lax.axis_size("ctx")
    pairs = runs // 2
    swap = [(i, i ^ 1) for i in range(runs)]

    def shape(dims, dtype):
        return jax.ShapeDtypeStruct(dims, dtype)

    group_width = width // groups
    per_group = heads // groups
    half = NSTATE // 2
    assert sum(WIDTHS) == width
    hbm = pl.BlockSpec(memory_space=pltpu.HBM)

    last_rows = features[tokens - TAIL :]
    tail = lax.ppermute(last_rows, "ctx", [(i, i + 1) for i in range(runs - 1)])
    prepared = (
        ((tokens, 4 * heads), bf16),
        ((4 * per_group, group_width), bf16),
        ((groups * NSTATE, tokens), bf16),
        ((16, width), f32),
        ((8, width), f32),
        ((1, width), f32),
        ((1, width), f32),
    )
    pieces, spread, bt, rows, taps, decay, parity = call(
        prep_kernel,
        (
            step_codes.T, head_rate[None], bypass_factor[None], input_proj, conv_weight,
            conv_bias.reshape(width // 128, 128),
        ),
        [hbm] * 6,
        after=(last_rows,),
        limit=PREP_LIMIT,
        cost=PREP_BYTES,
        grid=(1,),
        out_specs=[full(dims) for dims, _ in prepared],
        out_shape=[shape(*kind) for kind in prepared],
        scratch_shapes=[
            pltpu.VMEM((heads, tokens), jnp.int32),
            pltpu.VMEM((1, heads), f32),
            pltpu.VMEM((1, heads), f32),
            pltpu.VMEM((tokens, groups * NSTATE), bf16),
            pltpu.VMEM((KERNEL, width), bf16),
            pltpu.VMEM((width // 128, 128), bf16),
            pltpu.SemaphoreType.DMA((6,)),
        ],
    )

    def mixing_parts(after):
        kinds = (
            ((tokens, 16 * heads), bf16),
            ((16 * heads, tokens), bf16),
            ((groups, tokens, SUB), f32),
            ((tokens, groups * NSTATE), bf16),
        )
        return call(
            mixing_kernel,
            (pieces, bt, output_proj),
            [full((tokens, 4 * heads)), full((groups * NSTATE, tokens)), full((tokens, groups * NSTATE))],
            after,
            grid=(1,),
            out_specs=[full(dims) for dims, _ in kinds],
            out_shape=[shape(*kind) for kind in kinds],
        )

    gain = norm_gain[None]

    def conv_states(start, lanes, decay, after):
        first = start // LANES
        column = lambda i: (0, first + i)
        group = lambda i: (first + i) * LANES // group_width
        mine = lambda i: (0, i)
        return call(
            state_kernel,
            (decay, features, tail, taps, pieces, spread, bt, rows),
            [
                full((1, width)),
                pl.BlockSpec((tokens, LANES), column),
                pl.BlockSpec((TAIL, LANES), column),
                pl.BlockSpec((8, LANES), column),
                pl.BlockSpec((tokens, 4 * per_group), lambda i: (0, group(i))),
                pl.BlockSpec((4 * per_group, LANES), lambda i: (0, (first + i) % (group_width // LANES))),
                pl.BlockSpec((NSTATE, tokens), lambda i: (group(i), 0)),
                pl.BlockSpec((16, LANES), column),
            ],
            after,
            limit=STATE_LIMIT,
            cost=STATE_BYTES,
            grid=(lanes // LANES,),
            out_specs=[
                pl.BlockSpec((tokens, LANES), mine),
                pl.BlockSpec((NSUB - 1, NSTATE, LANES), lambda i: (0, 0, i)),
                pl.BlockSpec((half, LANES), mine),
                pl.BlockSpec((half, LANES), mine),
                full((1, width)),
            ],
            out_shape=(
                shape((tokens, lanes), bf16),
                shape((NSUB - 1, NSTATE, lanes), bf16),
                shape((half, lanes), bf16),
                shape((half, lanes), bf16),
                shape((1, width), f32),
            ),
        )

    def inside(start, lanes, inner, whole, filtered, local, filled, decay, after):
        first = start // ILANES
        skip = inner // ILANES
        heads_here = ILANES // HEAD_DIM
        column = lambda i: (0, first + i)
        group = lambda i: (first + i) * ILANES // group_width
        mine = lambda i: (0, skip + i)
        return call(
            functools.partial(inside_kernel, start),
            (decay, output_switch, filtered, local, reads, pieces, spread, left, right, scores, rows, head_rate, *filled),
            [
                full((1, width)),
                pl.BlockSpec((tokens, ILANES), column),
                pl.BlockSpec((tokens, ILANES), mine),
                pl.BlockSpec((NSUB - 1, NSTATE, ILANES), lambda i: (0, 0, skip + i)),
                pl.BlockSpec((tokens, NSTATE), lambda i: (0, group(i))),
                pl.BlockSpec((tokens, 4 * per_group), lambda i: (0, group(i))),
                pl.BlockSpec((4 * per_group, ILANES), lambda i: (0, (first + i) % (group_width // ILANES))),
                pl.BlockSpec((tokens, 16 * heads_here), column),
                pl.BlockSpec((16 * heads_here, tokens), lambda i: (first + i, 0)),
                pl.BlockSpec((1, tokens, SUB), lambda i: (group(i), 0, 0)),
                pl.BlockSpec((16, ILANES), column),
                pl.BlockSpec(memory_space=pltpu.SMEM),
            ]
            + [pl.BlockSpec(memory_space=pl.ANY)] * len(filled),
            after,
            limit=INSIDE_LIMIT,
            cost=INSIDE_BYTES,
            grid=(lanes // ILANES,),
            out_specs=[full((1, width))] + [pl.BlockSpec((tokens, ILANES), mine)] * 2,
            out_shape=(shape((1, width), f32), shape((tokens, whole), bf16), shape((tokens, whole), bf16)),
            input_output_aliases={12: 1, 13: 2} if filled else {},
            scratch_shapes=[pltpu.VMEM((16 * heads_here, heads_here * SUB), bf16)],
        )

    def final(start, lanes, inner, out, kept, growth, own, other, after):
        block = FLANES if start % FLANES == 0 and lanes % FLANES == 0 else LANES
        first = start // block
        skip = inner // block
        column = lambda i: (0, first + i)
        mine = lambda i: (0, i)
        operands = [kept, growth, own, other, reads, gain]
        in_specs = [
            pl.BlockSpec((tokens, block), mine),
            pl.BlockSpec((tokens, block), mine),
            pl.BlockSpec((half, block), lambda i: (0, skip + i)),
            pl.BlockSpec((half, block), lambda i: (0, skip + i)),
            pl.BlockSpec((tokens, NSTATE), lambda i: (0, (first + i) * block // group_width)),
            pl.BlockSpec((1, block), column),
        ]
        aliases = {}
        if out is not None:
            aliases = {len(operands): 0}
            operands.append(out)
            in_specs.append(pl.BlockSpec(memory_space=pl.ANY))
        return call(
            final_kernel,
            operands,
            in_specs,
            after,
            limit=FINAL_LIMIT,
            cost=FINAL_BYTES,
            grid=(lanes // block,),
            out_specs=pl.BlockSpec((tokens, block), column),
            out_shape=shape((tokens, width), bf16),
            input_output_aliases=aliases,
        )

    def carry(c, own, given):
        cols = slice(starts[c], starts[c] + WIDTHS[c])
        got = lax.ppermute(given, "ctx", swap)
        yield given

        odd = parity[:, cols] > 0.5

        def coefficients():
            mine, theirs = now["decay"][:, cols], now["other"][:, cols]
            return jnp.where(odd, theirs, mine), jnp.where(odd, mine, theirs)

        own, got = own.astype(f32), got.astype(f32)
        before, behind = jnp.where(odd, got, own), jnp.where(odd, own, got)
        entering = None
        for step in range(pairs - 1):
            even, later = coefficients()
            sent = before if entering is None else even * entering + before
            sent = (later * sent + behind).astype(bf16)
            route = [(2 * step + k, 2 * step + 2 + k) for k in range(2)]
            arrived = lax.ppermute(sent, "ctx", route).astype(f32)
            yield sent
            entering = arrived if entering is None else entering + arrived
        even, later = coefficients()
        between = before if entering is None else even * entering + before
        entering = jnp.zeros_like(between) if entering is None else entering
        mine = jnp.where(odd, between, entering).astype(bf16)
        given = jnp.where(odd, entering, between).astype(bf16)
        other = lax.ppermute(given, "ctx", swap)
        yield given
        yield mine, other

    starts = [sum(WIDTHS[:c]) for c in range(len(WIDTHS))]
    now = {"decay": decay}
    travel, entering, remaining = [], {}, []

    def advance():
        waited = []
        for c, steps in enumerate(travel):
            if remaining[c]:
                value = next(steps)
                remaining[c] -= 1
                if remaining[c]:
                    waited.append(value)
                else:
                    entering[c] = value
        return tuple(waited)

    def splits(lanes):
        return [(k, min(IWIDTH, lanes - k)) for k in range(0, lanes, IWIDTH)]

    made, token = [], ()
    for c, lanes in enumerate(WIDTHS):
        made.append(conv_states(starts[c], lanes, now["decay"], token))
        now["decay"] = made[c][4]
        if c == 0:
            now["other"] = lax.ppermute(now["decay"], "ctx", swap)
        travel.append(carry(c, made[c][2], made[c][3]))
        remaining.append(pairs + 2)
        token = advance()
    left, right, scores, reads = mixing_parts(token)
    token = token[:-1] + (reads,)
    kept = []
    for c, lanes in enumerate(WIDTHS):
        filled = ()
        for inner, size in splits(lanes):
            now["decay"], *filled = inside(
                starts[c] + inner, size, inner, lanes, made[c][0], made[c][1], filled, now["decay"], token
            )
            token = advance()
        kept.append(filled)
    out = None
    for c, lanes in enumerate(WIDTHS):
        while c not in entering:
            token = advance()
        out = final(starts[c], lanes, 0, out, *kept[c], *entering[c], token)
        token = advance()
    return out


def solution(mesh):
    placed = (
        P(("groups", "ctx"), "head"),
        P(("groups", "ctx"), "head"),
        P(("groups", "ctx"), "head"),
        P(("groups", "ctx"), "head"),
        P(("groups", "ctx"), "head"),
        P("head"),
        P(None, "head"),
        P("head"),
        P("head"),
        P("head"),
    )
    return jax.shard_map(
        per_device,
        mesh=mesh,
        in_specs=placed,
        out_specs=P(("groups", "ctx"), "head"),
        check_vma=False,
    )
```

time: 242 us -> 66.9 us (0.28)
  the two profiles are of different devices: /device:TPU:0 before, /device:TPU:16 now
where the time goes in v2:
time: 66.9 us; the launch traced here: 66.4 us
  Pallas kernels  34.6 us (52%)
  starting transfers between devices  16 us (24%)
  local copies, waits for them, and re-layouts  7.66 us (11%)
  waiting for transfers between devices  6.12 us (9%)
  other arithmetic  1.69 us (3%)
    pallas_call x10, Pallas kernels, call(): pl.pallas_call(ordered, in_specs=list(in_specs) + [pl.BlockSpec(memory_sp...  34.6 us
    unnamed x24, local copies, waits for them, and re-layouts  6.82 us
    ppermute x6, starting transfers between devices, carry(): arrived = lax.ppermute(sent, 'ctx', route).astype(f32)  6.73 us
    ppermute x1, starting transfers between devices, per_device(): tail = lax.ppermute(last_rows, 'ctx', [(i, i + 1) for i in range(runs - 1)])  3.42 us
    ppermute x6, waiting for transfers between devices, carry(): arrived = lax.ppermute(sent, 'ctx', route).astype(f32)  3.1 us
    ppermute x2, waiting for transfers between devices, carry(): other = lax.ppermute(given, 'ctx', swap)  2.8 us
    ppermute x2, starting transfers between devices, carry(): got = lax.ppermute(given, 'ctx', swap)  2.16 us
    ppermute x2, starting transfers between devices, carry(): other = lax.ppermute(given, 'ctx', swap)  2.15 us
  transfers between devices with their start and end apart: 12, of which 5 were waited for; matrix products, arithmetic and copies ran while one was open for 3% of the time, Pallas kernels for 39%

profile of v2, /device:TPU:16, one launch (start us, length us, event | category | flops | bytes accessed | tf_op | source)
XLA Modules:
  0.0 66.4 jit_solution(7352366503887563149)
XLA Ops:
  0.0 0.8 %slice.45.refs_6_ = bf16[8,4096]{1,0:T(8,128)(2,1)S(1)} slice(bf16[512,4096]{1,0:T(8,128)(2,1)} %refs_1_.7), slice={[504:512], [0:4096]} | slice | bytes 131072 | tf_op jit(solution)/shard_map/slice | solution.py:287
  0.8 3.4 %collective-permute-start = (bf16[8,4096]{1,0:T(8,128)(2,1)S(1)}, bf16[8,4096]{1,0:T(8,128)(2,1)S(1)}, u32[]{:S(2)}, u32[]{:S(2)}) collective-permute-start(bf16[8,4096]{1,0:T(8,128)(2,1)S(1)} %slice.45.refs_6_), channel_id=1, source_target_pairs={{0,2},{2,4},{4,6},{6,8},{8,10},{10,12},{12,14},{1,3},{3,5},{5,7},{... | collective-permute-start | bytes 196616 | tf_op jit(solution)/shard_map/ppermute | solution.py:288
  4.3 0.0 copy-start.4
  4.3 0.9 %copy-done.4 = bf16[512,256]{1,0:T(8,128)(2,1)S(1)} copy-done((bf16[512,256]{1,0:T(8,128)(2,1)S(1)}, bf16[512,256]{1,0:T(8,128)(2,1)}, u32[]{:S(2)}) %copy-start.4) | copy-done | bytes 262168
  5.2 0.9 %copy-done.5 = s32[512,64]{0,1:T(8,128)S(1)} copy-done((s32[512,64]{0,1:T(8,128)S(1)}, s32[512,64]{0,1:T(8,128)}, u32[]{:S(2)}) %copy-start.5) | copy-done | bytes 131096
  6.1 0.8 %copy-done.7 = bf16[4,4096]{1,0:T(4,128)(2,1)S(1)} copy-done((bf16[4,4096]{1,0:T(4,128)(2,1)S(1)}, bf16[4,4096]{1,0:T(4,128)(2,1)}, u32[]{:S(2)}) %copy-start.7) | copy-done | bytes 32792
  6.9 0.7 copy-done.8
  7.5 0.7 %copy-done.10 = bf16[4096]{0:T(1024)(128)(2,1)S(1)} copy-done((bf16[4096]{0:T(1024)(128)(2,1)S(1)}, bf16[4096]{0:T(1024)(128)(2,1)}, u32[]{:S(2)}) %copy-start.10) | copy-done | bytes 8216
  8.2 0.7 copy-done.11
  8.9 1.8 %shard_map.100 = (bf16[512,256]{1,0:T(8,128)(2,1)S(1)}, bf16[128,2048]{1,0:T(8,128)(2,1)S(1)}, bf16[256,512]{1,0:T(8,128)(2,1)S(1)}, f32[16,4096]{1,0:T(8,128)S(...) custom-call(s32[64,512]{1,0:T(8,128)S(1)} %bitcast.17, f32[1,64]{1,0:T(1,128)S(1)} %bitcast.20, ...), custom_call_target="tpu_custom_call" | custom-call | flops 1 | bytes 1 | tf_op jit(solution)/shard_map/pallas_call | solution.py:249
  10.8 0.0 copy-start.1
  10.8 2.2 %copy-done.1 = bf16[512,4096]{1,0:T(8,128)(2,1)S(1)} copy-done((bf16[512,4096]{1,0:T(8,128)(2,1)S(1)}, bf16[512,4096]{1,0:T(8,128)(2,1)}, u32[]{:S(2)}) %copy-start.1) | copy-done | bytes 4194328
  12.9 5.5 %shard_map.101 = (bf16[512,2048]{1,0:T(8,128)(2,1)S(1)}, bf16[3,128,2048]{2,1,0:T(8,128)(2,1)S(1)}, bf16[64,2048]{1,0:T(8,128)(2,1)S(1)}, bf16[64,2048]{1,0:T(8,128)(2,1)S(1)}, f32[1,4096]{1,0:T(1,128)S(1)}) custom-call(f32[1,4096]{1,0:T(1,128)S(1)} %get-tuple-element.38.refs_0_, bf16[512,4096]{1,0:T(8,128)(2,1)S(1)} %copy-done.1, ...), custom_call_target="tpu_custom_call" | custom-call | flops 1 | bytes 1 | tf_op jit(solution)/shard_map/pallas_call | solution.py:249
  18.4 1.6 %collective-permute-start.1 = (f32[1,4096]{1,0:T(1,128)S(1)}, f32[1,4096]{1,0:T(1,128)S(1)}, u32[]{:S(2)}, u32[]{:S(2)}) collective-permute-start(f32[1,4096]{1,0:T(1,128)S(1)} %get-tuple-element.44.refs_0_), channel_id=1, source_target_pairs={{0,2},{2,0},{4,6},{6,4},{8,10},{10,8},{12,14},{14,12},{1,3},{3,1},... | collective-permute-start | bytes 49160 | tf_op jit(solution)/shard_map/ppermute | solution.py:502
  20.0 0.1 fusion.9
  20.1 0.6 collective-permute-start.2
  20.7 5.5 %shard_map.102 = (bf16[512,2048]{1,0:T(8,128)(2,1)S(1)}, bf16[3,128,2048]{2,1,0:T(8,128)(2,1)S(1)}, bf16[64,2048]{1,0:T(8,128)(2,1)S(1)}, bf16[64,2048]{1,0:T(8,128)(2,1)S(1)}, f32[1,4096]{1,0:T(1,128)S(1)}) custom-call(f32[1,4096]{1,0:T(1,128)S(1)} %get-tuple-element.44.refs_0_, bf16[512,4096]{1,0:T(8,128)(2,1)S(1)} %copy-done.2, ...), custom_call_target="tpu_custom_call" | custom-call | flops 1 | bytes 1 | tf_op jit(solution)/shard_map/pallas_call | solution.py:249
  26.2 0.0 copy-start.9
  26.2 1.6 %collective-permute-start.4 = (bf16[64,2048]{1,0:T(8,128)(2,1)S(1)}, bf16[64,2048]{1,0:T(8,128)(2,1)S(1)}, u32[]{:S(2)}, u32[]{:S(2)}) collective-permute-start(bf16[64,2048]{1,0:T(8,128)(2,1)S(1)} %get-tuple-element.51.refs_4_), channel_id=1, source_target_pairs={{0,2},{2,0},{4,6},{6,4},{8,10},{10,8},{12,14},{14,12},{1,3},{3,1},... | collective-permute-start | bytes 786440 | tf_op jit(solution)/shard_map/ppermute | solution.py:449
  27.8 0.0 collective-permute-done.2
  27.8 0.1 add_convert_fusion.3.refs_3_.refs_12_
  27.9 0.7 %collective-permute-start.3 = (bf16[64,2048]{1,0:T(8,128)(2,1)S(1)}, bf16[64,2048]{1,0:T(8,128)(2,1)S(1)}, u32[]{:S(2)}, u32[]{:S(2)}) collective-permute-start(bf16[64,2048]{1,0:T(8,128)(2,1)S(1)} %add_convert_fusion.3.refs_3_.refs_12_), channel_id=1, source_target_pairs={{0,4},{2,6},{1,5},{3,7},{16,20},{18,22},{17,21},{19,23}} | collective-permute-start | bytes 786440 | tf_op jit(solution)/shard_map/ppermute | solution.py:466
  28.6 1.0 %shard_map.103 = (bf16[512,1024]{1,0:T(8,128)(2,1)S(1)}, bf16[1024,512]{1,0:T(8,128)(2,1)S(1)}, f32[2,512,128]{2,1,0:T(8,128)S(1)}, bf16[512,256]{1,0:T(8,128)(2,1)S(1)}) custom-call(bf16[512,256]{1,0:T(8,128)(2,1)S(1)} %get-tuple-element.40.refs_4_.refs_0_.refs_5_, bf16[256,512]{1,0:T(8,128)(2,1)S(1)} %get-tuple-element.42.refs_6_.refs_1_, ...), custom_call_target="tpu_custom_call" | custom-call | flops 1 | bytes 1 | tf_op jit(solution)/shard_map/pallas_call | solution.py:249
  29.6 3.6 %shard_map.104 = (f32[1,4096]{1,0:T(1,128)S(1)}, bf16[512,2048]{1,0:T(8,128)(2,1)S(1)}, bf16[512,2048]{1,0:T(8,128)(2,1)S(1)}) custom-call(f32[1,4096]{1,0:T(1,128)S(1)} %get-tuple-element.46.refs_0_, bf16[512,4096]{1,0:T(8,128)(2,1)S(1)} %copy-done, bf16[512,2048]{1,0:T(8,128)(2,1)S(1)} %get-tuple-element.47.refs_2_, ...), custom_call_target="tpu_custom_call" | custom-call | flops 1 | bytes 1 | tf_op jit(solution)/shard_map/pallas_call | solution.py:249
  33.2 0.2 collective-permute-done.4
  33.4 0.1 add_convert_fusion.2.refs_15_
  33.6 0.7 %collective-permute-start.6 = (bf16[64,2048]{1,0:T(8,128)(2,1)S(1)}, bf16[64,2048]{1,0:T(8,128)(2,1)S(1)}, u32[]{:S(2)}, u32[]{:S(2)}) collective-permute-start(bf16[64,2048]{1,0:T(8,128)(2,1)S(1)} %add_convert_fusion.2.refs_15_), channel_id=1, source_target_pairs={{0,4},{2,6},{1,5},{3,7},{16,20},{18,22},{17,21},{19,23}} | collective-permute-start | bytes 786440 | tf_op jit(solution)/shard_map/ppermute | solution.py:466
  34.3 0.2 fusion.3.refs_14_
  34.4 1.3 %collective-permute-start.5 = (bf16[64,2048]{1,0:T(8,128)(2,1)S(1)}, bf16[64,2048]{1,0:T(8,128)(2,1)S(1)}, u32[]{:S(2)}, u32[]{:S(2)}) collective-permute-start(bf16[64,2048]{1,0:T(8,128)(2,1)S(1)} %fusion.3.refs_14_), channel_id=1, source_target_pairs={{4,8},{6,10},{5,9},{7,11},{20,24},{22,26},{21,25},{23,27}} | collective-permute-start | bytes 786440 | tf_op jit(solution)/shard_map/ppermute | solution.py:466
  35.7 3.6 %shard_map.105 = (f32[1,4096]{1,0:T(1,128)S(1)}, bf16[512,2048]{1,0:T(8,128)(2,1)S(1)}, bf16[512,2048]{1,0:T(8,128)(2,1)S(1)}) custom-call(f32[1,4096]{1,0:T(1,128)S(1)} %get-tuple-element.56.refs_0_, bf16[512,4096]{1,0:T(8,128)(2,1)S(1)} %copy-done, ...), custom_call_target="tpu_custom_call", output_to_operand_aliasing={{1}: (12, {}), {2}: (13, {})} | custom-call | flops 1 | bytes 1 | tf_op jit(solution)/shard_map/pallas_call | solution.py:249
  39.4 0.2 fusion.7.refs_13_
  39.5 1.3 %collective-permute-start.8 = (bf16[64,2048]{1,0:T(8,128)(2,1)S(1)}, bf16[64,2048]{1,0:T(8,128)(2,1)S(1)}, u32[]{:S(2)}, u32[]{:S(2)}) collective-permute-start(bf16[64,2048]{1,0:T(8,128)(2,1)S(1)} %fusion.7.refs_13_), channel_id=1, source_target_pairs={{4,8},{6,10},{5,9},{7,11},{20,24},{22,26},{21,25},{23,27}} | collective-permute-start | bytes 786440 | tf_op jit(solution)/shard_map/ppermute | solution.py:466
  40.8 2.2 %collective-permute-done.5 = bf16[64,2048]{1,0:T(8,128)(2,1)S(1)} collective-permute-done((bf16[64,2048]{1,0:T(8,128)(2,1)S(1)}, bf16[64,2048]{1,0:T(8,128)(2,1)S(1)}, u32[]{:S(2)}, u32[]{:S(2)}) %collective-permute-start.5) | collective-permute-done | bytes 262176 | tf_op jit(solution)/shard_map/ppermute | solution.py:466
  43.1 0.2 add_convert_fusion.1.refs_12_
  43.3 1.3 %collective-permute-start.7 = (bf16[64,2048]{1,0:T(8,128)(2,1)S(1)}, bf16[64,2048]{1,0:T(8,128)(2,1)S(1)}, u32[]{:S(2)}, u32[]{:S(2)}) collective-permute-start(bf16[64,2048]{1,0:T(8,128)(2,1)S(1)} %add_convert_fusion.1.refs_12_), channel_id=1, source_target_pairs={{8,12},{10,14},{9,13},{11,15},{24,28},{26,30},{25,29},{27,31}} | collective-permute-start | bytes 786440 | tf_op jit(solution)/shard_map/ppermute | solution.py:466
  44.6 3.6 %shard_map.106 = (f32[1,4096]{1,0:T(1,128)S(1)}, bf16[512,2048]{1,0:T(8,128)(2,1)S(1)}, bf16[512,2048]{1,0:T(8,128)(2,1)S(1)}) custom-call(f32[1,4096]{1,0:T(1,128)S(1)} %get-tuple-element.60.refs_0_, bf16[512,4096]{1,0:T(8,128)(2,1)S(1)} %copy-done, bf16[512,2048]{1,0:T(8,128)(2,1)S(1)} %get-tuple-element.61.refs_2_, ...), custom_call_target="tpu_custom_call" | custom-call | flops 1 | bytes 1 | tf_op jit(solution)/shard_map/pallas_call | solution.py:249
  48.2 0.9 %collective-permute-done.8 = bf16[64,2048]{1,0:T(8,128)(2,1)S(1)} collective-permute-done((bf16[64,2048]{1,0:T(8,128)(2,1)S(1)}, bf16[64,2048]{1,0:T(8,128)(2,1)S(1)}, u32[]{:S(2)}, u32[]{:S(2)}) %collective-permute-start.8) | collective-permute-done | bytes 262176 | tf_op jit(solution)/shard_map/ppermute | solution.py:466
  49.1 0.2 add_convert_fusion.refs_15_
  49.3 1.5 %collective-permute-start.9 = (bf16[64,2048]{1,0:T(8,128)(2,1)S(1)}, bf16[64,2048]{1,0:T(8,128)(2,1)S(1)}, u32[]{:S(2)}, u32[]{:S(2)}) collective-permute-start(bf16[64,2048]{1,0:T(8,128)(2,1)S(1)} %add_convert_fusion.refs_15_), channel_id=1, source_target_pairs={{8,12},{10,14},{9,13},{11,15},{24,28},{26,30},{25,29},{27,31}} | collective-permute-start | bytes 786440 | tf_op jit(solution)/shard_map/ppermute | solution.py:466
  50.8 0.2 select_convert_fusion
  51.0 0.9 %collective-permute-start.11 = (bf16[64,2048]{1,0:T(8,128)(2,1)S(1)}, bf16[64,2048]{1,0:T(8,128)(2,1)S(1)}, u32[]{:S(2)}, u32[]{:S(2)}) collective-permute-start(bf16[64,2048]{1,0:T(8,128)(2,1)S(1)} %get-tuple-element.74.refs_14_), channel_id=1, source_target_pairs={{0,2},{2,0},{4,6},{6,4},{8,10},{10,8},{12,14},{14,12},{1,3},{3,1},... | collective-permute-start | bytes 786440 | tf_op jit(solution)/shard_map/ppermute | solution.py:474
  51.9 3.5 %shard_map.107 = (f32[1,4096]{1,0:T(1,128)S(1)}, bf16[512,2048]{1,0:T(8,128)(2,1)S(1)}, bf16[512,2048]{1,0:T(8,128)(2,1)S(1)}) custom-call(f32[1,4096]{1,0:T(1,128)S(1)} %get-tuple-element.63.refs_0_, bf16[512,4096]{1,0:T(8,128)(2,1)S(1)} %copy-done, ...), custom_call_target="tpu_custom_call", output_to_operand_aliasing={{1}: (12, {}), {2}: (13, {})} | custom-call | flops 1 | bytes 1 | tf_op jit(solution)/shard_map/pallas_call | solution.py:249
  55.5 0.2 select_convert_fusion.1
  55.8 1.3 %collective-permute-start.10 = (bf16[64,2048]{1,0:T(8,128)(2,1)S(1)}, bf16[64,2048]{1,0:T(8,128)(2,1)S(1)}, u32[]{:S(2)}, u32[]{:S(2)}) collective-permute-start(bf16[64,2048]{1,0:T(8,128)(2,1)S(1)} %get-tuple-element.75.refs_6_), channel_id=1, source_target_pairs={{0,2},{2,0},{4,6},{6,4},{8,10},{10,8},{12,14},{14,12},{1,3},{3,1},... | collective-permute-start | bytes 786440 | tf_op jit(solution)/shard_map/ppermute | solution.py:474
  57.0 2.4 %collective-permute-done.11.refs_3_ = bf16[64,2048]{1,0:T(8,128)(2,1)S(1)} collective-permute-done((bf16[64,2048]{1,0:T(8,128)(2,1)S(1)}, bf16[64,2048]{1,0:T(8,128)(2,1)S(1)}, u32[]{:S(2)}, u32[]{:S(2)}) %collective-permute-start.11) | collective-permute-done | bytes 262176 | tf_op jit(solution)/shard_map/ppermute | solution.py:474
  59.4 3.3 %shard_map.108.refs_6_ = bf16[512,4096]{1,0:T(8,128)(2,1)} custom-call(bf16[512,2048]{1,0:T(8,128)(2,1)S(1)} %get-tuple-element.69.refs_0_, bf16[512,2048]{1,0:T(8,128)(2,1)S(1)} %get-tuple-element.70.refs_1_, bf16[64,2048]{1,0:T(8,128)(2,1)S(1)} %get-tuple-element.73.refs_2_, bf16[64,2048]{1,0:T(8,128)(2,1)S(1)} %collective-permute-done.11.refs_3_, ...), custom_call_target="tpu_custom_call" | custom-call | flops 1 | bytes 1 | tf_op jit(solution)/shard_map/pallas_call | solution.py:249
  62.7 0.4 collective-permute-done.10.refs_3_
  63.1 3.3 %shard_map.109 = bf16[512,4096]{1,0:T(8,128)(2,1)} custom-call(bf16[512,2048]{1,0:T(8,128)(2,1)S(1)} %get-tuple-element.66.refs_0_, bf16[512,2048]{1,0:T(8,128)(2,1)S(1)} %get-tuple-element.67.refs_1_, bf16[64,2048]{1,0:T(8,128)(2,1)S(1)} %get-tuple-element.76.refs_2_, ...), custom_call_target="tpu_custom_call", output_to_operand_aliasing={{}: (6, {})} | custom-call | flops 1 | bytes 1 | tf_op jit(solution)/shard_map/pallas_call | solution.py:249
  (25 shorter events, 0.2 us)
Async XLA Ops:
  0.8 9.9 %collective-permute-start = (bf16[8,4096]{1,0:T(8,128)(2,1)S(1)}, bf16[8,4096]{1,0:T(8,128)(2,1)S(1)}, u32[]{:S(2)}, u32[]{:S(2)}) collective-permute-start(bf16[8,4096]{1,0:T(8,128)(2,1)S(1)} %slice.45.refs_6_), channel_id=1, source_target_pairs={{0,2},{2,4},{4,6},{6,8},{8,10},{10,12},{12,14},{1,3},{3,5},{5,7},{... | collective-permute-start | bytes 196616 | tf_op jit(solution)/shard_map/ppermute | solution.py:288
  4.3 1.0 %copy-start.4 = (bf16[512,256]{1,0:T(8,128)(2,1)S(1)}, bf16[512,256]{1,0:T(8,128)(2,1)}, u32[]{:S(2)}) copy-start(bf16[512,256]{1,0:T(8,128)(2,1)} %refs_3_.1) | copy-start | bytes 786436
  5.2 0.9 %copy-start.5 = (s32[512,64]{0,1:T(8,128)S(1)}, s32[512,64]{0,1:T(8,128)}, u32[]{:S(2)}) copy-start(s32[512,64]{0,1:T(8,128)} %param.14) | copy-start | bytes 393220
  6.1 0.8 %copy-start.7 = (bf16[4,4096]{1,0:T(4,128)(2,1)S(1)}, bf16[4,4096]{1,0:T(4,128)(2,1)}, u32[]{:S(2)}) copy-start(bf16[4,4096]{1,0:T(4,128)(2,1)} %refs_4_.1) | copy-start | bytes 98308
  6.9 0.7 copy-start.8
  7.5 0.7 %copy-start.10 = (bf16[4096]{0:T(1024)(128)(2,1)S(1)}, bf16[4096]{0:T(1024)(128)(2,1)}, u32[]{:S(2)}) copy-start(bf16[4096]{0:T(1024)(128)(2,1)} %param.17) | copy-start | bytes 24580
  8.2 0.7 copy-start.11
  10.8 2.2 %copy-start.1 = (bf16[512,4096]{1,0:T(8,128)(2,1)S(1)}, bf16[512,4096]{1,0:T(8,128)(2,1)}, u32[]{:S(2)}) copy-start(bf16[512,4096]{1,0:T(8,128)(2,1)} %refs_1_.7) | copy-start | bytes 12582916
  12.9 7.7 %copy-start.2 = (bf16[512,4096]{1,0:T(8,128)(2,1)S(1)}, bf16[512,4096]{1,0:T(8,128)(2,1)}, u32[]{:S(2)}) copy-start(bf16[512,4096]{1,0:T(8,128)(2,1)} %refs_1_.7) | copy-start | bytes 12582916
  18.4 9.3 %collective-permute-start.1 = (f32[1,4096]{1,0:T(1,128)S(1)}, f32[1,4096]{1,0:T(1,128)S(1)}, u32[]{:S(2)}, u32[]{:S(2)}) collective-permute-start(f32[1,4096]{1,0:T(1,128)S(1)} %get-tuple-element.44.refs_0_), channel_id=1, source_target_pairs={{0,2},{2,0},{4,6},{6,4},{8,10},{10,8},{12,14},{14,12},{1,3},{3,1},... | collective-permute-start | bytes 49160 | tf_op jit(solution)/shard_map/ppermute | solution.py:502
  20.1 8.5 %copy-start.3 = (bf16[512,256]{1,0:T(8,128)(2,1)S(1)}, bf16[512,256]{1,0:T(8,128)(2,1)}, u32[]{:S(2)}) copy-start(bf16[512,256]{1,0:T(8,128)(2,1)} %refs_2_.1) | copy-start | bytes 786436
  20.1 7.7 %collective-permute-start.2 = (bf16[64,2048]{1,0:T(8,128)(2,1)S(1)}, bf16[64,2048]{1,0:T(8,128)(2,1)S(1)}, u32[]{:S(2)}, u32[]{:S(2)}) collective-permute-start(bf16[64,2048]{1,0:T(8,128)(2,1)S(1)} %get-tuple-element.45.refs_8_), channel_id=1, source_target_pairs={{0,2},{2,0},{4,6},{6,4},{8,10},{10,8},{12,14},{14,12},{1,3},{3,1},... | collective-permute-start | bytes 786440 | tf_op jit(solution)/shard_map/ppermute | solution.py:449
  20.7 9.0 %copy-start = (bf16[512,4096]{1,0:T(8,128)(2,1)S(1)}, bf16[512,4096]{1,0:T(8,128)(2,1)}, u32[]{:S(2)}) copy-start(bf16[512,4096]{1,0:T(8,128)(2,1)} %refs_1_.11) | copy-start | bytes 12582916
  26.2 3.5 %copy-start.9 = (f32[64]{0:T(128)S(1)}, f32[64]{0:T(128)}, u32[]{:S(2)}) copy-start(f32[64]{0:T(128)} %refs_11_.7) | copy-start | bytes 772
  26.2 7.3 %collective-permute-start.4 = (bf16[64,2048]{1,0:T(8,128)(2,1)S(1)}, bf16[64,2048]{1,0:T(8,128)(2,1)S(1)}, u32[]{:S(2)}, u32[]{:S(2)}) collective-permute-start(bf16[64,2048]{1,0:T(8,128)(2,1)S(1)} %get-tuple-element.51.refs_4_), channel_id=1, source_target_pairs={{0,2},{2,0},{4,6},{6,4},{8,10},{10,8},{12,14},{14,12},{1,3},{3,1},... | collective-permute-start | bytes 786440 | tf_op jit(solution)/shard_map/ppermute | solution.py:449
  27.9 6.3 %collective-permute-start.3 = (bf16[64,2048]{1,0:T(8,128)(2,1)S(1)}, bf16[64,2048]{1,0:T(8,128)(2,1)S(1)}, u32[]{:S(2)}, u32[]{:S(2)}) collective-permute-start(bf16[64,2048]{1,0:T(8,128)(2,1)S(1)} %add_convert_fusion.3.refs_3_.refs_12_), channel_id=1, source_target_pairs={{0,4},{2,6},{1,5},{3,7},{16,20},{18,22},{17,21},{19,23}} | collective-permute-start | bytes 786440 | tf_op jit(solution)/shard_map/ppermute | solution.py:466
  33.6 5.8 %collective-permute-start.6 = (bf16[64,2048]{1,0:T(8,128)(2,1)S(1)}, bf16[64,2048]{1,0:T(8,128)(2,1)S(1)}, u32[]{:S(2)}, u32[]{:S(2)}) collective-permute-start(bf16[64,2048]{1,0:T(8,128)(2,1)S(1)} %add_convert_fusion.2.refs_15_), channel_id=1, source_target_pairs={{0,4},{2,6},{1,5},{3,7},{16,20},{18,22},{17,21},{19,23}} | collective-permute-start | bytes 786440 | tf_op jit(solution)/shard_map/ppermute | solution.py:466
  34.4 8.6 %collective-permute-start.5 = (bf16[64,2048]{1,0:T(8,128)(2,1)S(1)}, bf16[64,2048]{1,0:T(8,128)(2,1)S(1)}, u32[]{:S(2)}, u32[]{:S(2)}) collective-permute-start(bf16[64,2048]{1,0:T(8,128)(2,1)S(1)} %fusion.3.refs_14_), channel_id=1, source_target_pairs={{4,8},{6,10},{5,9},{7,11},{20,24},{22,26},{21,25},{23,27}} | collective-permute-start | bytes 786440 | tf_op jit(solution)/shard_map/ppermute | solution.py:466
  39.5 9.5 %collective-permute-start.8 = (bf16[64,2048]{1,0:T(8,128)(2,1)S(1)}, bf16[64,2048]{1,0:T(8,128)(2,1)S(1)}, u32[]{:S(2)}, u32[]{:S(2)}) collective-permute-start(bf16[64,2048]{1,0:T(8,128)(2,1)S(1)} %fusion.7.refs_13_), channel_id=1, source_target_pairs={{4,8},{6,10},{5,9},{7,11},{20,24},{22,26},{21,25},{23,27}} | collective-permute-start | bytes 786440 | tf_op jit(solution)/shard_map/ppermute | solution.py:466
  43.3 7.5 %collective-permute-start.7 = (bf16[64,2048]{1,0:T(8,128)(2,1)S(1)}, bf16[64,2048]{1,0:T(8,128)(2,1)S(1)}, u32[]{:S(2)}, u32[]{:S(2)}) collective-permute-start(bf16[64,2048]{1,0:T(8,128)(2,1)S(1)} %add_convert_fusion.1.refs_12_), channel_id=1, source_target_pairs={{8,12},{10,14},{9,13},{11,15},{24,28},{26,30},{25,29},{27,31}} | collective-permute-start | bytes 786440 | tf_op jit(solution)/shard_map/ppermute | solution.py:466
  49.3 6.2 %collective-permute-start.9 = (bf16[64,2048]{1,0:T(8,128)(2,1)S(1)}, bf16[64,2048]{1,0:T(8,128)(2,1)S(1)}, u32[]{:S(2)}, u32[]{:S(2)}) collective-permute-start(bf16[64,2048]{1,0:T(8,128)(2,1)S(1)} %add_convert_fusion.refs_15_), channel_id=1, source_target_pairs={{8,12},{10,14},{9,13},{11,15},{24,28},{26,30},{25,29},{27,31}} | collective-permute-start | bytes 786440 | tf_op jit(solution)/shard_map/ppermute | solution.py:466
  51.0 8.4 %collective-permute-start.11 = (bf16[64,2048]{1,0:T(8,128)(2,1)S(1)}, bf16[64,2048]{1,0:T(8,128)(2,1)S(1)}, u32[]{:S(2)}, u32[]{:S(2)}) collective-permute-start(bf16[64,2048]{1,0:T(8,128)(2,1)S(1)} %get-tuple-element.74.refs_14_), channel_id=1, source_target_pairs={{0,2},{2,0},{4,6},{6,4},{8,10},{10,8},{12,14},{14,12},{1,3},{3,1},... | collective-permute-start | bytes 786440 | tf_op jit(solution)/shard_map/ppermute | solution.py:474
  51.9 7.5 %copy-start.6 = (f32[4096]{0:T(1024)S(1)}, f32[4096]{0:T(1024)}, u32[]{:S(2)}) copy-start(f32[4096]{0:T(1024)} %param.19) | copy-start | bytes 49156
  55.8 7.3 %collective-permute-start.10 = (bf16[64,2048]{1,0:T(8,128)(2,1)S(1)}, bf16[64,2048]{1,0:T(8,128)(2,1)S(1)}, u32[]{:S(2)}, u32[]{:S(2)}) collective-permute-start(bf16[64,2048]{1,0:T(8,128)(2,1)S(1)} %get-tuple-element.75.refs_6_), channel_id=1, source_target_pairs={{0,2},{2,0},{4,6},{6,4},{8,10},{10,8},{12,14},{14,12},{1,3},{3,1},... | collective-permute-start | bytes 786440 | tf_op jit(solution)/shard_map/ppermute | solution.py:474

commit v3 on v2

--- a/solution.py
+++ b/solution.py
@@ -28,7 +28,7 @@
 LOG2E = math.log2(math.e)
 MIB = 1024 * 1024
 PREP_LIMIT, STATE_LIMIT, INSIDE_LIMIT, FINAL_LIMIT = 16, 16, 16, 16
-PREP_BYTES, STATE_BYTES, INSIDE_BYTES, FINAL_BYTES = 1, 1, 1, 1
+TAIL_BYTES, PREP_BYTES, STATE_BYTES, INSIDE_BYTES, FINAL_BYTES = 16 << 20, 1, 1, 1, 1
 
 
 def iota(shape, axis):
@@ -113,7 +113,8 @@
     taps_ref[KERNEL + 1 :, :] = jnp.zeros((7 - KERNEL, width), f32)
 
 
-def mixing_kernel(pieces_ref, bt_ref, c_ref, left_ref, right_ref, scores_ref, ct_ref):
+def mixing_kernel(decay_in, pieces_ref, bt_ref, c_ref, left_ref, right_ref, scores_ref, ct_ref, decay_ref):
+    decay_ref[...] = decay_in[...]
     groups = c_ref.shape[1] // NSTATE
     heads = pieces_ref.shape[1] // 4
     per_group = heads // groups
@@ -144,11 +145,16 @@
             scores_ref[g, rows, :] = jnp.where(causal, dot(reads[rows], bt_ref[cols, rows]), 0.0)
 
 
-def state_kernel(decay_in, x_ref, tail_ref, taps_ref, pieces_ref, spread_ref, bt_ref, rows_ref, f_ref, local_ref, own_ref, given_ref, decay_ref):
+def state_kernel(start, decay_in, x_ref, tail_ref, taps_ref, pieces_ref, spread_ref, bt_ref, rows_ref, f_ref, local_ref, own_ref, given_ref, decay_ref):
     half = NSTATE // 2
+    group_width = x_ref.shape[1] // (bt_ref.shape[0] // NSTATE)
     decay_ref[...] = decay_in[...]
-    for t in range(LANES // TILE):
-        cols = slice(t * TILE, (t + 1) * TILE)
+    for t in range(f_ref.shape[1] // TILE):
+        here = slice(t * TILE, (t + 1) * TILE)
+        lane = start + t * TILE
+        cols = slice(lane, lane + TILE)
+        inner = slice(lane % group_width, lane % group_width + TILE)
+        mine = slice(lane // group_width * NSTATE, (lane // group_width + 1) * NSTATE)
         taps = taps_ref[:, cols]
         rate = rows_ref[0:1, cols]
         running = None
@@ -165,59 +171,68 @@
                 moved = pltpu.roll(padded, back, 0)[TAIL:]
                 summed = summed + taps[KERNEL - 1 - back : KERNEL - back] * moved
             filtered = silu_of_twice(summed).astype(bf16)
-            f_ref[rows, cols] = filtered
-            wide = dot(pieces_ref[rows, :], spread_ref[:, cols])
+            f_ref[rows, here] = filtered
+            wide = dot(pieces_ref[rows, mine], spread_ref[:, inner])
             weight = jnp.exp2(rate * (wide[SUB - 1 : SUB] - wide))
             weighted = (weight * filtered.astype(f32)).astype(bf16)
-            part = dot(bt_ref[:, rows], weighted)
+            part = dot(bt_ref[mine, rows], weighted)
             running = part if s == 0 else rows_ref[2 + s : 3 + s, cols] * running + part
             if s < NSUB - 1:
-                local_ref[s, :, cols] = running.astype(bf16)
+                local_ref[s, :, here] = running.astype(bf16)
         running = running.astype(bf16)
-        own_ref[:, cols] = running[:half]
-        given_ref[:, cols] = running[half:]
+        own_ref[:, here] = running[:half]
+        given_ref[:, here] = running[half:]
 
 
 def inside_kernel(
-    start, decay_in, z_ref, f_ref, local_ref, c_ref, pieces_ref, spread_ref, left_ref, right_ref, scores_ref, rows_ref,
-    rate_ref, *refs,
+    start, skip, size, decay_in, z_ref, f_ref, local_ref, c_ref, pieces_ref, spread_ref, left_ref, right_ref,
+    scores_ref, rows_ref, rate_ref, *refs,
 ):
     decay_ref, p_ref, g_ref, wall = refs[-4:]
     decay_ref[...] = decay_in[...]
-    first_head = (start + pl.program_id(0) * ILANES) >> HEAD_SHIFT
+    group_width = z_ref.shape[1] // (c_ref.shape[1] // NSTATE)
     wall[...] = jnp.zeros_like(wall)
     first_lanes = iota((SUB, 128), 1) < HEAD_DIM
-    for s in range(NSUB):
-        rows = slice(s * SUB, (s + 1) * SUB)
-        for q in range(ILANES // HEAD_DIM):
-            wall[16 * q : 16 * q + 16, q * SUB : (q + 1) * SUB] = right_ref[16 * q : 16 * q + 16, rows]
-        scores = scores_ref[0, rows, :]
-        left = left_ref[rows, :]
-        pieces = pieces_ref[rows, :]
-        reads = c_ref[rows, :]
-        for r in range(ILANES // TILE):
-            cols = slice(r * TILE, (r + 1) * TILE)
-            growth = jnp.exp2(rows_ref[0:1, cols] * dot(pieces, spread_ref[:, cols]))
-            gate = silu_of_twice(0.5 * z_ref[rows, cols].astype(f32))
-            g_ref[rows, cols] = (gate * growth * rows_ref[8 + s : 9 + s, cols]).astype(bf16)
-            filtered = f_ref[rows, cols].astype(f32)
-            total = rows_ref[1:2, cols] * filtered
-            if s > 0:
-                total = total + growth * dot(reads, local_ref[s - 1, :, cols])
-            insides = []
-            for q in range(2 * r, 2 * r + 2):
-                spans = dot(left, wall[:, 2 * q * SUB : (2 * q + 2) * SUB])
-                mixing = []
-                for k in range(2):
-                    scale = rate_ref[first_head + 2 * q + k] * (-LOG2E / 1024.0)
-                    decays = jnp.exp2(jnp.maximum(spans[:, k * SUB : (k + 1) * SUB], 0.0) * scale)
-                    mixing.append((decays * scores).astype(bf16))
-                pair = filtered[:, 128 * (q - 2 * r) : 128 * (q - 2 * r) + 128]
-                stacked = jnp.concatenate(
-                    [jnp.where(first_lanes, pair, 0.0), jnp.where(first_lanes, 0.0, pair)], axis=0
-                ).astype(bf16)
-                insides.append(dot(jnp.concatenate(mixing, axis=1), stacked))
-            p_ref[rows, cols] = ((total + jnp.concatenate(insides, axis=1)) * gate).astype(bf16)
+    for b in range(size // ILANES):
+        lane = start + b * ILANES
+        group = lane // group_width
+        mine = slice(group * NSTATE, (group + 1) * NSTATE)
+        place = lane // HEAD_DIM * 16
+        for s in range(NSUB):
+            rows = slice(s * SUB, (s + 1) * SUB)
+            for q in range(ILANES // HEAD_DIM):
+                wall[16 * q : 16 * q + 16, q * SUB : (q + 1) * SUB] = right_ref[place + 16 * q : place + 16 * q + 16, rows]
+            scores = scores_ref[group, rows, :]
+            left = left_ref[rows, place : place + ILANES // HEAD_DIM * 16]
+            pieces = pieces_ref[rows, mine]
+            reads = c_ref[rows, mine]
+            for r in range(ILANES // TILE):
+                first = lane + r * TILE
+                cols = slice(first, first + TILE)
+                here = slice(skip + b * ILANES + r * TILE, skip + b * ILANES + (r + 1) * TILE)
+                inner = slice(first % group_width, first % group_width + TILE)
+                growth = jnp.exp2(rows_ref[0:1, cols] * dot(pieces, spread_ref[:, inner]))
+                gate = silu_of_twice(0.5 * z_ref[rows, cols].astype(f32))
+                g_ref[rows, here] = (gate * growth * rows_ref[8 + s : 9 + s, cols]).astype(bf16)
+                filtered = f_ref[rows, here].astype(f32)
+                total = rows_ref[1:2, cols] * filtered
+                if s > 0:
+                    total = total + growth * dot(reads, local_ref[s - 1, :, here])
+                insides = []
+                for q in range(2):
+                    base = 2 * (2 * r + q)
+                    spans = dot(left, wall[:, base * SUB : (base + 2) * SUB])
+                    mixing = []
+                    for k in range(2):
+                        scale = rate_ref[lane // HEAD_DIM + base + k] * (-LOG2E / 1024.0)
+                        decays = jnp.exp2(jnp.maximum(spans[:, k * SUB : (k + 1) * SUB], 0.0) * scale)
+                        mixing.append((decays * scores).astype(bf16))
+                    pair = filtered[:, 128 * q : 128 * q + 128]
+                    stacked = jnp.concatenate(
+                        [jnp.where(first_lanes, pair, 0.0), jnp.where(first_lanes, 0.0, pair)], axis=0
+                    ).astype(bf16)
+                    insides.append(dot(jnp.concatenate(mixing, axis=1), stacked))
+                p_ref[rows, here] = ((total + jnp.concatenate(insides, axis=1)) * gate).astype(bf16)
 
 
 def final_kernel(p_ref, g_ref, mine_ref, other_ref, c_ref, gain_ref, *rest):
@@ -226,12 +241,13 @@
     mean = jnp.where(same, 1.0 / HEAD_DIM, 0.0).astype(bf16)
     for t in range(out_ref.shape[1] // TILE):
         cols = slice(t * TILE, (t + 1) * TILE)
-        entering = jnp.concatenate([mine_ref[:, cols], other_ref[:, cols]], axis=0)
+        here = pl.ds(pl.multiple_of(pl.program_id(0) * out_ref.shape[1] + t * TILE, TILE), TILE)
+        entering = jnp.concatenate([mine_ref[:, here], other_ref[:, here]], axis=0)
         gain = gain_ref[:, cols]
         for s in range(NSUB):
             rows = slice(s * SUB, (s + 1) * SUB)
             carried = dot(c_ref[rows, :], entering)
-            gated = p_ref[rows, cols].astype(f32) + carried * g_ref[rows, cols].astype(f32)
+            gated = p_ref[rows, here].astype(f32) + carried * g_ref[rows, here].astype(f32)
             meansq = dot((gated * gated).astype(bf16), mean)
             out_ref[rows, cols] = (gated * lax.rsqrt(meansq + 1e-05) * gain).astype(bf16)
 
@@ -284,7 +300,19 @@
     assert sum(WIDTHS) == width
     hbm = pl.BlockSpec(memory_space=pltpu.HBM)
 
-    last_rows = features[tokens - TAIL :]
+    def last_rows_kernel(x_ref, out_ref):
+        out_ref[...] = x_ref[...].astype(f32)[16 - TAIL :].astype(bf16)
+
+    last_rows = call(
+        last_rows_kernel,
+        (features,),
+        [pl.BlockSpec((16, width), lambda i: (tokens // 16 - 1, 0))],
+        limit=16,
+        cost=TAIL_BYTES,
+        grid=(1,),
+        out_specs=full((TAIL, width)),
+        out_shape=shape((TAIL, width), bf16),
+    )
     tail = lax.ppermute(last_rows, "ctx", [(i, i + 1) for i in range(runs - 1)])
     prepared = (
         ((tokens, 4 * heads), bf16),
@@ -319,17 +347,18 @@
         ],
     )
 
-    def mixing_parts(after):
+    def mixing_parts(decay, after):
         kinds = (
             ((tokens, 16 * heads), bf16),
             ((16 * heads, tokens), bf16),
             ((groups, tokens, SUB), f32),
             ((tokens, groups * NSTATE), bf16),
+            ((1, width), f32),
         )
         return call(
             mixing_kernel,
-            (pieces, bt, output_proj),
-            [full((tokens, 4 * heads)), full((groups * NSTATE, tokens)), full((tokens, groups * NSTATE))],
+            (decay, pieces, bt, output_proj),
+            [full((1, width)), full((tokens, 4 * heads)), full((groups * NSTATE, tokens)), full((tokens, groups * NSTATE))],
             after,
             grid=(1,),
             out_specs=[full(dims) for dims, _ in kinds],
@@ -337,36 +366,17 @@
         )
 
     gain = norm_gain[None]
+    vmem = pl.BlockSpec(memory_space=pltpu.VMEM)
 
     def conv_states(start, lanes, decay, after):
-        first = start // LANES
-        column = lambda i: (0, first + i)
-        group = lambda i: (first + i) * LANES // group_width
-        mine = lambda i: (0, i)
         return call(
-            state_kernel,
+            functools.partial(state_kernel, start),
             (decay, features, tail, taps, pieces, spread, bt, rows),
-            [
-                full((1, width)),
-                pl.BlockSpec((tokens, LANES), column),
-                pl.BlockSpec((TAIL, LANES), column),
-                pl.BlockSpec((8, LANES), column),
-                pl.BlockSpec((tokens, 4 * per_group), lambda i: (0, group(i))),
-                pl.BlockSpec((4 * per_group, LANES), lambda i: (0, (first + i) % (group_width // LANES))),
-                pl.BlockSpec((NSTATE, tokens), lambda i: (group(i), 0)),
-                pl.BlockSpec((16, LANES), column),
-            ],
+            [vmem] * 8,
             after,
             limit=STATE_LIMIT,
             cost=STATE_BYTES,
-            grid=(lanes // LANES,),
-            out_specs=[
-                pl.BlockSpec((tokens, LANES), mine),
-                pl.BlockSpec((NSUB - 1, NSTATE, LANES), lambda i: (0, 0, i)),
-                pl.BlockSpec((half, LANES), mine),
-                pl.BlockSpec((half, LANES), mine),
-                full((1, width)),
-            ],
+            out_specs=[vmem] * 5,
             out_shape=(
                 shape((tokens, lanes), bf16),
                 shape((NSUB - 1, NSTATE, lanes), bf16),
@@ -377,35 +387,15 @@
         )
 
     def inside(start, lanes, inner, whole, filtered, local, filled, decay, after):
-        first = start // ILANES
-        skip = inner // ILANES
         heads_here = ILANES // HEAD_DIM
-        column = lambda i: (0, first + i)
-        group = lambda i: (first + i) * ILANES // group_width
-        mine = lambda i: (0, skip + i)
         return call(
-            functools.partial(inside_kernel, start),
+            functools.partial(inside_kernel, start, inner, lanes),
             (decay, output_switch, filtered, local, reads, pieces, spread, left, right, scores, rows, head_rate, *filled),
-            [
-                full((1, width)),
-                pl.BlockSpec((tokens, ILANES), column),
-                pl.BlockSpec((tokens, ILANES), mine),
-                pl.BlockSpec((NSUB - 1, NSTATE, ILANES), lambda i: (0, 0, skip + i)),
-                pl.BlockSpec((tokens, NSTATE), lambda i: (0, group(i))),
-                pl.BlockSpec((tokens, 4 * per_group), lambda i: (0, group(i))),
-                pl.BlockSpec((4 * per_group, ILANES), lambda i: (0, (first + i) % (group_width // ILANES))),
-                pl.BlockSpec((tokens, 16 * heads_here), column),
-                pl.BlockSpec((16 * heads_here, tokens), lambda i: (first + i, 0)),
-                pl.BlockSpec((1, tokens, SUB), lambda i: (group(i), 0, 0)),
-                pl.BlockSpec((16, ILANES), column),
-                pl.BlockSpec(memory_space=pltpu.SMEM),
-            ]
-            + [pl.BlockSpec(memory_space=pl.ANY)] * len(filled),
+            [vmem] * 11 + [pl.BlockSpec(memory_space=pltpu.SMEM)] + [vmem] * len(filled),
             after,
             limit=INSIDE_LIMIT,
             cost=INSIDE_BYTES,
-            grid=(lanes // ILANES,),
-            out_specs=[full((1, width))] + [pl.BlockSpec((tokens, ILANES), mine)] * 2,
+            out_specs=[vmem] * 3,
             out_shape=(shape((1, width), f32), shape((tokens, whole), bf16), shape((tokens, whole), bf16)),
             input_output_aliases={12: 1, 13: 2} if filled else {},
             scratch_shapes=[pltpu.VMEM((16 * heads_here, heads_here * SUB), bf16)],
@@ -414,15 +404,13 @@
     def final(start, lanes, inner, out, kept, growth, own, other, after):
         block = FLANES if start % FLANES == 0 and lanes % FLANES == 0 else LANES
         first = start // block
-        skip = inner // block
         column = lambda i: (0, first + i)
-        mine = lambda i: (0, i)
         operands = [kept, growth, own, other, reads, gain]
         in_specs = [
-            pl.BlockSpec((tokens, block), mine),
-            pl.BlockSpec((tokens, block), mine),
-            pl.BlockSpec((half, block), lambda i: (0, skip + i)),
-            pl.BlockSpec((half, block), lambda i: (0, skip + i)),
+            vmem,
+            vmem,
+            vmem,
+            vmem,
             pl.BlockSpec((tokens, NSTATE), lambda i: (0, (first + i) * block // group_width)),
             pl.BlockSpec((1, block), column),
         ]
@@ -479,10 +467,10 @@
     now = {"decay": decay}
     travel, entering, remaining = [], {}, []
 
-    def advance():
+    def advance(*chosen):
         waited = []
         for c, steps in enumerate(travel):
-            if remaining[c]:
+            if remaining[c] and c in (chosen or range(len(WIDTHS))):
                 value = next(steps)
                 remaining[c] -= 1
                 if remaining[c]:
@@ -502,18 +490,16 @@
             now["other"] = lax.ppermute(now["decay"], "ctx", swap)
         travel.append(carry(c, made[c][2], made[c][3]))
         remaining.append(pairs + 2)
+        token = advance(c)
+    left, right, scores, reads, now["decay"] = mixing_parts(now["decay"], token)
+    token = advance(*range(len(WIDTHS) - 1))
+    calls = [(c, inner, size) for c, lanes in enumerate(WIDTHS) for inner, size in splits(lanes)]
+    kept = [() for _ in WIDTHS]
+    for k, (c, inner, size) in enumerate(calls):
+        now["decay"], *kept[c] = inside(
+            starts[c] + inner, size, inner, WIDTHS[c], made[c][0], made[c][1], kept[c], now["decay"], token
+        )
         token = advance()
-    left, right, scores, reads = mixing_parts(token)
-    token = token[:-1] + (reads,)
-    kept = []
-    for c, lanes in enumerate(WIDTHS):
-        filled = ()
-        for inner, size in splits(lanes):
-            now["decay"], *filled = inside(
-                starts[c] + inner, size, inner, lanes, made[c][0], made[c][1], filled, now["decay"], token
-            )
-            token = advance()
-        kept.append(filled)
     out = None
     for c, lanes in enumerate(WIDTHS):
         while c not in entering:

time: 66.9 us -> 62.7 us (0.937)
  Pallas kernels: 34.6 us -> 29.8 us
  waiting for transfers between devices: 6.12 us -> 10.2 us
  local copies, waits for them, and re-layouts: 7.66 us -> 4.07 us
    pallas_call x10 -> x11, Pallas kernels: 34.6 us -> 29.8 us  [call(): pl.pallas_call(ordered, in_specs=list(in_specs) + [pl.BlockSpec(memory_sp...]
    unnamed x24 -> x22, local copies, waits for them, and re-layouts: 6.82 us -> 4.07 us
    ppermute x6, waiting for transfers between devices: 3.1 us -> 4.7 us  [carry(): arrived = lax.ppermute(sent, 'ctx', route).astype(f32)]
    ppermute x2, waiting for transfers between devices: 0.22 us -> 1.75 us  [carry(): got = lax.ppermute(given, 'ctx', swap)]
    ppermute x2, waiting for transfers between devices: 2.8 us -> 3.7 us  [carry(): other = lax.ppermute(given, 'ctx', swap)]
    slice x1 -> x0, local copies, waits for them, and re-layouts: 0.84 us -> none  [per_device(): last_rows = features[tokens - TAIL:]]
  transfers between devices with their start and end apart: 12 -> 12, of which waited for: 5 -> 6; matrix products, arithmetic and copies ran while one was open for 3% -> 3% of each run, Pallas kernels for 39% -> 36%
where the time goes in v3:
time: 62.7 us; the launch traced here: 62.4 us
  Pallas kernels  29.8 us (48%)
  starting transfers between devices  16.3 us (26%)
  waiting for transfers between devices  10.2 us (16%)
  local copies, waits for them, and re-layouts  4.07 us (6%)
  other arithmetic  1.69 us (3%)
    pallas_call x11, Pallas kernels, call(): pl.pallas_call(ordered, in_specs=list(in_specs) + [pl.BlockSpec(memory_sp...  29.8 us
    ppermute x6, starting transfers between devices, carry(): arrived = lax.ppermute(sent, 'ctx', route).astype(f32)  6.95 us
    ppermute x6, waiting for transfers between devices, carry(): arrived = lax.ppermute(sent, 'ctx', route).astype(f32)  4.7 us
    unnamed x22, local copies, waits for them, and re-layouts  4.07 us
    ppermute x2, waiting for transfers between devices, carry(): other = lax.ppermute(given, 'ctx', swap)  3.7 us
    ppermute x1, starting transfers between devices, per_device(): tail = lax.ppermute(last_rows, 'ctx', [(i, i + 1) for i in range(runs - 1)])  3.69 us
    ppermute x2, starting transfers between devices, carry(): got = lax.ppermute(given, 'ctx', swap)  2.16 us
    ppermute x2, starting transfers between devices, carry(): other = lax.ppermute(given, 'ctx', swap)  1.95 us
  transfers between devices with their start and end apart: 12, of which 6 were waited for; matrix products, arithmetic and copies ran while one was open for 3% of the time, Pallas kernels for 36%

profile of v3, /device:TPU:16, one launch (start us, length us, event | category | flops | bytes accessed | tf_op | source)
XLA Modules:
  0.0 62.4 jit_solution(11133890534143893780)
XLA Ops:
  0.0 2.2 %copy-done.1 = bf16[512,4096]{1,0:T(8,128)(2,1)S(1)} copy-done((bf16[512,4096]{1,0:T(8,128)(2,1)S(1)}, bf16[512,4096]{1,0:T(8,128)(2,1)}, u32[]{:S(2)}) %copy-start.1) | copy-done | bytes 4194328
  2.2 3.7 %collective-permute-start = (bf16[8,4096]{1,0:T(8,128)(2,1)S(1)}, bf16[8,4096]{1,0:T(8,128)(2,1)S(1)}, u32[]{:S(2)}, u32[]{:S(2)}) collective-permute-start(bf16[8,4096]{1,0:T(8,128)(2,1)S(1)} %shard_map.100.refs_6_), channel_id=1, source_target_pairs={{0,2},{2,4},{4,6},{6,8},{8,10},{10,12},{12,14},{1,3},{3,5},{5,7},{... | collective-permute-start | bytes 196616 | tf_op jit(solution)/shard_map/ppermute | solution.py:316
  6.0 0.0 copy-start.3
  6.0 0.9 %copy-done.3 = bf16[512,256]{1,0:T(8,128)(2,1)S(1)} copy-done((bf16[512,256]{1,0:T(8,128)(2,1)S(1)}, bf16[512,256]{1,0:T(8,128)(2,1)}, u32[]{:S(2)}) %copy-start.3) | copy-done | bytes 262168
  6.9 0.9 %copy-done.5 = s32[512,64]{0,1:T(8,128)S(1)} copy-done((s32[512,64]{0,1:T(8,128)S(1)}, s32[512,64]{0,1:T(8,128)}, u32[]{:S(2)}) %copy-start.5) | copy-done | bytes 131096
  7.8 1.8 %shard_map.101 = (bf16[512,256]{1,0:T(8,128)(2,1)S(1)}, bf16[128,2048]{1,0:T(8,128)(2,1)S(1)}, bf16[256,512]{1,0:T(8,128)(2,1)S(1)}, f32[16,4096]{1,0:T(8,128)S(...) custom-call(s32[64,512]{1,0:T(8,128)S(1)} %bitcast.17, f32[1,64]{1,0:T(1,128)S(1)} %bitcast.20, ...), custom_call_target="tpu_custom_call" | custom-call | flops 1 | bytes 1 | tf_op jit(solution)/shard_map/pallas_call | solution.py:265
  9.7 0.0 collective-permute-done.refs_2_
  9.7 4.3 %shard_map.102 = (bf16[512,2048]{1,0:T(8,128)(2,1)S(1)}, bf16[3,128,2048]{2,1,0:T(8,128)(2,1)S(1)}, bf16[64,2048]{1,0:T(8,128)(2,1)S(1)}, bf16[64,2048]{1,0:T(8,128)(2,1)S(1)}, f32[1,4096]{1,0:T(1,128)S(1)}) custom-call(f32[1,4096]{1,0:T(1,128)S(1)} %get-tuple-element.39.refs_0_, bf16[512,4096]{1,0:T(8,128)(2,1)S(1)} %copy-done.2, ...), custom_call_target="tpu_custom_call" | custom-call | flops 1 | bytes 1 | tf_op jit(solution)/shard_map/pallas_call | solution.py:265
  14.0 1.6 %collective-permute-start.1 = (f32[1,4096]{1,0:T(1,128)S(1)}, f32[1,4096]{1,0:T(1,128)S(1)}, u32[]{:S(2)}, u32[]{:S(2)}) collective-permute-start(f32[1,4096]{1,0:T(1,128)S(1)} %get-tuple-element.45.refs_0_), channel_id=1, source_target_pairs={{0,2},{2,0},{4,6},{6,4},{8,10},{10,8},{12,14},{14,12},{1,3},{3,1},... | collective-permute-start | bytes 49160 | tf_op jit(solution)/shard_map/ppermute | solution.py:490
  15.6 0.1 fusion.9
  15.6 0.6 collective-permute-start.2
  16.2 4.3 %shard_map.103 = (bf16[512,2048]{1,0:T(8,128)(2,1)S(1)}, bf16[3,128,2048]{2,1,0:T(8,128)(2,1)S(1)}, bf16[64,2048]{1,0:T(8,128)(2,1)S(1)}, bf16[64,2048]{1,0:T(8,128)(2,1)S(1)}, f32[1,4096]{1,0:T(1,128)S(1)}) custom-call(f32[1,4096]{1,0:T(1,128)S(1)} %get-tuple-element.45.refs_0_, bf16[512,4096]{1,0:T(8,128)(2,1)S(1)} %copy-done.2, ...), custom_call_target="tpu_custom_call" | custom-call | flops 1 | bytes 1 | tf_op jit(solution)/shard_map/pallas_call | solution.py:265
  20.5 1.6 %collective-permute-start.4 = (bf16[64,2048]{1,0:T(8,128)(2,1)S(1)}, bf16[64,2048]{1,0:T(8,128)(2,1)S(1)}, u32[]{:S(2)}, u32[]{:S(2)}) collective-permute-start(bf16[64,2048]{1,0:T(8,128)(2,1)S(1)} %get-tuple-element.48.refs_4_), channel_id=1, source_target_pairs={{0,2},{2,0},{4,6},{6,4},{8,10},{10,8},{12,14},{14,12},{1,3},{3,1},... | collective-permute-start | bytes 786440 | tf_op jit(solution)/shard_map/ppermute | solution.py:437
  22.1 1.0 %shard_map.104 = (bf16[512,1024]{1,0:T(8,128)(2,1)S(1)}, bf16[1024,512]{1,0:T(8,128)(2,1)S(1)}, f32[2,512,128]{2,1,0:T(8,128)S(1)}, bf16[512,256]{1,0:T(8,128)(2,1)S(1)}, f32[1,4096]{1,0:T(1,128)S(1)}) custom-call(f32[1,4096]{1,0:T(1,128)S(1)} %get-tuple-element.47.refs_0_, bf16[512,256]{1,0:T(8,128)(2,1)S(1)} %get-tuple-element.41.refs_4_.refs_1_.refs_5_, ...), custom_call_target="tpu_custom_call" | custom-call | flops 1 | bytes 1 | tf_op jit(solution)/shard_map/pallas_call | solution.py:265
  23.1 0.0 collective-permute-done.1
  23.1 1.4 %collective-permute-done.2 = bf16[64,2048]{1,0:T(8,128)(2,1)S(1)} collective-permute-done((bf16[64,2048]{1,0:T(8,128)(2,1)S(1)}, bf16[64,2048]{1,0:T(8,128)(2,1)S(1)}, u32[]{:S(2)}, u32[]{:S(2)}) %collective-permute-start.2) | collective-permute-done | bytes 262176 | tf_op jit(solution)/shard_map/ppermute | solution.py:437
  24.5 0.1 add_convert_fusion.3.refs_12_
  24.6 0.9 %collective-permute-start.3 = (bf16[64,2048]{1,0:T(8,128)(2,1)S(1)}, bf16[64,2048]{1,0:T(8,128)(2,1)S(1)}, u32[]{:S(2)}, u32[]{:S(2)}) collective-permute-start(bf16[64,2048]{1,0:T(8,128)(2,1)S(1)} %add_convert_fusion.3.refs_12_), channel_id=1, source_target_pairs={{0,4},{2,6},{1,5},{3,7},{16,20},{18,22},{17,21},{19,23}} | collective-permute-start | bytes 786440 | tf_op jit(solution)/shard_map/ppermute | solution.py:454
  25.5 3.1 %shard_map.105 = (f32[1,4096]{1,0:T(1,128)S(1)}, bf16[512,2048]{1,0:T(8,128)(2,1)S(1)}, bf16[512,2048]{1,0:T(8,128)(2,1)S(1)}) custom-call(f32[1,4096]{1,0:T(1,128)S(1)} %get-tuple-element.49.refs_0_, bf16[512,4096]{1,0:T(8,128)(2,1)S(1)} %copy-done, bf16[512,2048]{1,0:T(8,128)(2,1)S(1)} %get-tuple-element.50.refs_2_, ...), custom_call_target="tpu_custom_call" | custom-call | flops 1 | bytes 1 | tf_op jit(solution)/shard_map/pallas_call | solution.py:265
  28.6 0.3 collective-permute-done.4
  29.0 0.1 add_convert_fusion.2.refs_15_
  29.1 0.7 %collective-permute-start.6 = (bf16[64,2048]{1,0:T(8,128)(2,1)S(1)}, bf16[64,2048]{1,0:T(8,128)(2,1)S(1)}, u32[]{:S(2)}, u32[]{:S(2)}) collective-permute-start(bf16[64,2048]{1,0:T(8,128)(2,1)S(1)} %add_convert_fusion.2.refs_15_), channel_id=1, source_target_pairs={{0,4},{2,6},{1,5},{3,7},{16,20},{18,22},{17,21},{19,23}} | collective-permute-start | bytes 786440 | tf_op jit(solution)/shard_map/ppermute | solution.py:454
  29.8 0.0 collective-permute-done.3
  29.8 0.2 fusion.3.refs_14_
  30.0 1.3 %collective-permute-start.5 = (bf16[64,2048]{1,0:T(8,128)(2,1)S(1)}, bf16[64,2048]{1,0:T(8,128)(2,1)S(1)}, u32[]{:S(2)}, u32[]{:S(2)}) collective-permute-start(bf16[64,2048]{1,0:T(8,128)(2,1)S(1)} %fusion.3.refs_14_), channel_id=1, source_target_pairs={{4,8},{6,10},{5,9},{7,11},{20,24},{22,26},{21,25},{23,27}} | collective-permute-start | bytes 786440 | tf_op jit(solution)/shard_map/ppermute | solution.py:454
  31.3 3.1 %shard_map.106 = (f32[1,4096]{1,0:T(1,128)S(1)}, bf16[512,2048]{1,0:T(8,128)(2,1)S(1)}, bf16[512,2048]{1,0:T(8,128)(2,1)S(1)}) custom-call(f32[1,4096]{1,0:T(1,128)S(1)} %get-tuple-element.58.refs_0_, bf16[512,4096]{1,0:T(8,128)(2,1)S(1)} %copy-done, ...), custom_call_target="tpu_custom_call", output_to_operand_aliasing={{1}: (12, {}), {2}: (13, {})} | custom-call | flops 1 | bytes 1 | tf_op jit(solution)/shard_map/pallas_call | solution.py:265
  34.4 0.0 collective-permute-done.6
  34.4 0.2 fusion.7.refs_13_
  34.6 1.3 %collective-permute-start.8 = (bf16[64,2048]{1,0:T(8,128)(2,1)S(1)}, bf16[64,2048]{1,0:T(8,128)(2,1)S(1)}, u32[]{:S(2)}, u32[]{:S(2)}) collective-permute-start(bf16[64,2048]{1,0:T(8,128)(2,1)S(1)} %fusion.7.refs_13_), channel_id=1, source_target_pairs={{4,8},{6,10},{5,9},{7,11},{20,24},{22,26},{21,25},{23,27}} | collective-permute-start | bytes 786440 | tf_op jit(solution)/shard_map/ppermute | solution.py:454
  35.9 3.6 %collective-permute-done.5 = bf16[64,2048]{1,0:T(8,128)(2,1)S(1)} collective-permute-done((bf16[64,2048]{1,0:T(8,128)(2,1)S(1)}, bf16[64,2048]{1,0:T(8,128)(2,1)S(1)}, u32[]{:S(2)}, u32[]{:S(2)}) %collective-permute-start.5) | collective-permute-done | bytes 262176 | tf_op jit(solution)/shard_map/ppermute | solution.py:454
  39.5 0.2 add_convert_fusion.1.refs_12_
  39.7 1.3 %collective-permute-start.7 = (bf16[64,2048]{1,0:T(8,128)(2,1)S(1)}, bf16[64,2048]{1,0:T(8,128)(2,1)S(1)}, u32[]{:S(2)}, u32[]{:S(2)}) collective-permute-start(bf16[64,2048]{1,0:T(8,128)(2,1)S(1)} %add_convert_fusion.1.refs_12_), channel_id=1, source_target_pairs={{8,12},{10,14},{9,13},{11,15},{24,28},{26,30},{25,29},{27,31}} | collective-permute-start | bytes 786440 | tf_op jit(solution)/shard_map/ppermute | solution.py:454
  41.0 3.1 %shard_map.107 = (f32[1,4096]{1,0:T(1,128)S(1)}, bf16[512,2048]{1,0:T(8,128)(2,1)S(1)}, bf16[512,2048]{1,0:T(8,128)(2,1)S(1)}) custom-call(f32[1,4096]{1,0:T(1,128)S(1)} %get-tuple-element.62.refs_0_, bf16[512,4096]{1,0:T(8,128)(2,1)S(1)} %copy-done, bf16[512,2048]{1,0:T(8,128)(2,1)S(1)} %get-tuple-element.63.refs_2_, ...), custom_call_target="tpu_custom_call" | custom-call | flops 1 | bytes 1 | tf_op jit(solution)/shard_map/pallas_call | solution.py:265
  44.1 0.9 %collective-permute-done.8 = bf16[64,2048]{1,0:T(8,128)(2,1)S(1)} collective-permute-done((bf16[64,2048]{1,0:T(8,128)(2,1)S(1)}, bf16[64,2048]{1,0:T(8,128)(2,1)S(1)}, u32[]{:S(2)}, u32[]{:S(2)}) %collective-permute-start.8) | collective-permute-done | bytes 262176 | tf_op jit(solution)/shard_map/ppermute | solution.py:454
  45.1 0.2 add_convert_fusion.refs_15_
  45.3 1.5 %collective-permute-start.9 = (bf16[64,2048]{1,0:T(8,128)(2,1)S(1)}, bf16[64,2048]{1,0:T(8,128)(2,1)S(1)}, u32[]{:S(2)}, u32[]{:S(2)}) collective-permute-start(bf16[64,2048]{1,0:T(8,128)(2,1)S(1)} %add_convert_fusion.refs_15_), channel_id=1, source_target_pairs={{8,12},{10,14},{9,13},{11,15},{24,28},{26,30},{25,29},{27,31}} | collective-permute-start | bytes 786440 | tf_op jit(solution)/shard_map/ppermute | solution.py:454
  46.8 0.0 collective-permute-done.7
  46.8 0.2 select_convert_fusion
  47.1 0.1 collective-permute-start.11
  47.1 0.0 copy-start.6
  47.1 3.1 %shard_map.108 = (f32[1,4096]{1,0:T(1,128)S(1)}, bf16[512,2048]{1,0:T(8,128)(2,1)S(1)}, bf16[512,2048]{1,0:T(8,128)(2,1)S(1)}) custom-call(f32[1,4096]{1,0:T(1,128)S(1)} %get-tuple-element.65.refs_0_, bf16[512,4096]{1,0:T(8,128)(2,1)S(1)} %copy-done, ...), custom_call_target="tpu_custom_call", output_to_operand_aliasing={{1}: (12, {}), {2}: (13, {})} | custom-call | flops 1 | bytes 1 | tf_op jit(solution)/shard_map/pallas_call | solution.py:265
  50.3 0.2 collective-permute-done.9
  50.5 0.2 select_convert_fusion.1
  50.7 1.9 %collective-permute-start.10 = (bf16[64,2048]{1,0:T(8,128)(2,1)S(1)}, bf16[64,2048]{1,0:T(8,128)(2,1)S(1)}, u32[]{:S(2)}, u32[]{:S(2)}) collective-permute-start(bf16[64,2048]{1,0:T(8,128)(2,1)S(1)} %get-tuple-element.77.refs_6_), channel_id=1, source_target_pairs={{0,2},{2,0},{4,6},{6,4},{8,10},{10,8},{12,14},{14,12},{1,3},{3,1},... | collective-permute-start | bytes 786440 | tf_op jit(solution)/shard_map/ppermute | solution.py:462
  52.6 3.7 %collective-permute-done.11.refs_3_ = bf16[64,2048]{1,0:T(8,128)(2,1)S(1)} collective-permute-done((bf16[64,2048]{1,0:T(8,128)(2,1)S(1)}, bf16[64,2048]{1,0:T(8,128)(2,1)S(1)}, u32[]{:S(2)}, u32[]{:S(2)}) %collective-permute-start.11) | collective-permute-done | bytes 262176 | tf_op jit(solution)/shard_map/ppermute | solution.py:462
  56.3 3.0 %shard_map.109.refs_6_ = bf16[512,4096]{1,0:T(8,128)(2,1)} custom-call(bf16[512,2048]{1,0:T(8,128)(2,1)S(1)} %get-tuple-element.71.refs_0_, bf16[512,2048]{1,0:T(8,128)(2,1)S(1)} %get-tuple-element.72.refs_1_, bf16[64,2048]{1,0:T(8,128)(2,1)S(1)} %get-tuple-element.75.refs_2_, bf16[64,2048]{1,0:T(8,128)(2,1)S(1)} %collective-permute-done.11.refs_3_, ...), custom_call_target="tpu_custom_call" | custom-call | flops 1 | bytes 1 | tf_op jit(solution)/shard_map/pallas_call | solution.py:265
  59.3 0.0 collective-permute-done.10.refs_3_
  59.3 3.0 %shard_map.110 = bf16[512,4096]{1,0:T(8,128)(2,1)} custom-call(bf16[512,2048]{1,0:T(8,128)(2,1)S(1)} %get-tuple-element.68.refs_0_, bf16[512,2048]{1,0:T(8,128)(2,1)S(1)} %get-tuple-element.69.refs_1_, bf16[64,2048]{1,0:T(8,128)(2,1)S(1)} %get-tuple-element.78.refs_2_, ...), custom_call_target="tpu_custom_call", output_to_operand_aliasing={{}: (6, {})} | custom-call | flops 1 | bytes 1 | tf_op jit(solution)/shard_map/pallas_call | solution.py:265
  (23 shorter events, 0.2 us)
Async XLA Ops:
  0.0 2.2 %copy-start.1 = (bf16[512,4096]{1,0:T(8,128)(2,1)S(1)}, bf16[512,4096]{1,0:T(8,128)(2,1)}, u32[]{:S(2)}) copy-start(bf16[512,4096]{1,0:T(8,128)(2,1)} %refs_1_.7) | copy-start | bytes 12582916
  2.2 3.7 %copy-start.7 = (bf16[4,4096]{1,0:T(4,128)(2,1)S(1)}, bf16[4,4096]{1,0:T(4,128)(2,1)}, u32[]{:S(2)}) copy-start(bf16[4,4096]{1,0:T(4,128)(2,1)} %refs_4_.1) | copy-start | bytes 98308
  2.2 3.7 %copy-start.8 = (f32[64]{0:T(128)S(1)}, f32[64]{0:T(128)}, u32[]{:S(2)}) copy-start(f32[64]{0:T(128)} %refs_11_.7) | copy-start | bytes 772
  2.2 3.8 %copy-start.9 = (bf16[4096]{0:T(1024)(128)(2,1)S(1)}, bf16[4096]{0:T(1024)(128)(2,1)}, u32[]{:S(2)}) copy-start(bf16[4096]{0:T(1024)(128)(2,1)} %param.17) | copy-start | bytes 24580
  2.2 3.8 %copy-start.10 = (f32[64]{0:T(128)S(1)}, f32[64]{0:T(128)}, u32[]{:S(2)}) copy-start(f32[64]{0:T(128)} %param.18) | copy-start | bytes 772
  2.2 7.5 %copy-start.2 = (bf16[512,4096]{1,0:T(8,128)(2,1)S(1)}, bf16[512,4096]{1,0:T(8,128)(2,1)}, u32[]{:S(2)}) copy-start(bf16[512,4096]{1,0:T(8,128)(2,1)} %refs_1_.7) | copy-start | bytes 12582916
  2.2 7.4 %collective-permute-start = (bf16[8,4096]{1,0:T(8,128)(2,1)S(1)}, bf16[8,4096]{1,0:T(8,128)(2,1)S(1)}, u32[]{:S(2)}, u32[]{:S(2)}) collective-permute-start(bf16[8,4096]{1,0:T(8,128)(2,1)S(1)} %shard_map.100.refs_6_), channel_id=1, source_target_pairs={{0,2},{2,4},{4,6},{6,8},{8,10},{10,12},{12,14},{1,3},{3,5},{5,7},{... | collective-permute-start | bytes 196616 | tf_op jit(solution)/shard_map/ppermute | solution.py:316
  6.0 1.0 %copy-start.3 = (bf16[512,256]{1,0:T(8,128)(2,1)S(1)}, bf16[512,256]{1,0:T(8,128)(2,1)}, u32[]{:S(2)}) copy-start(bf16[512,256]{1,0:T(8,128)(2,1)} %refs_3_.2) | copy-start | bytes 786436
  6.9 0.9 %copy-start.5 = (s32[512,64]{0,1:T(8,128)S(1)}, s32[512,64]{0,1:T(8,128)}, u32[]{:S(2)}) copy-start(s32[512,64]{0,1:T(8,128)} %param.14) | copy-start | bytes 393220
  14.0 9.1 %collective-permute-start.1 = (f32[1,4096]{1,0:T(1,128)S(1)}, f32[1,4096]{1,0:T(1,128)S(1)}, u32[]{:S(2)}, u32[]{:S(2)}) collective-permute-start(f32[1,4096]{1,0:T(1,128)S(1)} %get-tuple-element.45.refs_0_), channel_id=1, source_target_pairs={{0,2},{2,0},{4,6},{6,4},{8,10},{10,8},{12,14},{14,12},{1,3},{3,1},... | collective-permute-start | bytes 49160 | tf_op jit(solution)/shard_map/ppermute | solution.py:490
  15.6 6.4 %copy-start.4 = (bf16[512,256]{1,0:T(8,128)(2,1)S(1)}, bf16[512,256]{1,0:T(8,128)(2,1)}, u32[]{:S(2)}) copy-start(bf16[512,256]{1,0:T(8,128)(2,1)} %refs_3_.3) | copy-start | bytes 786436
  15.6 8.9 %collective-permute-start.2 = (bf16[64,2048]{1,0:T(8,128)(2,1)S(1)}, bf16[64,2048]{1,0:T(8,128)(2,1)S(1)}, u32[]{:S(2)}, u32[]{:S(2)}) collective-permute-start(bf16[64,2048]{1,0:T(8,128)(2,1)S(1)} %get-tuple-element.46.refs_8_), channel_id=1, source_target_pairs={{0,2},{2,0},{4,6},{6,4},{8,10},{10,8},{12,14},{14,12},{1,3},{3,1},... | collective-permute-start | bytes 786440 | tf_op jit(solution)/shard_map/ppermute | solution.py:437
  16.2 9.3 %copy-start = (bf16[512,4096]{1,0:T(8,128)(2,1)S(1)}, bf16[512,4096]{1,0:T(8,128)(2,1)}, u32[]{:S(2)}) copy-start(bf16[512,4096]{1,0:T(8,128)(2,1)} %refs_1_.11) | copy-start | bytes 12582916
  20.5 8.5 %collective-permute-start.4 = (bf16[64,2048]{1,0:T(8,128)(2,1)S(1)}, bf16[64,2048]{1,0:T(8,128)(2,1)S(1)}, u32[]{:S(2)}, u32[]{:S(2)}) collective-permute-start(bf16[64,2048]{1,0:T(8,128)(2,1)S(1)} %get-tuple-element.48.refs_4_), channel_id=1, source_target_pairs={{0,2},{2,0},{4,6},{6,4},{8,10},{10,8},{12,14},{14,12},{1,3},{3,1},... | collective-permute-start | bytes 786440 | tf_op jit(solution)/shard_map/ppermute | solution.py:437
  24.6 5.1 %collective-permute-start.3 = (bf16[64,2048]{1,0:T(8,128)(2,1)S(1)}, bf16[64,2048]{1,0:T(8,128)(2,1)S(1)}, u32[]{:S(2)}, u32[]{:S(2)}) collective-permute-start(bf16[64,2048]{1,0:T(8,128)(2,1)S(1)} %add_convert_fusion.3.refs_12_), channel_id=1, source_target_pairs={{0,4},{2,6},{1,5},{3,7},{16,20},{18,22},{17,21},{19,23}} | collective-permute-start | bytes 786440 | tf_op jit(solution)/shard_map/ppermute | solution.py:454
  29.1 5.3 %collective-permute-start.6 = (bf16[64,2048]{1,0:T(8,128)(2,1)S(1)}, bf16[64,2048]{1,0:T(8,128)(2,1)S(1)}, u32[]{:S(2)}, u32[]{:S(2)}) collective-permute-start(bf16[64,2048]{1,0:T(8,128)(2,1)S(1)} %add_convert_fusion.2.refs_15_), channel_id=1, source_target_pairs={{0,4},{2,6},{1,5},{3,7},{16,20},{18,22},{17,21},{19,23}} | collective-permute-start | bytes 786440 | tf_op jit(solution)/shard_map/ppermute | solution.py:454
  30.0 9.5 %collective-permute-start.5 = (bf16[64,2048]{1,0:T(8,128)(2,1)S(1)}, bf16[64,2048]{1,0:T(8,128)(2,1)S(1)}, u32[]{:S(2)}, u32[]{:S(2)}) collective-permute-start(bf16[64,2048]{1,0:T(8,128)(2,1)S(1)} %fusion.3.refs_14_), channel_id=1, source_target_pairs={{4,8},{6,10},{5,9},{7,11},{20,24},{22,26},{21,25},{23,27}} | collective-permute-start | bytes 786440 | tf_op jit(solution)/shard_map/ppermute | solution.py:454
  34.6 10.5 %collective-permute-start.8 = (bf16[64,2048]{1,0:T(8,128)(2,1)S(1)}, bf16[64,2048]{1,0:T(8,128)(2,1)S(1)}, u32[]{:S(2)}, u32[]{:S(2)}) collective-permute-start(bf16[64,2048]{1,0:T(8,128)(2,1)S(1)} %fusion.7.refs_13_), channel_id=1, source_target_pairs={{4,8},{6,10},{5,9},{7,11},{20,24},{22,26},{21,25},{23,27}} | collective-permute-start | bytes 786440 | tf_op jit(solution)/shard_map/ppermute | solution.py:454
  39.7 7.1 %collective-permute-start.7 = (bf16[64,2048]{1,0:T(8,128)(2,1)S(1)}, bf16[64,2048]{1,0:T(8,128)(2,1)S(1)}, u32[]{:S(2)}, u32[]{:S(2)}) collective-permute-start(bf16[64,2048]{1,0:T(8,128)(2,1)S(1)} %add_convert_fusion.1.refs_12_), channel_id=1, source_target_pairs={{8,12},{10,14},{9,13},{11,15},{24,28},{26,30},{25,29},{27,31}} | collective-permute-start | bytes 786440 | tf_op jit(solution)/shard_map/ppermute | solution.py:454
  45.3 5.2 %collective-permute-start.9 = (bf16[64,2048]{1,0:T(8,128)(2,1)S(1)}, bf16[64,2048]{1,0:T(8,128)(2,1)S(1)}, u32[]{:S(2)}, u32[]{:S(2)}) collective-permute-start(bf16[64,2048]{1,0:T(8,128)(2,1)S(1)} %add_convert_fusion.refs_15_), channel_id=1, source_target_pairs={{8,12},{10,14},{9,13},{11,15},{24,28},{26,30},{25,29},{27,31}} | collective-permute-start | bytes 786440 | tf_op jit(solution)/shard_map/ppermute | solution.py:454
  47.1 9.2 %collective-permute-start.11 = (bf16[64,2048]{1,0:T(8,128)(2,1)S(1)}, bf16[64,2048]{1,0:T(8,128)(2,1)S(1)}, u32[]{:S(2)}, u32[]{:S(2)}) collective-permute-start(bf16[64,2048]{1,0:T(8,128)(2,1)S(1)} %get-tuple-element.76.refs_14_), channel_id=1, source_target_pairs={{0,2},{2,0},{4,6},{6,4},{8,10},{10,8},{12,14},{14,12},{1,3},{3,1},... | collective-permute-start | bytes 786440 | tf_op jit(solution)/shard_map/ppermute | solution.py:462
  47.1 9.1 %copy-start.6 = (f32[4096]{0:T(1024)S(1)}, f32[4096]{0:T(1024)}, u32[]{:S(2)}) copy-start(f32[4096]{0:T(1024)} %param.19) | copy-start | bytes 49156
  50.7 8.6 %collective-permute-start.10 = (bf16[64,2048]{1,0:T(8,128)(2,1)S(1)}, bf16[64,2048]{1,0:T(8,128)(2,1)S(1)}, u32[]{:S(2)}, u32[]{:S(2)}) collective-permute-start(bf16[64,2048]{1,0:T(8,128)(2,1)S(1)} %get-tuple-element.77.refs_6_), channel_id=1, source_target_pairs={{0,2},{2,0},{4,6},{6,4},{8,10},{10,8},{12,14},{14,12},{1,3},{3,1},... | collective-permute-start | bytes 786440 | tf_op jit(solution)/shard_map/ppermute | solution.py:462

commit v4 on v3

--- a/solution.py
+++ b/solution.py
@@ -174,7 +174,7 @@
             f_ref[rows, here] = filtered
             wide = dot(pieces_ref[rows, mine], spread_ref[:, inner])
             weight = jnp.exp2(rate * (wide[SUB - 1 : SUB] - wide))
-            weighted = (weight * filtered.astype(f32)).astype(bf16)
+            weighted = weight.astype(bf16) * filtered
             part = dot(bt_ref[mine, rows], weighted)
             running = part if s == 0 else rows_ref[2 + s : 3 + s, cols] * running + part
             if s < NSUB - 1:

time: 62.7 us -> 62.8 us (level)
  waiting for transfers between devices: 10.2 us -> 11.1 us
    ppermute x6, waiting for transfers between devices: 4.7 us -> 5.63 us  [carry(): arrived = lax.ppermute(sent, 'ctx', route).astype(f32)]
  transfers between devices with their start and end apart: 12 -> 12, of which waited for: 6 -> 7; matrix products, arithmetic and copies ran while one was open for 3% -> 3% of each run, Pallas kernels for 36% -> 36%
where the time goes in v4:
time: 62.8 us; the launch traced here: 62.5 us
  Pallas kernels  29.4 us (47%)
  starting transfers between devices  16 us (25%)
  waiting for transfers between devices  11.1 us (18%)
  local copies, waits for them, and re-layouts  4.07 us (6%)
  other arithmetic  1.69 us (3%)
    pallas_call x11, Pallas kernels, call(): pl.pallas_call(ordered, in_specs=list(in_specs) + [pl.BlockSpec(memory_sp...  29.4 us
    ppermute x6, starting transfers between devices, carry(): arrived = lax.ppermute(sent, 'ctx', route).astype(f32)  6.95 us
    ppermute x6, waiting for transfers between devices, carry(): arrived = lax.ppermute(sent, 'ctx', route).astype(f32)  5.63 us
    unnamed x22, local copies, waits for them, and re-layouts  4.07 us
    ppermute x1, starting transfers between devices, per_device(): tail = lax.ppermute(last_rows, 'ctx', [(i, i + 1) for i in range(runs - 1)])  3.69 us
    ppermute x2, waiting for transfers between devices, carry(): other = lax.ppermute(given, 'ctx', swap)  3.49 us
    ppermute x2, starting transfers between devices, carry(): got = lax.ppermute(given, 'ctx', swap)  2.16 us
    ppermute x2, waiting for transfers between devices, carry(): got = lax.ppermute(given, 'ctx', swap)  1.93 us
  transfers between devices with their start and end apart: 12, of which 7 were waited for; matrix products, arithmetic and copies ran while one was open for 3% of the time, Pallas kernels for 36%

profile of v4, /device:TPU:16, one launch (start us, length us, event | category | flops | bytes accessed | tf_op | source)
XLA Modules:
  0.0 62.5 jit_solution(15342948442484344283)
XLA Ops:
  0.0 2.2 %copy-done.1 = bf16[512,4096]{1,0:T(8,128)(2,1)S(1)} copy-done((bf16[512,4096]{1,0:T(8,128)(2,1)S(1)}, bf16[512,4096]{1,0:T(8,128)(2,1)}, u32[]{:S(2)}) %copy-start.1) | copy-done | bytes 4194328
  2.2 3.7 %collective-permute-start = (bf16[8,4096]{1,0:T(8,128)(2,1)S(1)}, bf16[8,4096]{1,0:T(8,128)(2,1)S(1)}, u32[]{:S(2)}, u32[]{:S(2)}) collective-permute-start(bf16[8,4096]{1,0:T(8,128)(2,1)S(1)} %shard_map.100.refs_6_), channel_id=1, source_target_pairs={{0,2},{2,4},{4,6},{6,8},{8,10},{10,12},{12,14},{1,3},{3,5},{5,7},{... | collective-permute-start | bytes 196616 | tf_op jit(solution)/shard_map/ppermute | solution.py:316
  6.0 0.0 copy-start.3
  6.0 0.9 %copy-done.3 = bf16[512,256]{1,0:T(8,128)(2,1)S(1)} copy-done((bf16[512,256]{1,0:T(8,128)(2,1)S(1)}, bf16[512,256]{1,0:T(8,128)(2,1)}, u32[]{:S(2)}) %copy-start.3) | copy-done | bytes 262168
  6.9 0.9 %copy-done.5 = s32[512,64]{0,1:T(8,128)S(1)} copy-done((s32[512,64]{0,1:T(8,128)S(1)}, s32[512,64]{0,1:T(8,128)}, u32[]{:S(2)}) %copy-start.5) | copy-done | bytes 131096
  7.8 1.8 %shard_map.101 = (bf16[512,256]{1,0:T(8,128)(2,1)S(1)}, bf16[128,2048]{1,0:T(8,128)(2,1)S(1)}, bf16[256,512]{1,0:T(8,128)(2,1)S(1)}, f32[16,4096]{1,0:T(8,128)S(...) custom-call(s32[64,512]{1,0:T(8,128)S(1)} %bitcast.17, f32[1,64]{1,0:T(1,128)S(1)} %bitcast.20, ...), custom_call_target="tpu_custom_call" | custom-call | flops 1 | bytes 1 | tf_op jit(solution)/shard_map/pallas_call | solution.py:265
  9.7 0.0 collective-permute-done.refs_2_
  9.7 4.1 %shard_map.102 = (bf16[512,2048]{1,0:T(8,128)(2,1)S(1)}, bf16[3,128,2048]{2,1,0:T(8,128)(2,1)S(1)}, bf16[64,2048]{1,0:T(8,128)(2,1)S(1)}, bf16[64,2048]{1,0:T(8,128)(2,1)S(1)}, f32[1,4096]{1,0:T(1,128)S(1)}) custom-call(f32[1,4096]{1,0:T(1,128)S(1)} %get-tuple-element.39.refs_0_, bf16[512,4096]{1,0:T(8,128)(2,1)S(1)} %copy-done.2, ...), custom_call_target="tpu_custom_call" | custom-call | flops 1 | bytes 1 | tf_op jit(solution)/shard_map/pallas_call | solution.py:265
  13.8 1.6 %collective-permute-start.1 = (f32[1,4096]{1,0:T(1,128)S(1)}, f32[1,4096]{1,0:T(1,128)S(1)}, u32[]{:S(2)}, u32[]{:S(2)}) collective-permute-start(f32[1,4096]{1,0:T(1,128)S(1)} %get-tuple-element.45.refs_0_), channel_id=1, source_target_pairs={{0,2},{2,0},{4,6},{6,4},{8,10},{10,8},{12,14},{14,12},{1,3},{3,1},... | collective-permute-start | bytes 49160 | tf_op jit(solution)/shard_map/ppermute | solution.py:490
  15.4 0.1 fusion.9
  15.4 0.6 collective-permute-start.2
  16.0 4.1 %shard_map.103 = (bf16[512,2048]{1,0:T(8,128)(2,1)S(1)}, bf16[3,128,2048]{2,1,0:T(8,128)(2,1)S(1)}, bf16[64,2048]{1,0:T(8,128)(2,1)S(1)}, bf16[64,2048]{1,0:T(8,128)(2,1)S(1)}, f32[1,4096]{1,0:T(1,128)S(1)}) custom-call(f32[1,4096]{1,0:T(1,128)S(1)} %get-tuple-element.45.refs_0_, bf16[512,4096]{1,0:T(8,128)(2,1)S(1)} %copy-done.2, ...), custom_call_target="tpu_custom_call" | custom-call | flops 1 | bytes 1 | tf_op jit(solution)/shard_map/pallas_call | solution.py:265
  20.1 1.6 %collective-permute-start.4 = (bf16[64,2048]{1,0:T(8,128)(2,1)S(1)}, bf16[64,2048]{1,0:T(8,128)(2,1)S(1)}, u32[]{:S(2)}, u32[]{:S(2)}) collective-permute-start(bf16[64,2048]{1,0:T(8,128)(2,1)S(1)} %get-tuple-element.48.refs_4_), channel_id=1, source_target_pairs={{0,2},{2,0},{4,6},{6,4},{8,10},{10,8},{12,14},{14,12},{1,3},{3,1},... | collective-permute-start | bytes 786440 | tf_op jit(solution)/shard_map/ppermute | solution.py:437
  21.7 1.0 %shard_map.104 = (bf16[512,1024]{1,0:T(8,128)(2,1)S(1)}, bf16[1024,512]{1,0:T(8,128)(2,1)S(1)}, f32[2,512,128]{2,1,0:T(8,128)S(1)}, bf16[512,256]{1,0:T(8,128)(2,1)S(1)}, f32[1,4096]{1,0:T(1,128)S(1)}) custom-call(f32[1,4096]{1,0:T(1,128)S(1)} %get-tuple-element.47.refs_0_, bf16[512,256]{1,0:T(8,128)(2,1)S(1)} %get-tuple-element.41.refs_4_.refs_1_.refs_5_, ...), custom_call_target="tpu_custom_call" | custom-call | flops 1 | bytes 1 | tf_op jit(solution)/shard_map/pallas_call | solution.py:265
  22.7 0.0 collective-permute-done.1
  22.7 1.8 %collective-permute-done.2 = bf16[64,2048]{1,0:T(8,128)(2,1)S(1)} collective-permute-done((bf16[64,2048]{1,0:T(8,128)(2,1)S(1)}, bf16[64,2048]{1,0:T(8,128)(2,1)S(1)}, u32[]{:S(2)}, u32[]{:S(2)}) %collective-permute-start.2) | collective-permute-done | bytes 262176 | tf_op jit(solution)/shard_map/ppermute | solution.py:437
  24.5 0.1 add_convert_fusion.3.refs_12_
  24.6 0.9 %collective-permute-start.3 = (bf16[64,2048]{1,0:T(8,128)(2,1)S(1)}, bf16[64,2048]{1,0:T(8,128)(2,1)S(1)}, u32[]{:S(2)}, u32[]{:S(2)}) collective-permute-start(bf16[64,2048]{1,0:T(8,128)(2,1)S(1)} %add_convert_fusion.3.refs_12_), channel_id=1, source_target_pairs={{0,4},{2,6},{1,5},{3,7},{16,20},{18,22},{17,21},{19,23}} | collective-permute-start | bytes 786440 | tf_op jit(solution)/shard_map/ppermute | solution.py:454
  25.5 3.1 %shard_map.105 = (f32[1,4096]{1,0:T(1,128)S(1)}, bf16[512,2048]{1,0:T(8,128)(2,1)S(1)}, bf16[512,2048]{1,0:T(8,128)(2,1)S(1)}) custom-call(f32[1,4096]{1,0:T(1,128)S(1)} %get-tuple-element.49.refs_0_, bf16[512,4096]{1,0:T(8,128)(2,1)S(1)} %copy-done, bf16[512,2048]{1,0:T(8,128)(2,1)S(1)} %get-tuple-element.50.refs_2_, ...), custom_call_target="tpu_custom_call" | custom-call | flops 1 | bytes 1 | tf_op jit(solution)/shard_map/pallas_call | solution.py:265
  28.6 0.1 collective-permute-done.4
  28.8 0.1 add_convert_fusion.2.refs_15_
  28.9 0.7 %collective-permute-start.6 = (bf16[64,2048]{1,0:T(8,128)(2,1)S(1)}, bf16[64,2048]{1,0:T(8,128)(2,1)S(1)}, u32[]{:S(2)}, u32[]{:S(2)}) collective-permute-start(bf16[64,2048]{1,0:T(8,128)(2,1)S(1)} %add_convert_fusion.2.refs_15_), channel_id=1, source_target_pairs={{0,4},{2,6},{1,5},{3,7},{16,20},{18,22},{17,21},{19,23}} | collective-permute-start | bytes 786440 | tf_op jit(solution)/shard_map/ppermute | solution.py:454
  29.6 0.0 collective-permute-done.3
  29.6 0.2 fusion.3.refs_14_
  29.8 1.3 %collective-permute-start.5 = (bf16[64,2048]{1,0:T(8,128)(2,1)S(1)}, bf16[64,2048]{1,0:T(8,128)(2,1)S(1)}, u32[]{:S(2)}, u32[]{:S(2)}) collective-permute-start(bf16[64,2048]{1,0:T(8,128)(2,1)S(1)} %fusion.3.refs_14_), channel_id=1, source_target_pairs={{4,8},{6,10},{5,9},{7,11},{20,24},{22,26},{21,25},{23,27}} | collective-permute-start | bytes 786440 | tf_op jit(solution)/shard_map/ppermute | solution.py:454
  31.1 3.1 %shard_map.106 = (f32[1,4096]{1,0:T(1,128)S(1)}, bf16[512,2048]{1,0:T(8,128)(2,1)S(1)}, bf16[512,2048]{1,0:T(8,128)(2,1)S(1)}) custom-call(f32[1,4096]{1,0:T(1,128)S(1)} %get-tuple-element.58.refs_0_, bf16[512,4096]{1,0:T(8,128)(2,1)S(1)} %copy-done, ...), custom_call_target="tpu_custom_call", output_to_operand_aliasing={{1}: (12, {}), {2}: (13, {})} | custom-call | flops 1 | bytes 1 | tf_op jit(solution)/shard_map/pallas_call | solution.py:265
  34.2 0.0 collective-permute-done.6
  34.2 0.2 fusion.7.refs_13_
  34.4 1.3 %collective-permute-start.8 = (bf16[64,2048]{1,0:T(8,128)(2,1)S(1)}, bf16[64,2048]{1,0:T(8,128)(2,1)S(1)}, u32[]{:S(2)}, u32[]{:S(2)}) collective-permute-start(bf16[64,2048]{1,0:T(8,128)(2,1)S(1)} %fusion.7.refs_13_), channel_id=1, source_target_pairs={{4,8},{6,10},{5,9},{7,11},{20,24},{22,26},{21,25},{23,27}} | collective-permute-start | bytes 786440 | tf_op jit(solution)/shard_map/ppermute | solution.py:454
  35.7 4.5 %collective-permute-done.5 = bf16[64,2048]{1,0:T(8,128)(2,1)S(1)} collective-permute-done((bf16[64,2048]{1,0:T(8,128)(2,1)S(1)}, bf16[64,2048]{1,0:T(8,128)(2,1)S(1)}, u32[]{:S(2)}, u32[]{:S(2)}) %collective-permute-start.5) | collective-permute-done | bytes 262176 | tf_op jit(solution)/shard_map/ppermute | solution.py:454
  40.2 0.2 add_convert_fusion.1.refs_12_
  40.4 1.3 %collective-permute-start.7 = (bf16[64,2048]{1,0:T(8,128)(2,1)S(1)}, bf16[64,2048]{1,0:T(8,128)(2,1)S(1)}, u32[]{:S(2)}, u32[]{:S(2)}) collective-permute-start(bf16[64,2048]{1,0:T(8,128)(2,1)S(1)} %add_convert_fusion.1.refs_12_), channel_id=1, source_target_pairs={{8,12},{10,14},{9,13},{11,15},{24,28},{26,30},{25,29},{27,31}} | collective-permute-start | bytes 786440 | tf_op jit(solution)/shard_map/ppermute | solution.py:454
  41.7 3.1 %shard_map.107 = (f32[1,4096]{1,0:T(1,128)S(1)}, bf16[512,2048]{1,0:T(8,128)(2,1)S(1)}, bf16[512,2048]{1,0:T(8,128)(2,1)S(1)}) custom-call(f32[1,4096]{1,0:T(1,128)S(1)} %get-tuple-element.62.refs_0_, bf16[512,4096]{1,0:T(8,128)(2,1)S(1)} %copy-done, bf16[512,2048]{1,0:T(8,128)(2,1)S(1)} %get-tuple-element.63.refs_2_, ...), custom_call_target="tpu_custom_call" | custom-call | flops 1 | bytes 1 | tf_op jit(solution)/shard_map/pallas_call | solution.py:265
  44.9 0.6 collective-permute-done.8
  45.4 0.2 add_convert_fusion.refs_15_
  45.6 1.5 %collective-permute-start.9 = (bf16[64,2048]{1,0:T(8,128)(2,1)S(1)}, bf16[64,2048]{1,0:T(8,128)(2,1)S(1)}, u32[]{:S(2)}, u32[]{:S(2)}) collective-permute-start(bf16[64,2048]{1,0:T(8,128)(2,1)S(1)} %add_convert_fusion.refs_15_), channel_id=1, source_target_pairs={{8,12},{10,14},{9,13},{11,15},{24,28},{26,30},{25,29},{27,31}} | collective-permute-start | bytes 786440 | tf_op jit(solution)/shard_map/ppermute | solution.py:454
  47.2 0.0 collective-permute-done.7
  47.2 0.2 select_convert_fusion
  47.4 0.1 collective-permute-start.11
  47.5 0.0 copy-start.6
  47.5 3.1 %shard_map.108 = (f32[1,4096]{1,0:T(1,128)S(1)}, bf16[512,2048]{1,0:T(8,128)(2,1)S(1)}, bf16[512,2048]{1,0:T(8,128)(2,1)S(1)}) custom-call(f32[1,4096]{1,0:T(1,128)S(1)} %get-tuple-element.65.refs_0_, bf16[512,4096]{1,0:T(8,128)(2,1)S(1)} %copy-done, ...), custom_call_target="tpu_custom_call", output_to_operand_aliasing={{1}: (12, {}), {2}: (13, {})} | custom-call | flops 1 | bytes 1 | tf_op jit(solution)/shard_map/pallas_call | solution.py:265
  50.6 0.6 collective-permute-done.9
  51.2 0.2 select_convert_fusion.1
  51.5 1.5 %collective-permute-start.10 = (bf16[64,2048]{1,0:T(8,128)(2,1)S(1)}, bf16[64,2048]{1,0:T(8,128)(2,1)S(1)}, u32[]{:S(2)}, u32[]{:S(2)}) collective-permute-start(bf16[64,2048]{1,0:T(8,128)(2,1)S(1)} %get-tuple-element.77.refs_6_), channel_id=1, source_target_pairs={{0,2},{2,0},{4,6},{6,4},{8,10},{10,8},{12,14},{14,12},{1,3},{3,1},... | collective-permute-start | bytes 786440 | tf_op jit(solution)/shard_map/ppermute | solution.py:462
  53.0 3.1 %collective-permute-done.11.refs_3_ = bf16[64,2048]{1,0:T(8,128)(2,1)S(1)} collective-permute-done((bf16[64,2048]{1,0:T(8,128)(2,1)S(1)}, bf16[64,2048]{1,0:T(8,128)(2,1)S(1)}, u32[]{:S(2)}, u32[]{:S(2)}) %collective-permute-start.11) | collective-permute-done | bytes 262176 | tf_op jit(solution)/shard_map/ppermute | solution.py:462
  56.1 3.0 %shard_map.109.refs_6_ = bf16[512,4096]{1,0:T(8,128)(2,1)} custom-call(bf16[512,2048]{1,0:T(8,128)(2,1)S(1)} %get-tuple-element.71.refs_0_, bf16[512,2048]{1,0:T(8,128)(2,1)S(1)} %get-tuple-element.72.refs_1_, bf16[64,2048]{1,0:T(8,128)(2,1)S(1)} %get-tuple-element.75.refs_2_, bf16[64,2048]{1,0:T(8,128)(2,1)S(1)} %collective-permute-done.11.refs_3_, ...), custom_call_target="tpu_custom_call" | custom-call | flops 1 | bytes 1 | tf_op jit(solution)/shard_map/pallas_call | solution.py:265
  59.1 0.4 collective-permute-done.10.refs_3_
  59.5 3.0 %shard_map.110 = bf16[512,4096]{1,0:T(8,128)(2,1)} custom-call(bf16[512,2048]{1,0:T(8,128)(2,1)S(1)} %get-tuple-element.68.refs_0_, bf16[512,2048]{1,0:T(8,128)(2,1)S(1)} %get-tuple-element.69.refs_1_, bf16[64,2048]{1,0:T(8,128)(2,1)S(1)} %get-tuple-element.78.refs_2_, ...), custom_call_target="tpu_custom_call", output_to_operand_aliasing={{}: (6, {})} | custom-call | flops 1 | bytes 1 | tf_op jit(solution)/shard_map/pallas_call | solution.py:265
  (23 shorter events, 0.2 us)
Async XLA Ops:
  0.0 2.2 %copy-start.1 = (bf16[512,4096]{1,0:T(8,128)(2,1)S(1)}, bf16[512,4096]{1,0:T(8,128)(2,1)}, u32[]{:S(2)}) copy-start(bf16[512,4096]{1,0:T(8,128)(2,1)} %refs_1_.7) | copy-start | bytes 12582916
  2.2 3.7 %copy-start.7 = (bf16[4,4096]{1,0:T(4,128)(2,1)S(1)}, bf16[4,4096]{1,0:T(4,128)(2,1)}, u32[]{:S(2)}) copy-start(bf16[4,4096]{1,0:T(4,128)(2,1)} %refs_4_.1) | copy-start | bytes 98308
  2.2 3.7 %copy-start.8 = (f32[64]{0:T(128)S(1)}, f32[64]{0:T(128)}, u32[]{:S(2)}) copy-start(f32[64]{0:T(128)} %refs_11_.7) | copy-start | bytes 772
  2.2 3.8 %copy-start.9 = (bf16[4096]{0:T(1024)(128)(2,1)S(1)}, bf16[4096]{0:T(1024)(128)(2,1)}, u32[]{:S(2)}) copy-start(bf16[4096]{0:T(1024)(128)(2,1)} %param.17) | copy-start | bytes 24580
  2.2 3.8 %copy-start.10 = (f32[64]{0:T(128)S(1)}, f32[64]{0:T(128)}, u32[]{:S(2)}) copy-start(f32[64]{0:T(128)} %param.18) | copy-start | bytes 772
  2.2 7.5 %copy-start.2 = (bf16[512,4096]{1,0:T(8,128)(2,1)S(1)}, bf16[512,4096]{1,0:T(8,128)(2,1)}, u32[]{:S(2)}) copy-start(bf16[512,4096]{1,0:T(8,128)(2,1)} %refs_1_.7) | copy-start | bytes 12582916
  2.2 7.4 %collective-permute-start = (bf16[8,4096]{1,0:T(8,128)(2,1)S(1)}, bf16[8,4096]{1,0:T(8,128)(2,1)S(1)}, u32[]{:S(2)}, u32[]{:S(2)}) collective-permute-start(bf16[8,4096]{1,0:T(8,128)(2,1)S(1)} %shard_map.100.refs_6_), channel_id=1, source_target_pairs={{0,2},{2,4},{4,6},{6,8},{8,10},{10,12},{12,14},{1,3},{3,5},{5,7},{... | collective-permute-start | bytes 196616 | tf_op jit(solution)/shard_map/ppermute | solution.py:316
  6.0 1.0 %copy-start.3 = (bf16[512,256]{1,0:T(8,128)(2,1)S(1)}, bf16[512,256]{1,0:T(8,128)(2,1)}, u32[]{:S(2)}) copy-start(bf16[512,256]{1,0:T(8,128)(2,1)} %refs_3_.2) | copy-start | bytes 786436
  6.9 0.9 %copy-start.5 = (s32[512,64]{0,1:T(8,128)S(1)}, s32[512,64]{0,1:T(8,128)}, u32[]{:S(2)}) copy-start(s32[512,64]{0,1:T(8,128)} %param.14) | copy-start | bytes 393220
  13.8 8.9 %collective-permute-start.1 = (f32[1,4096]{1,0:T(1,128)S(1)}, f32[1,4096]{1,0:T(1,128)S(1)}, u32[]{:S(2)}, u32[]{:S(2)}) collective-permute-start(f32[1,4096]{1,0:T(1,128)S(1)} %get-tuple-element.45.refs_0_), channel_id=1, source_target_pairs={{0,2},{2,0},{4,6},{6,4},{8,10},{10,8},{12,14},{14,12},{1,3},{3,1},... | collective-permute-start | bytes 49160 | tf_op jit(solution)/shard_map/ppermute | solution.py:490
  15.4 6.3 %copy-start.4 = (bf16[512,256]{1,0:T(8,128)(2,1)S(1)}, bf16[512,256]{1,0:T(8,128)(2,1)}, u32[]{:S(2)}) copy-start(bf16[512,256]{1,0:T(8,128)(2,1)} %refs_3_.3) | copy-start | bytes 786436
  15.4 9.1 %collective-permute-start.2 = (bf16[64,2048]{1,0:T(8,128)(2,1)S(1)}, bf16[64,2048]{1,0:T(8,128)(2,1)S(1)}, u32[]{:S(2)}, u32[]{:S(2)}) collective-permute-start(bf16[64,2048]{1,0:T(8,128)(2,1)S(1)} %get-tuple-element.46.refs_8_), channel_id=1, source_target_pairs={{0,2},{2,0},{4,6},{6,4},{8,10},{10,8},{12,14},{14,12},{1,3},{3,1},... | collective-permute-start | bytes 786440 | tf_op jit(solution)/shard_map/ppermute | solution.py:437
  16.0 9.5 %copy-start = (bf16[512,4096]{1,0:T(8,128)(2,1)S(1)}, bf16[512,4096]{1,0:T(8,128)(2,1)}, u32[]{:S(2)}) copy-start(bf16[512,4096]{1,0:T(8,128)(2,1)} %refs_1_.11) | copy-start | bytes 12582916
  20.1 8.7 %collective-permute-start.4 = (bf16[64,2048]{1,0:T(8,128)(2,1)S(1)}, bf16[64,2048]{1,0:T(8,128)(2,1)S(1)}, u32[]{:S(2)}, u32[]{:S(2)}) collective-permute-start(bf16[64,2048]{1,0:T(8,128)(2,1)S(1)} %get-tuple-element.48.refs_4_), channel_id=1, source_target_pairs={{0,2},{2,0},{4,6},{6,4},{8,10},{10,8},{12,14},{14,12},{1,3},{3,1},... | collective-permute-start | bytes 786440 | tf_op jit(solution)/shard_map/ppermute | solution.py:437
  24.6 5.0 %collective-permute-start.3 = (bf16[64,2048]{1,0:T(8,128)(2,1)S(1)}, bf16[64,2048]{1,0:T(8,128)(2,1)S(1)}, u32[]{:S(2)}, u32[]{:S(2)}) collective-permute-start(bf16[64,2048]{1,0:T(8,128)(2,1)S(1)} %add_convert_fusion.3.refs_12_), channel_id=1, source_target_pairs={{0,4},{2,6},{1,5},{3,7},{16,20},{18,22},{17,21},{19,23}} | collective-permute-start | bytes 786440 | tf_op jit(solution)/shard_map/ppermute | solution.py:454
  28.9 5.3 %collective-permute-start.6 = (bf16[64,2048]{1,0:T(8,128)(2,1)S(1)}, bf16[64,2048]{1,0:T(8,128)(2,1)S(1)}, u32[]{:S(2)}, u32[]{:S(2)}) collective-permute-start(bf16[64,2048]{1,0:T(8,128)(2,1)S(1)} %add_convert_fusion.2.refs_15_), channel_id=1, source_target_pairs={{0,4},{2,6},{1,5},{3,7},{16,20},{18,22},{17,21},{19,23}} | collective-permute-start | bytes 786440 | tf_op jit(solution)/shard_map/ppermute | solution.py:454
  29.8 10.4 %collective-permute-start.5 = (bf16[64,2048]{1,0:T(8,128)(2,1)S(1)}, bf16[64,2048]{1,0:T(8,128)(2,1)S(1)}, u32[]{:S(2)}, u32[]{:S(2)}) collective-permute-start(bf16[64,2048]{1,0:T(8,128)(2,1)S(1)} %fusion.3.refs_14_), channel_id=1, source_target_pairs={{4,8},{6,10},{5,9},{7,11},{20,24},{22,26},{21,25},{23,27}} | collective-permute-start | bytes 786440 | tf_op jit(solution)/shard_map/ppermute | solution.py:454
  34.4 11.0 %collective-permute-start.8 = (bf16[64,2048]{1,0:T(8,128)(2,1)S(1)}, bf16[64,2048]{1,0:T(8,128)(2,1)S(1)}, u32[]{:S(2)}, u32[]{:S(2)}) collective-permute-start(bf16[64,2048]{1,0:T(8,128)(2,1)S(1)} %fusion.7.refs_13_), channel_id=1, source_target_pairs={{4,8},{6,10},{5,9},{7,11},{20,24},{22,26},{21,25},{23,27}} | collective-permute-start | bytes 786440 | tf_op jit(solution)/shard_map/ppermute | solution.py:454
  40.4 6.8 %collective-permute-start.7 = (bf16[64,2048]{1,0:T(8,128)(2,1)S(1)}, bf16[64,2048]{1,0:T(8,128)(2,1)S(1)}, u32[]{:S(2)}, u32[]{:S(2)}) collective-permute-start(bf16[64,2048]{1,0:T(8,128)(2,1)S(1)} %add_convert_fusion.1.refs_12_), channel_id=1, source_target_pairs={{8,12},{10,14},{9,13},{11,15},{24,28},{26,30},{25,29},{27,31}} | collective-permute-start | bytes 786440 | tf_op jit(solution)/shard_map/ppermute | solution.py:454
  45.6 5.6 %collective-permute-start.9 = (bf16[64,2048]{1,0:T(8,128)(2,1)S(1)}, bf16[64,2048]{1,0:T(8,128)(2,1)S(1)}, u32[]{:S(2)}, u32[]{:S(2)}) collective-permute-start(bf16[64,2048]{1,0:T(8,128)(2,1)S(1)} %add_convert_fusion.refs_15_), channel_id=1, source_target_pairs={{8,12},{10,14},{9,13},{11,15},{24,28},{26,30},{25,29},{27,31}} | collective-permute-start | bytes 786440 | tf_op jit(solution)/shard_map/ppermute | solution.py:454
  47.4 8.6 %collective-permute-start.11 = (bf16[64,2048]{1,0:T(8,128)(2,1)S(1)}, bf16[64,2048]{1,0:T(8,128)(2,1)S(1)}, u32[]{:S(2)}, u32[]{:S(2)}) collective-permute-start(bf16[64,2048]{1,0:T(8,128)(2,1)S(1)} %get-tuple-element.76.refs_14_), channel_id=1, source_target_pairs={{0,2},{2,0},{4,6},{6,4},{8,10},{10,8},{12,14},{14,12},{1,3},{3,1},... | collective-permute-start | bytes 786440 | tf_op jit(solution)/shard_map/ppermute | solution.py:462
  47.5 8.5 %copy-start.6 = (f32[4096]{0:T(1024)S(1)}, f32[4096]{0:T(1024)}, u32[]{:S(2)}) copy-start(f32[4096]{0:T(1024)} %param.19) | copy-start | bytes 49156
  51.5 8.0 %collective-permute-start.10 = (bf16[64,2048]{1,0:T(8,128)(2,1)S(1)}, bf16[64,2048]{1,0:T(8,128)(2,1)S(1)}, u32[]{:S(2)}, u32[]{:S(2)}) collective-permute-start(bf16[64,2048]{1,0:T(8,128)(2,1)S(1)} %get-tuple-element.77.refs_6_), channel_id=1, source_target_pairs={{0,2},{2,0},{4,6},{6,4},{8,10},{10,8},{12,14},{14,12},{1,3},{3,1},... | collective-permute-start | bytes 786440 | tf_op jit(solution)/shard_map/ppermute | solution.py:462
